TPU v7x, 32 devices: a whole 2x2x4 slice. The times are simulated.
32 devices in a mesh: jobs: 2 (over x), clus: 16 (over z, y, core).
Axes of the slice: x: 2, y: 2, z: 4, core: 2. Of those that a mesh axis runs over, the one named last changes fastest.
Arguments:
- vertices: float32 [3, 65536], P(None, ('jobs', 'clus')), parts along dimension 1, may hold values from 0 to 17
- panel_vertices: int32 [3, 131072], P(None, ('jobs', 'clus')), parts along dimension 1, may hold values from 0 to 32767, as said below
- near_pairs: int32 [512, 4], P(('jobs', 'clus')), parts along dimension 0, may hold values from -1 to 255, as said below
- far_pairs: int32 [512, 32], P(('jobs', 'clus')), parts along dimension 0, may hold values from 0 to 255, as said below
- basis: float32 [32, 131072], P(None, ('jobs', 'clus')), parts along dimension 1, may hold values from -0.75 to 0.75
- krylov: float32 [16, 131072], P(None, ('jobs', 'clus')), parts along dimension 1, may hold values from -12 to 12
Outputs:
- next_basis: float32 [16, 131072], P(None, ('jobs', 'clus')), parts along dimension 1
- second_image: float32 [16, 131072], P(None, ('jobs', 'clus')), parts along dimension 1
There are 2 independent parts, one for each index of `jobs`. A program takes and returns all parts, laid end to end along the dimension named above; each array names one. Nothing has to cross between parts.
Inputs may be any that keep to these rules, and one draw needn't show every extreme that they name: `panel_vertices`: the vertices of a panel of cluster c are among vertices c * 128 to (c + 1) * 128 - 1. `near_pairs`: row c starts with c itself, then distinct clusters j with |j // 16 - c // 16| <= 1; live entries come first and -1 fills the rest; some row has all 4 slots live. `far_pairs`: row c holds 32 distinct clusters j with 2 <= |j // 16 - c // 16| <= 4.
All inputs are finite; a program needn't handle non-finite values.
Results may differ from a plain program's by a relative error of at most 0.0003.
Values sent between devices are 32-bit elements; how exact they have to be, the bound alone decides.
No kernel may reach another device: no remote copies, remote signals or barrier semaphores. Data moves between devices by JAX's collectives and lax.ppermute only.
A program may use at most 128 MiB of HBM per device.

v0:
```python
import functools

import jax
import jax.numpy as jnp
import numpy as np
from jax import lax
from jax.experimental import pallas as pl
from jax.experimental.pallas import tpu as pltpu
from jax.sharding import PartitionSpec as P

REACH = 4
SMOOTHING = 0.04
COULOMB = 2.0
PROXY_RADIUS = 0.6
LANES = 128
FEATURES = 80
GRID = 1.5 * 2.0 ** 22
F32 = jnp.float32
BF16 = jnp.bfloat16


def proxy_offsets(points):
    counter = np.arange(points, dtype=np.float32)
    height = 1.0 - (2.0 * counter + 1.0) / points
    radial = np.sqrt(1.0 - height * height)
    azimuth = counter * 2.399963
    return PROXY_RADIUS * np.stack([radial * np.cos(azimuth), radial * np.sin(azimuth), height]).astype(np.float32)


def split(value):
    high = value.astype(BF16)
    return high, (value - high.astype(F32)).astype(BF16)


def stacked(value):
    return jnp.concatenate(split(value), axis=0)


def folded(value):
    half = value.shape[0] // 2
    return value[:half] + value[half:]


def dot_nt(left, right):
    return lax.dot_general(left, right, (((1,), (1,)), ((), ())), preferred_element_type=F32)


def dot_nn(left, right):
    return lax.dot_general(left, right, (((1,), (0,)), ((), ())), preferred_element_type=F32)


def quartered(value):
    half = value.shape[1] // 2
    value = folded(value)
    return value[:, 0:half] + value[:, half:]


def moments_of(weighted, basis_pieces):
    return quartered(dot_nt(stacked(weighted), basis_pieces))


def copies(pairs, sems):
    moves = [pltpu.make_async_copy(source, target, sems.at[i]) for i, (source, target) in enumerate(pairs)]
    for move in moves:
        move.start()
    return moves


def pair_list(near, position, clusters):
    block = lax.div(near, clusters) - position
    partner = block * (1 - 2 * lax.rem(position, 2)) > 0
    place = (lax.rem(near, clusters) + jnp.where((block != 0) & ~partner, clusters, 0)).astype(F32)
    across = lax.broadcasted_iota(jnp.int32, (clusters, clusters), 1)
    down = lax.broadcasted_iota(jnp.int32, (clusters, clusters), 0)
    upright = lambda value: jnp.sum(jnp.where(across == down, value, 0.0), axis=1, keepdims=True)
    row = lax.broadcasted_iota(jnp.int32, (clusters, LANES), 1).astype(F32)
    target = lax.broadcasted_iota(jnp.int32, (clusters, 1), 0).astype(F32)
    rows = lax.broadcasted_iota(jnp.int32, (8, LANES), 0)
    out = jnp.zeros((8, LANES), F32)
    for which in range(2):
        here = block != 0 if which else block == 0
        live = jnp.where(here & (near >= 0), 1.0, 0.0)
        counts = sum(live[k:k + 1] for k in range(1, near.shape[0]))
        first = jnp.sum(jnp.where(across < down, counts, 0.0), axis=1, keepdims=True)
        found = jnp.zeros((clusters, LANES), F32)
        for k in range(1, near.shape[0]):
            alive = upright(live[k:k + 1])
            hit = jnp.where(row == first, alive, 0.0)
            found = found + hit * (target * 64 + upright(place[k:k + 1]))
            first = first + alive
        count = jnp.sum(counts, axis=1, keepdims=True)
        found = jnp.where(row[0:1] < count, jnp.sum(found, axis=0, keepdims=True), (1.0 + which) * clusters)
        out = jnp.where(rows == which, found, jnp.where(rows == 2 + which, count, out))
    return out.astype(jnp.int32)


def prepare_kernel(cl, vcl, rank, position_ref, vertices_hbm, corners_hbm, krylov_hbm, basis_hbm, far_hbm, near_hbm, offsets_hbm,
                   payload_ref, heavy_ref, area_ref, center_ref, at_ref, pairs_ref, basis_ref, krylov_ref, offsets_ref,
                   vertices_ref, corners_ref, raw_ref, far_ref, near_ref, mesh_ref, local_ref, sems):
    moves = copies((
        (vertices_hbm, vertices_ref), (corners_hbm, corners_ref), (krylov_hbm, krylov_ref), (basis_hbm, raw_ref),
        (far_hbm, far_ref), (near_hbm, near_ref), (offsets_hbm, offsets_ref),
    ), sems)
    rhs, panels = krylov_ref.shape
    clusters = panels // cl
    parts = cl // LANES
    moves[0].wait()
    for c in range(clusters):
        mesh_ref[3 * c:3 * c + 3, :] = vertices_ref[:, c * vcl:(c + 1) * vcl]
    moves[1].wait()
    for i in range(clusters * parts):
        local_ref[3 * i:3 * i + 3, :] = corners_ref[:, i * LANES:(i + 1) * LANES]
    first = position_ref[0] * (vcl * clusters) + vcl * lax.broadcasted_iota(jnp.int32, (clusters, LANES), 0)
    tables = [mesh_ref[pl.ds(k, clusters, stride=3), :] for k in range(3)]
    sums = [None] * 3
    for h in range(parts):
        local = [local_ref[pl.ds(3 * h + m, clusters, stride=3 * parts), :] - first for m in range(3)]
        corner = [[jnp.take_along_axis(tables[k], local[m], axis=1, mode="promise_in_bounds") for k in range(3)] for m in range(3)]
        for k in range(3):
            middle = (corner[0][k] + corner[1][k] + corner[2][k]) / 3.0
            lanes = slice(panels + k * cl + h * LANES, panels + k * cl + (h + 1) * LANES)
            payload_ref[:, lanes] = middle
            heavy_ref[:, lanes] = middle
            sums[k] = middle if h == 0 else sums[k] + middle
        one = [corner[1][k] - corner[0][k] for k in range(3)]
        two = [corner[2][k] - corner[0][k] for k in range(3)]
        normal = [one[1] * two[2] - one[2] * two[1], one[2] * two[0] - one[0] * two[2], one[0] * two[1] - one[1] * two[0]]
        area_ref[:, h * LANES:(h + 1) * LANES] = 0.5 * jnp.sqrt(normal[0] * normal[0] + normal[1] * normal[1] + normal[2] * normal[2])
    span = clusters * rank
    table = panels + 3 * cl
    mine = lax.broadcasted_iota(jnp.int32, (clusters, span), 1) // rank == lax.broadcasted_iota(jnp.int32, (clusters, span), 0)
    half = span // 2
    payload_ref[:, table + span:] = jnp.zeros_like(payload_ref[:, table + span:])
    for k in range(3):
        center = jnp.sum(sums[k], axis=1, keepdims=True) / cl
        center_ref[:, k * LANES:(k + 1) * LANES] = jnp.broadcast_to(center, (clusters, LANES))
        row = jnp.sum(jnp.where(mine, center, 0.0), axis=0, keepdims=True)
        payload_ref[k:k + 1, table + span:] = row[:, 0:half]
        payload_ref[8 + k:9 + k, table + span:] = row[:, half:]
    moves[2].wait()
    moves[3].wait()
    for c in range(clusters):
        lanes = slice(c * cl, (c + 1) * cl)
        basis_ref[:, lanes] = stacked(raw_ref[:, lanes])
        charges = area_ref[c:c + 1, :] * krylov_ref[:, lanes]
        payload_ref[:, lanes] = charges
        heavy_ref[:, lanes] = charges
        payload_ref[:, table + c * rank:table + (c + 1) * rank] = moments_of(charges, basis_ref[:, lanes])
    moves[4].wait()
    far = far_ref[...]
    step = (lax.div(far, clusters) - position_ref[0]) * (1 - 2 * lax.rem(position_ref[0], 2))
    block = jnp.where(step < 0, step + REACH, step + REACH - 3)
    per = LANES // rank
    turn = lax.rem(lax.broadcasted_iota(jnp.int32, far.shape, 1) - far + per * clusters * 2 ** 16, per)
    at_ref[...] = (turn * 6 + block) * (span // LANES) + lax.div(lax.rem(far, clusters), per)
    moves[5].wait()
    pairs_ref[...] = pair_list(near_ref[...], position_ref[0], clusters)
    moves[6].wait()


def features_of(payload_ref, panels, c, cl, target):
    rows = [payload_ref[c:c + 1, panels + k * cl:panels + (k + 1) * cl] for k in range(3)]
    value = jnp.concatenate(rows + [jnp.zeros((5, cl), F32)], axis=0)
    coarse = (value + GRID) - GRID
    middle = (value - coarse).astype(BF16).astype(F32)
    low = (value - coarse - middle).astype(BF16).astype(F32)
    pieces = [coarse, middle, low]
    rest = middle + low
    row = lax.broadcasted_iota(jnp.int32, (8, cl), 0)
    square = jnp.sum(coarse * coarse, axis=0, keepdims=True)
    extra = jnp.sum((2.0 * coarse + rest) * rest, axis=0, keepdims=True) + (SMOOTHING if target else 0.0)
    square_high = square.astype(BF16).astype(F32)
    extra_high = extra.astype(BF16).astype(F32)
    extra_middle = (extra - extra_high).astype(BF16).astype(F32)
    ones = jnp.ones((1, cl), F32)

    def placed(base, start, *values):
        for i, one in enumerate(values):
            base = jnp.where(row == start + i, one, base)
        return base

    squares, extras = (square_high, square - square_high), (extra_high, extra_middle, extra - extra_high - extra_middle)
    if target:
        scaled = [-2.0 * piece for piece in pieces]
        first = placed(scaled[0], 3, *squares, ones, ones)
        last = placed(jnp.zeros((8, cl), F32), 0, *extras, ones, ones, ones)
    else:
        first = placed(coarse, 3, ones, ones, *squares)
        last = placed(jnp.zeros((8, cl), F32), 0, ones, ones, ones, *extras)
    combos = [(scaled[i] if target else pieces[j]) for i in range(3) for j in range(3) if i + j]
    return jnp.concatenate([first, *combos, last], axis=0)


def fill_features(sources_ref, blocks, panels, cl):
    clusters = panels // cl
    for b, ref in enumerate(blocks):
        for c in range(clusters):
            sources_ref[b * clusters + c] = features_of(ref, panels, c, cl, False).astype(BF16)
    sources_ref[len(blocks) * clusters] = sources_ref[0]


def near_block(target, source, out_ref):
    cl = target.shape[0]
    for first in range(0, cl, LANES):
        high, low = split(lax.rsqrt(dot_nn(target[first:first + LANES, :], source)))
        out_ref[first:first + LANES, :] = high
        out_ref[cl + first:cl + first + LANES, :] = low


def self_product(pieces, block_ref, cl):
    return dot_nn(pieces, block_ref[0:cl, :]) + dot_nn(pieces, block_ref[cl:2 * cl, :])


def near_product(pieces, block_ref, cl):
    return dot_nt(pieces, block_ref[0:cl, :]) + dot_nt(pieces, block_ref[cl:2 * cl, :])


def fill_charges(pieces_ref, blocks, clusters, cl):
    for b, ref in enumerate(blocks):
        for c in range(clusters):
            pieces_ref[b * clusters + c] = stacked(ref[:, c * cl:(c + 1) * cl])
    pieces_ref[len(blocks) * clusters] = jnp.zeros_like(pieces_ref[0])


def pair_at(pairs_ref, which, i):
    pair = pairs_ref[which, i]
    return lax.shift_right_logical(pair, 6), lax.bitwise_and(pair, 63)


def near_kernel(cl, which, number, pairs_ref, *refs):
    blocks = refs[:number]
    if which:
        targets_ref, start_ref, kept_ref, near_out_ref, pieces_ref, sources_ref, total_ref = refs[number:]
    else:
        _, own_ref, kept_ref, near_out_ref, targets_ref, tail_ref, pieces_ref, sources_ref, total_ref = refs[number:]
        tail_ref[...] = blocks[0][:, blocks[0].shape[1] - tail_ref.shape[1]:]
    panels = near_out_ref.shape[1]
    clusters = panels // cl
    group = kept_ref.shape[1]
    fill_charges(pieces_ref, blocks, clusters, cl)
    fill_features(sources_ref, blocks, panels, cl)
    if which:
        total_ref[...] = jnp.zeros_like(total_ref)
    else:
        for c in range(clusters):
            targets_ref[c] = jnp.transpose(features_of(blocks[0], panels, c, cl, True)).astype(BF16)
            near_block(targets_ref[c], sources_ref[c], own_ref.at[c])
            total_ref[c] = self_product(pieces_ref[c], own_ref.at[c], cl)
    def step(m, _):
        pairs = [pair_at(pairs_ref, which, group * m + w) for w in range(group)]
        parts = []
        for w, (c, j) in enumerate(pairs):
            near_block(targets_ref[c], sources_ref[j], kept_ref.at[m, w])
            parts.append(near_product(pieces_ref[j], kept_ref.at[m, w], cl))
        for (c, j), part in zip(pairs, parts):
            total_ref[c] += part
        return 0

    lax.fori_loop(0, (pairs_ref[2 + which, 0] + group - 1) // group, step, 0)
    for c in range(clusters):
        lanes = slice(c * cl, (c + 1) * cl)
        near = folded(total_ref[c])
        near_out_ref[:, lanes] = start_ref[:, lanes] + near if which else near


def near_again_kernel(cl, which, number, pairs_ref, *refs):
    blocks = refs[:number]
    if which:
        start_ref, kept_ref, near_out_ref, pieces_ref, total_ref = refs[number:]
    else:
        _, own_ref, kept_ref, near_out_ref, tail_ref, pieces_ref, total_ref = refs[number:]
        tail_ref[...] = blocks[0][:, blocks[0].shape[1] - tail_ref.shape[1]:]
    clusters = near_out_ref.shape[1] // cl
    group = kept_ref.shape[1]
    fill_charges(pieces_ref, blocks, clusters, cl)
    if which:
        total_ref[...] = jnp.zeros_like(total_ref)
    else:
        for c in range(clusters):
            total_ref[c] = self_product(pieces_ref[c], own_ref.at[c], cl)

    def step(m, _):
        pairs = [pair_at(pairs_ref, which, group * m + w) for w in range(group)]
        parts = [near_product(pieces_ref[j], kept_ref.at[m, w], cl) for w, (c, j) in enumerate(pairs)]
        for (c, j), part in zip(pairs, parts):
            total_ref[c] += part
        return 0

    lax.fori_loop(0, (pairs_ref[2 + which, 0] + group - 1) // group, step, 0)
    for c in range(clusters):
        lanes = slice(c * cl, (c + 1) * cl)
        near = folded(total_ref[c])
        near_out_ref[:, lanes] = start_ref[:, lanes] + near if which else near


def load_window(tables, clusters, rank, pieces_ref, middle_ref):
    per = LANES // rank
    span = clusters * rank
    count = pieces_ref.shape[0] // per
    groups = span // LANES
    for at in range(count):
        (ref, first), g = tables[at // groups], at % groups
        tile = ref[:, first + g * LANES:first + (g + 1) * LANES]
        for s in range(per):
            pieces_ref[s * count + at] = stacked(pltpu.roll(tile, s * rank, 1) if s else tile)
        if middle_ref is not None:
            half = groups // 2
            row, lane = 8 * (g // half), first + span + g % half * LANES
            tile = ref[row:row + 8, lane:lane + LANES]
            for s in range(per):
                middle_ref[s * count + at] = pltpu.roll(tile, s * rank, 1) if s else tile


def six_tables(near_ref, far_ref, swapped_ref):
    width = near_ref.shape[1] // 2
    return (far_ref, 0), (far_ref, width), (near_ref, 0), (swapped_ref, width), (swapped_ref, 0), (swapped_ref, 3 * width)


def pick(source_ref, at_ref, c, g, per, lane):
    row = None
    for u in range(per):
        take = source_ref[at_ref[c, g * per + u]]
        row = take if row is None else jnp.where(lane == u, take, row)
    return row


def far_fields(gathered_ref, coupling_ref, fields_ref):
    for c in range(gathered_ref.shape[0]):
        field = quartered(dot_nt(gathered_ref[c], coupling_ref[c]))
        fields_ref[c] = stacked(jnp.concatenate([field, field], axis=1))


def far_potential(fields_ref, c, basis):
    return folded(dot_nn(fields_ref[c], basis))


def image_kernel(cl, rank, at_ref, near_pair_ref, far_pair_ref, swapped_ref, center_ref, area_ref, near_ref, basis_ref, krylov_ref, offsets_ref,
                 image_ref, payload_ref, heavy_ref, coupling_ref, pieces_ref, middle_ref, gathered_ref, fields_ref):
    rhs, panels = near_ref.shape
    clusters = panels // cl
    per = LANES // rank
    span = clusters * rank
    load_window(six_tables(near_pair_ref, far_pair_ref, swapped_ref), clusters, rank, pieces_ref, middle_ref)
    lane = lax.broadcasted_iota(jnp.int32, (1, LANES), 1) // rank
    for c in range(clusters):
        mine = [offsets_ref[3, k:k + 1, :] - center_ref[c:c + 1, k * LANES:(k + 1) * LANES] for k in range(3)]
        for g in range(at_ref.shape[1] // per):
            lanes = slice(g * LANES, (g + 1) * LANES)
            gathered_ref[c, :, lanes] = pick(pieces_ref, at_ref, c, g, per, lane)
            center = pick(middle_ref, at_ref, c, g, per, lane)
            gap = [(center[k:k + 1] + mine[k]) - offsets_ref[k] for k in range(3)]
            high, low = split(lax.rsqrt(gap[0] * gap[0] + gap[1] * gap[1] + gap[2] * gap[2] + SMOOTHING))
            coupling_ref[c, 0:rank, lanes] = high
            coupling_ref[c, rank:2 * rank, lanes] = low
    far_fields(gathered_ref, coupling_ref, fields_ref)
    squared = correlation = jnp.zeros((rhs, cl), F32)
    for c in range(clusters):
        lanes = slice(c * cl, (c + 1) * cl)
        basis = basis_ref[:, lanes]
        area = area_ref[c:c + 1, :]
        image = COULOMB * area * (near_ref[:, lanes] + far_potential(fields_ref, c, basis))
        charges = area * image
        image_ref[:, lanes] = image
        payload_ref[:, lanes] = charges
        heavy_ref[:, lanes] = charges
        payload_ref[:, panels + c * rank:panels + (c + 1) * rank] = moments_of(charges, basis)
        krylov = krylov_ref[:, lanes]
        squared = squared + krylov * krylov
        correlation = correlation + krylov * image
    squared = jnp.sum(squared, axis=1, keepdims=True)
    correlation = jnp.sum(correlation, axis=1, keepdims=True)
    local = ratio(correlation, squared)
    residual = image_ref[...] - local * krylov_ref[...]
    payload_ref[:, panels + span:] = in_lanes(squared, correlation, jnp.sum(residual * residual, axis=1, keepdims=True), local)


def far_again_kernel(cl, rank, at_ref, near_pair_ref, far_pair_ref, swapped_ref, near_ref, area_ref, coupling_ref, basis_ref,
                     image_ref, pieces_ref, gathered_ref, fields_ref):
    clusters = near_ref.shape[1] // cl
    per = LANES // rank
    load_window(six_tables(near_pair_ref, far_pair_ref, swapped_ref), clusters, rank, pieces_ref, None)
    lane = lax.broadcasted_iota(jnp.int32, (1, LANES), 1) // rank
    for c in range(clusters):
        for g in range(at_ref.shape[1] // per):
            gathered_ref[c, :, g * LANES:(g + 1) * LANES] = pick(pieces_ref, at_ref, c, g, per, lane)
    far_fields(gathered_ref, coupling_ref, fields_ref)
    for c in range(clusters):
        lanes = slice(c * cl, (c + 1) * cl)
        image_ref[:, lanes] = COULOMB * area_ref[c:c + 1, :] * (near_ref[:, lanes] + far_potential(fields_ref, c, basis_ref[:, lanes]))


def finish_kernel(total, one_ref, two_ref, image_ref, again_ref, krylov_ref, next_hbm, second_hbm, next_ref, second_ref, sems):
    squared, correlation, energy, local = merged([one_ref[...], two_ref[...]])
    projection = correlation / (squared + 1e-06)
    gap = projection - local
    scaling = 1.0 / jnp.sqrt((energy + gap * gap * squared) / total + 1e-06)
    moves = []
    part = next_ref.shape[1] // 4
    for h in range(4):
        lanes = slice(h * part, (h + 1) * part)
        image = image_ref[:, lanes]
        next_ref[:, lanes] = (image - projection * krylov_ref[:, lanes]) * scaling
        second_ref[:, lanes] = (again_ref[:, lanes] - projection * image) * scaling
        for held, hbm in ((next_ref, next_hbm), (second_ref, second_hbm)):
            moves.append(pltpu.make_async_copy(held.at[:, lanes], hbm.at[:, lanes], sems.at[len(moves)]))
            moves[-1].start()
    for move in moves:
        move.wait()


def ratio(correlation, squared):
    return jnp.where(squared > 0, correlation / jnp.where(squared > 0, squared, 1.0), 0.0)


def in_lanes(*columns):
    lane = lax.broadcasted_iota(jnp.int32, (columns[0].shape[0], LANES), 1)
    out = columns[-1]
    for i, column in enumerate(columns[:-1]):
        out = jnp.where(lane == i, column, out)
    return out


def merged(groups):
    squared = sum(group[:, 0:1] for group in groups)
    correlation = sum(group[:, 1:2] for group in groups)
    local = ratio(correlation, squared)
    energy = 0.0
    for group in groups:
        gap = local - group[:, 3:4]
        energy = energy + (group[:, 2:3] + gap * gap * group[:, 0:1])
    return squared, correlation, energy, local


def window_sums_kernel(payload_ref, partner_ref, near_pair_ref, far_pair_ref, swapped_ref, out_ref):
    width = near_pair_ref.shape[1] // 2
    ends = [(payload_ref, payload_ref.shape[1]), (partner_ref, partner_ref.shape[1])]
    ends += [(ref, end) for ref in (near_pair_ref, far_pair_ref, swapped_ref) for end in (width, 2 * width)]
    out_ref[...] = in_lanes(*merged([ref[:, end - LANES:end] for ref, end in ends]))


def merge_kernel(one_ref, two_ref, out_ref):
    out_ref[...] = in_lanes(*merged([one_ref[...], two_ref[...]]))


def call(kernel, outs, scratch, memory, *args, limit=10, us=1.0):
    spaces = {"s": pltpu.SMEM, "v": pltpu.VMEM, "p": pltpu.VMEM, "h": pltpu.HBM}
    ins, out_spaces = memory.split(">")
    pinned = {"h": pltpu.HBM, "p": pltpu.VMEM}
    return pl.pallas_call(
        kernel,
        out_shape=[pltpu.VMEM(*out) if m == "p" else jax.ShapeDtypeStruct(*out) for m, out in zip(out_spaces, outs)],
        in_specs=[pl.BlockSpec(memory_space=spaces[m]) for m in ins],
        out_specs=[pl.BlockSpec(memory_space=spaces[m]) for m in out_spaces],
        scratch_shapes=scratch,
        compiler_params=pltpu.CompilerParams(vmem_limit_bytes=limit * 2 ** 20),
        cost_estimate=pl.CostEstimate(flops=int(us * 5e8), bytes_accessed=int(us * 3.6e6), transcendentals=0),
    )(*(pltpu.with_memory_space_constraint(a, pinned[m]) if m in pinned else a for m, a in zip(ins, args)))


def body(vertices, panel_vertices, near_pairs, far_pairs, basis, krylov):
    clusters, slots = near_pairs.shape
    partners = far_pairs.shape[1]
    rhs, panels = krylov.shape
    rank = basis.shape[0]
    cl = panels // clusters
    vcl = vertices.shape[1] // clusters
    span = clusters * rank
    per = LANES // rank
    devices = lax.axis_size("clus")
    position = lax.axis_index("clus").reshape(1).astype(jnp.int32)
    offsets = proxy_offsets(rank)
    flat = np.concatenate([np.tile(offsets, (1, per)), np.zeros((rank - 3, LANES), np.float32)])
    offsets = jnp.asarray(np.concatenate([np.broadcast_to(offsets[:, :, None], (3, rank, LANES)), flat[None]]))
    width = span + span // 2
    pairing = [(i, i + 1 - 2 * (i % 2)) for i in range(devices)]
    bridging = [(i, i - 1 + 2 * (i % 2)) for i in range(1, devices - 1)] + [(0, 0), (devices - 1, devices - 1)]

    def move(value, pairs):
        return lax.ppermute(value, "clus", pairs)

    def outward(value, steps):
        return move(value, [(i, (i + steps * (1 - 2 * (i % 2))) % devices) for i in range(devices)])

    def exchange(payload, heavy):
        other = move(heavy, bridging)
        partner = move(payload, pairing)
        pair = jnp.concatenate([value[:, heavy.shape[1]:] for value in (payload, partner)], axis=1)
        return partner, other, outward(pair, 2), outward(pair, 4)

    def swapped(near_pair, far_pair, tail):
        return move(jnp.concatenate([near_pair, far_pair, tail], axis=1), pairing)

    whole = ((rhs, panels), F32)
    payload, heavy, area, centers, at, pairs, basis, krylov, offsets = call(
        functools.partial(prepare_kernel, cl, vcl, rank),
        [
            ((rhs, panels + 3 * cl + width), F32), ((rhs, panels + 3 * cl), F32), ((clusters, cl), F32), ((clusters, 3 * LANES), F32),
            (far_pairs.shape, jnp.int32), ((8, LANES), jnp.int32), ((2 * rank, panels), BF16), whole, (offsets.shape, F32),
        ],
        [
            pltpu.VMEM(vertices.shape, F32),
            pltpu.VMEM(panel_vertices.shape, jnp.int32),
            pltpu.VMEM(basis.shape, F32),
            pltpu.VMEM(far_pairs.shape, jnp.int32),
            pltpu.VMEM((slots, clusters), jnp.int32),
            pltpu.VMEM((3 * clusters, vcl), F32),
            pltpu.VMEM((3 * panels // LANES, LANES), jnp.int32),
            pltpu.SemaphoreType.DMA((7,)),
        ],
        "shhhhhhh>vvvvvvppp",
        position, vertices, panel_vertices, krylov, basis, far_pairs, near_pairs.T, offsets,
        us=1.5,
    )
    partner, other, near_pair, far_pair = exchange(payload, heavy)
    total = pltpu.VMEM((clusters, 2 * rhs, cl), F32)

    group = 4
    own = ((clusters, 2 * cl, cl), BF16)
    kept = ((clusters * (slots - 1) // group, group, 2 * cl, cl), BF16)

    def pieces(number):
        return pltpu.VMEM((number * clusters + 1, 2 * rhs, cl), BF16)

    def sources(number):
        return pltpu.VMEM((number * clusters + 1, FEATURES, cl), BF16)

    own_blocks, blocks, near, targets, tail = call(
        functools.partial(near_kernel, cl, 0, 1),
        [own, kept, whole, ((clusters, cl, FEATURES), BF16), ((rhs, LANES), F32)],
        [pieces(1), sources(1), total],
        "svv>ppvpv",
        pairs, payload, partner,
        us=8.0,
    )
    swap = swapped(near_pair, far_pair, tail)
    blocks_other, near = call(
        functools.partial(near_kernel, cl, 1, 2),
        [kept, whole],
        [pieces(2), sources(2), total],
        "svvpv>pv",
        pairs, partner, other, targets, near,
        us=4.0,
    )
    tiles = 6 * per * span // LANES
    window = pltpu.VMEM((tiles, 2 * rhs, LANES), BF16)
    gathered = pltpu.VMEM((clusters, 2 * rhs, partners * rank), BF16)
    fields = pltpu.VMEM((clusters, 2 * rhs, 2 * rank), BF16)
    image, payload, heavy, coupling = call(
        functools.partial(image_kernel, cl, rank),
        [whole, ((rhs, panels + span + LANES), F32), whole, ((clusters, 2 * rank, partners * rank), BF16)],
        [window, pltpu.VMEM((tiles, 8, LANES), F32), gathered, fields],
        "svvvvvvppp>vvvp",
        at, near_pair, far_pair, swap, centers, area, near, basis, krylov, offsets,
        us=4.5,
    )
    partner, other, near_pair, far_pair = exchange(payload, heavy)
    near, tail = call(
        functools.partial(near_again_kernel, cl, 0, 1),
        [whole, ((rhs, LANES), F32)],
        [pieces(1), total],
        "svvpp>vv",
        pairs, payload, partner, own_blocks, blocks,
        us=8.0,
    )
    swap = swapped(near_pair, far_pair, tail)
    (near,) = call(
        functools.partial(near_again_kernel, cl, 1, 2),
        [whole],
        [pieces(2), total],
        "svvvp>v",
        pairs, partner, other, near, blocks_other,
        us=2.0,
    )
    sums_shape = ((rhs, LANES), F32)
    (one,) = call(window_sums_kernel, [sums_shape], [], "vvvvv>v", payload, partner, near_pair, far_pair, swap, us=0.3)
    size = 8
    many = outward(one, size)
    while 2 * size < devices:
        (one,) = call(merge_kernel, [sums_shape], [], "vv>v", one, many, us=0.3)
        size = 2 * size
        many = outward(one, size)
    (again,) = call(
        functools.partial(far_again_kernel, cl, rank),
        [whole],
        [window, gathered, fields],
        "svvvvvpp>v",
        at, near_pair, far_pair, swap, near, area, coupling, basis,
        us=2.0,
    )
    here = pltpu.VMEM((rhs, panels), F32)
    return tuple(call(
        functools.partial(finish_kernel, panels * devices),
        [whole, whole],
        [here, here, pltpu.SemaphoreType.DMA((8,))],
        "vvvvp>hh",
        one, many, image, again, krylov,
    ))


def solution(mesh):
    whole = P(None, ("jobs", "clus"))
    rows = P(("jobs", "clus"), None)
    return jax.shard_map(
        body,
        mesh=mesh,
        in_specs=(whole, whole, rows, rows, whole, whole),
        out_specs=(whole, whole),
        check_vma=False,
    )
```

profile of v0, /device:TPU:0, one launch (start us, length us, event | category | flops | bytes accessed | tf_op | source)
XLA Modules:
  0.0 49.0 jit_solution(15656369759249507048)
XLA Ops:
  0.6 1.8 %shard_map.86 = (f32[16,5632]{1,0:T(8,128)S(1)}, f32[16,4864]{1,0:T(8,128)S(1)}, f32[16,256]{1,0:T(8,128)S(1)}, f32[16,384]{1,0:T(8,128)S(1)}, s32[16,32]{1,0:T(...) custom-call(s32[1]{0:T(128)} %bitcast.position_ref, ...), custom_call_target="tpu_custom_call" | custom-call | flops 750000000 | bytes 5400000 | tf_op jit(solution)/shard_map/pallas_call | solution.py:449
  2.4 0.5 %collective-permute-start = (f32[16,5632]{1,0:T(8,128)S(1)}, f32[16,5632]{1,0:T(8,128)S(1)}, u32[]{:S(2)}, u32[]{:S(2)}) collective-permute-start(f32[16,5632]{1,0:T(8,128)S(1)} %get-tuple-element.25.refs_0_), channel_id=1, source_target_pairs={{0,1},{1,0},{2,3},{3,2},{4,5},{5,4},{6,7},{7,6},{8,9},{9,8},{10,11... | collective-permute-start | bytes 1081352 | tf_op jit(solution)/shard_map/ppermute | solution.py:479
  3.0 0.7 %collective-permute-start.4 = (f32[16,4864]{1,0:T(8,128)S(1)}, f32[16,4864]{1,0:T(8,128)S(1)}, u32[]{:S(2)}, u32[]{:S(2)}) collective-permute-start(f32[16,4864]{1,0:T(8,128)S(1)} %get-tuple-element.30), channel_id=1, source_target_pairs={{1,2},{2,1},{3,4},{4,3},{5,6},{6,5},{7,8},{8,7},{9,10},{10,9},{11,... | collective-permute-start | bytes 933896 | tf_op jit(solution)/shard_map/ppermute | solution.py:479
  3.6 0.6 %collective-permute-done.refs_1_.refs_0_ = f32[16,5632]{1,0:T(8,128)S(1)} collective-permute-done((f32[16,5632]{1,0:T(8,128)S(1)}, f32[16,5632]{1,0:T(8,128)S(1)}, u32[]{:S(2)}, u32[]{:S(2)}) %collective-permute-start) | collective-permute-done | bytes 360480 | tf_op jit(solution)/shard_map/ppermute | solution.py:479
  4.3 4.8 %collective-permute-start.2 = (f32[16,1536]{1,0:T(8,128)S(1)}, f32[16,1536]{1,0:T(8,128)S(1)}, u32[]{:S(2)}, u32[]{:S(2)}) collective-permute-start(f32[16,1536]{1,0:T(8,128)S(1)} %pad_maximum_fusion.2), channel_id=1, source_target_pairs={{0,4},{1,13},{2,6},{3,15},{4,8},{5,1},{6,10},{7,3},{8,12},{9,5},{1... | collective-permute-start | bytes 294920 | tf_op jit(solution)/shard_map/ppermute | solution.py:479
  9.1 0.6 %collective-permute-start.1 = (f32[16,1536]{1,0:T(8,128)S(1)}, f32[16,1536]{1,0:T(8,128)S(1)}, u32[]{:S(2)}, u32[]{:S(2)}) collective-permute-start(f32[16,1536]{1,0:T(8,128)S(1)} %pad_maximum_fusion.2), channel_id=1, source_target_pairs={{0,2},{1,15},{2,4},{3,1},{4,6},{5,3},{6,8},{7,5},{8,10},{9,7},{10,... | collective-permute-start | bytes 294920 | tf_op jit(solution)/shard_map/ppermute | solution.py:479
  9.7 3.9 %shard_map.87 = (bf16[16,512,256]{2,1,0:T(8,128)(2,1)S(1)}, bf16[12,4,512,256]{3,2,1,0:T(8,128)(2,1)S(1)}, f32[16,4096]{1,0:T(8,128)S(1)}, bf16[16,256,80]{2,1,0:T(8,128)(2,1)S(1)}, f32[16,128]{1,0:T(8,128)S(1)}) custom-call(s32[8,128]{1,0:T(8,128)S(1)} %get-tuple-element.26.pairs_ref, f32[16,5632]{1,0:T(8,128)S(1)} %get-tuple-element.25.refs_0_, ...), custom_call_target="tpu_custom_call" | custom-call | flops 4000000000 | bytes 28800000 | tf_op jit(solution)/shard_map/pallas_call | solution.py:449
  13.6 5.2 %collective-permute-done.2.far_pair_ref = f32[16,1536]{1,0:T(8,128)S(1)} collective-permute-done((f32[16,1536]{1,0:T(8,128)S(1)}, f32[16,1536]{1,0:T(8,128)S(1)}, u32[]{:S(2)}, u32[]{:S(2)}) %collective-permute-start.2) | collective-permute-done | bytes 98336 | tf_op jit(solution)/shard_map/ppermute | solution.py:479
  18.8 0.0 collective-permute-done.1.near_pair_ref
  18.8 0.1 collective-permute-start.3
  18.9 0.0 collective-permute-done.4.refs_1_
  18.9 4.3 %shard_map.88 = (bf16[12,4,512,256]{3,2,1,0:T(8,128)(2,1)S(1)}, f32[16,4096]{1,0:T(8,128)S(1)}) custom-call(s32[8,128]{1,0:T(8,128)S(1)} %get-tuple-element.26.pairs_ref, f32[16,5632]{1,0:T(8,128)S(1)} %collective-permute-done.refs_1_.refs_0_, f32[16,4864]{1,0:T(8,128)S(1)} %collective-permute-done.4.refs_1_, ...), custom_call_target="tpu_custom_call" | custom-call | flops 2000000000 | bytes 14400000 | tf_op jit(solution)/shard_map/pallas_call | solution.py:449
  23.2 0.0 collective-permute-done.3.swapped_ref
  23.2 4.3 %shard_map.89 = (f32[16,4096]{1,0:T(8,128)S(1)}, f32[16,4736]{1,0:T(8,128)S(1)}, f32[16,4096]{1,0:T(8,128)S(1)}, bf16[16,64,1024]{2,1,0:T(8,128)(2,1)S(1)}) custom-call(s32[16,32]{1,0:T(8,128)S(1)} %get-tuple-element.24.at_ref, f32[16,1536]{1,0:T(8,128)S(1)} %collective-permute-done.1.near_pair_ref, f32[16,1536]{1,0:T(8,128)S(1)} %collective-permute-done.2.far_pair_ref, ...), custom_call_target="tpu_custom_call" | custom-call | flops 2249999872 | bytes 16200000 | tf_op jit(solution)/shard_map/pallas_call | solution.py:449
  27.5 0.1 collective-permute-start.5
  27.5 0.7 %collective-permute-start.10 = (f32[16,4096]{1,0:T(8,128)S(1)}, f32[16,4096]{1,0:T(8,128)S(1)}, u32[]{:S(2)}, u32[]{:S(2)}) collective-permute-start(f32[16,4096]{1,0:T(8,128)S(1)} %get-tuple-element.42), channel_id=1, source_target_pairs={{1,2},{2,1},{3,4},{4,3},{5,6},{6,5},{7,8},{8,7},{9,10},{10,9},{11,... | collective-permute-start | bytes 786440 | tf_op jit(solution)/shard_map/ppermute | solution.py:479
  28.2 0.9 %collective-permute-done.5.refs_1_.partner_ref.refs_0_ = f32[16,4736]{1,0:T(8,128)S(1)} collective-permute-done((f32[16,4736]{1,0:T(8,128)S(1)}, f32[16,4736]{1,0:T(8,128)S(1)}, u32[]{:S(2)}, u32[]{:S(2)}) %collective-permute-start.5) | collective-permute-done | bytes 303136 | tf_op jit(solution)/shard_map/ppermute | solution.py:479
  29.1 3.1 %collective-permute-start.7 = (f32[16,1280]{1,0:T(8,128)S(1)}, f32[16,1280]{1,0:T(8,128)S(1)}, u32[]{:S(2)}, u32[]{:S(2)}) collective-permute-start(f32[16,1280]{1,0:T(8,128)S(1)} %pad_maximum_fusion.3), channel_id=1, source_target_pairs={{0,4},{1,13},{2,6},{3,15},{4,8},{5,1},{6,10},{7,3},{8,12},{9,5},{1... | collective-permute-start | bytes 245768 | tf_op jit(solution)/shard_map/ppermute | solution.py:479
  32.2 0.0 collective-permute-start.6
  32.2 2.3 %shard_map.90 = (f32[16,4096]{1,0:T(8,128)S(1)}, f32[16,128]{1,0:T(8,128)S(1)}) custom-call(s32[8,128]{1,0:T(8,128)S(1)} %get-tuple-element.26.pairs_ref, f32[16,4736]{1,0:T(8,128)S(1)} %get-tuple-element.37.refs_0_.payload_ref, f32[16,4736]{1,0:T(8,128)S(1)} %collective-permute-done.5.refs_1_.partner_ref.refs_0_, ...), custom_call_target="tpu_custom_call" | custom-call | flops 4000000000 | bytes 28800000 | tf_op jit(solution)/shard_map/pallas_call | solution.py:449
  34.6 5.8 %collective-permute-done.7.far_pair_ref = f32[16,1280]{1,0:T(8,128)S(1)} collective-permute-done((f32[16,1280]{1,0:T(8,128)S(1)}, f32[16,1280]{1,0:T(8,128)S(1)}, u32[]{:S(2)}, u32[]{:S(2)}) %collective-permute-start.7) | collective-permute-done | bytes 81952 | tf_op jit(solution)/shard_map/ppermute | solution.py:479
  40.3 0.0 collective-permute-done.6.near_pair_ref
  40.4 0.1 collective-permute-start.8
  40.4 0.0 collective-permute-done.10.refs_1_
  40.5 2.4 %shard_map.92.near_ref = f32[16,4096]{1,0:T(8,128)S(1)} custom-call(s32[8,128]{1,0:T(8,128)S(1)} %get-tuple-element.26.pairs_ref, f32[16,4736]{1,0:T(8,128)S(1)} %collective-permute-done.5.refs_1_.partner_ref.refs_0_, f32[16,4096]{1,0:T(8,128)S(1)} %collective-permute-done.10.refs_1_, f32[16,4096]{1,0:T(8,128)S(1)} %get-tuple-element.43.refs_2_, ...), custom_call_target="tpu_custom_call" | custom-call | flops 1000000000 | bytes 7200000 | tf_op jit(solution)/shard_map/pallas_call | solution.py:449
  42.9 0.0 collective-permute-done.8.swapped_ref
  42.9 0.3 shard_map.91.one_ref
  43.2 0.0 collective-permute-start.9
  43.2 2.1 %shard_map.93.again_ref = f32[16,4096]{1,0:T(8,128)S(1)} custom-call(s32[16,32]{1,0:T(8,128)S(1)} %get-tuple-element.24.at_ref, f32[16,1280]{1,0:T(8,128)S(1)} %collective-permute-done.6.near_pair_ref, f32[16,1280]{1,0:T(8,128)S(1)} %collective-permute-done.7.far_pair_ref, f32[16,2688]{1,0:T(8,128)S(1)} %collective-permute-done.8.swapped_ref, ...), custom_call_target="tpu_custom_call" | custom-call | flops 1000000000 | bytes 7200000 | tf_op jit(solution)/shard_map/pallas_call | solution.py:449
  45.4 2.4 %collective-permute-done.9.two_ref = f32[16,128]{1,0:T(8,128)S(1)} collective-permute-done((f32[16,128]{1,0:T(8,128)S(1)}, f32[16,128]{1,0:T(8,128)S(1)}, u32[]{:S(2)}, u32[]{:S(2)}) %collective-permute-start.9) | collective-permute-done | bytes 8224 | tf_op jit(solution)/shard_map/ppermute | solution.py:479
  47.8 1.2 %shard_map.94 = (f32[16,4096]{1,0:T(8,128)}, f32[16,4096]{1,0:T(8,128)}) custom-call(f32[16,128]{1,0:T(8,128)S(1)} %shard_map.91.one_ref, f32[16,128]{1,0:T(8,128)S(1)} %collective-permute-done.9.two_ref, f32[16,4096]{1,0:T(8,128)S(1)} %get-tuple-element.41.image_ref, f32[16,4096]{1,0:T(8,128)S(1)} %shard_map.93.again_ref, ...), custom_call_target="tpu_custom_call" | custom-call | flops 500000000 | bytes 3600000 | tf_op jit(solution)/shard_map/pallas_call | solution.py:449
  (8 shorter events, 0.1 us)
Async XLA Ops:
  2.4 1.8 %collective-permute-start = (f32[16,5632]{1,0:T(8,128)S(1)}, f32[16,5632]{1,0:T(8,128)S(1)}, u32[]{:S(2)}, u32[]{:S(2)}) collective-permute-start(f32[16,5632]{1,0:T(8,128)S(1)} %get-tuple-element.25.refs_0_), channel_id=1, source_target_pairs={{0,1},{1,0},{2,3},{3,2},{4,5},{5,4},{6,7},{7,6},{8,9},{9,8},{10,11... | collective-permute-start | bytes 1081352 | tf_op jit(solution)/shard_map/ppermute | solution.py:479
  3.0 15.9 %collective-permute-start.4 = (f32[16,4864]{1,0:T(8,128)S(1)}, f32[16,4864]{1,0:T(8,128)S(1)}, u32[]{:S(2)}, u32[]{:S(2)}) collective-permute-start(f32[16,4864]{1,0:T(8,128)S(1)} %get-tuple-element.30), channel_id=1, source_target_pairs={{1,2},{2,1},{3,4},{4,3},{5,6},{6,5},{7,8},{8,7},{9,10},{10,9},{11,... | collective-permute-start | bytes 933896 | tf_op jit(solution)/shard_map/ppermute | solution.py:479
  4.3 14.5 %collective-permute-start.2 = (f32[16,1536]{1,0:T(8,128)S(1)}, f32[16,1536]{1,0:T(8,128)S(1)}, u32[]{:S(2)}, u32[]{:S(2)}) collective-permute-start(f32[16,1536]{1,0:T(8,128)S(1)} %pad_maximum_fusion.2), channel_id=1, source_target_pairs={{0,4},{1,13},{2,6},{3,15},{4,8},{5,1},{6,10},{7,3},{8,12},{9,5},{1... | collective-permute-start | bytes 294920 | tf_op jit(solution)/shard_map/ppermute | solution.py:479
  9.1 9.7 %collective-permute-start.1 = (f32[16,1536]{1,0:T(8,128)S(1)}, f32[16,1536]{1,0:T(8,128)S(1)}, u32[]{:S(2)}, u32[]{:S(2)}) collective-permute-start(f32[16,1536]{1,0:T(8,128)S(1)} %pad_maximum_fusion.2), channel_id=1, source_target_pairs={{0,2},{1,15},{2,4},{3,1},{4,6},{5,3},{6,8},{7,5},{8,10},{9,7},{10,... | collective-permute-start | bytes 294920 | tf_op jit(solution)/shard_map/ppermute | solution.py:479
  18.8 4.4 %collective-permute-start.3 = (f32[16,3200]{1,0:T(8,128)S(1)}, f32[16,3200]{1,0:T(8,128)S(1)}, u32[]{:S(2)}, u32[]{:S(2)}) collective-permute-start(f32[16,3200]{1,0:T(8,128)S(1)} %pad_maximum_fusion), channel_id=1, source_target_pairs={{0,1},{1,0},{2,3},{3,2},{4,5},{5,4},{6,7},{7,6},{8,9},{9,8},{10,11... | collective-permute-start | bytes 614408 | tf_op jit(solution)/shard_map/ppermute | solution.py:479
  27.5 1.7 %collective-permute-start.5 = (f32[16,4736]{1,0:T(8,128)S(1)}, f32[16,4736]{1,0:T(8,128)S(1)}, u32[]{:S(2)}, u32[]{:S(2)}) collective-permute-start(f32[16,4736]{1,0:T(8,128)S(1)} %get-tuple-element.37.refs_0_.payload_ref), channel_id=1, source_target_pairs={{0,1},{1,0},{2,3},{3,2},{4,5},{5,4},{6,7},{7,6},{8,9},{9,8},{10,11... | collective-permute-start | bytes 909320 | tf_op jit(solution)/shard_map/ppermute | solution.py:479
  27.5 12.9 %collective-permute-start.10 = (f32[16,4096]{1,0:T(8,128)S(1)}, f32[16,4096]{1,0:T(8,128)S(1)}, u32[]{:S(2)}, u32[]{:S(2)}) collective-permute-start(f32[16,4096]{1,0:T(8,128)S(1)} %get-tuple-element.42), channel_id=1, source_target_pairs={{1,2},{2,1},{3,4},{4,3},{5,6},{6,5},{7,8},{8,7},{9,10},{10,9},{11,... | collective-permute-start | bytes 786440 | tf_op jit(solution)/shard_map/ppermute | solution.py:479
  29.1 11.2 %collective-permute-start.7 = (f32[16,1280]{1,0:T(8,128)S(1)}, f32[16,1280]{1,0:T(8,128)S(1)}, u32[]{:S(2)}, u32[]{:S(2)}) collective-permute-start(f32[16,1280]{1,0:T(8,128)S(1)} %pad_maximum_fusion.3), channel_id=1, source_target_pairs={{0,4},{1,13},{2,6},{3,15},{4,8},{5,1},{6,10},{7,3},{8,12},{9,5},{1... | collective-permute-start | bytes 245768 | tf_op jit(solution)/shard_map/ppermute | solution.py:479
  32.2 8.1 %collective-permute-start.6 = (f32[16,1280]{1,0:T(8,128)S(1)}, f32[16,1280]{1,0:T(8,128)S(1)}, u32[]{:S(2)}, u32[]{:S(2)}) collective-permute-start(f32[16,1280]{1,0:T(8,128)S(1)} %pad_maximum_fusion.3), channel_id=1, source_target_pairs={{0,2},{1,15},{2,4},{3,1},{4,6},{5,3},{6,8},{7,5},{8,10},{9,7},{10,... | collective-permute-start | bytes 245768 | tf_op jit(solution)/shard_map/ppermute | solution.py:479
  40.4 2.5 %collective-permute-start.8 = (f32[16,2688]{1,0:T(8,128)S(1)}, f32[16,2688]{1,0:T(8,128)S(1)}, u32[]{:S(2)}, u32[]{:S(2)}) collective-permute-start(f32[16,2688]{1,0:T(8,128)S(1)} %pad_maximum_fusion.1), channel_id=1, source_target_pairs={{0,1},{1,0},{2,3},{3,2},{4,5},{5,4},{6,7},{7,6},{8,9},{9,8},{10,11... | collective-permute-start | bytes 516104 | tf_op jit(solution)/shard_map/ppermute | solution.py:479
  43.2 4.6 %collective-permute-start.9 = (f32[16,128]{1,0:T(8,128)S(1)}, f32[16,128]{1,0:T(8,128)S(1)}, u32[]{:S(2)}, u32[]{:S(2)}) collective-permute-start(f32[16,128]{1,0:T(8,128)S(1)} %shard_map.91.one_ref), channel_id=1, source_target_pairs={{0,8},{1,9},{2,10},{3,11},{4,12},{5,13},{6,14},{7,15},{8,0},{9,1},... | collective-permute-start | bytes 24584 | tf_op jit(solution)/shard_map/ppermute | solution.py:479
where the time goes:
time: 49.6 us; the launch traced here: 49 us
  Pallas kernels  22.6 us (46%)
  waiting for transfers between devices  14.9 us (30%)
  starting transfers between devices  10.6 us (21%)
  between operations  0.79 us (2%)
    pallas_call x9, Pallas kernels, call(): pl.pallas_call(kernel, out_shape=[pltpu.VMEM(*out) if m == 'p' else jax.S...  22.6 us
    ppermute x11, waiting for transfers between devices, move(): return lax.ppermute(value, 'clus', pairs)  14.9 us
    ppermute x11, starting transfers between devices, move(): return lax.ppermute(value, 'clus', pairs)  10.6 us
  transfers between devices with their start and end apart: 11, of which 5 were waited for; matrix products, arithmetic and copies ran while one was open for 0% of the time, Pallas kernels for 31%

commit v1 on v0

--- a/solution.py
+++ b/solution.py
@@ -199,12 +199,19 @@
     sources_ref[len(blocks) * clusters] = sources_ref[0]
 
 
-def near_block(target, source, out_ref):
+def near_block(target, source, pieces, out_ref, symmetric):
     cl = target.shape[0]
+    parts = []
     for first in range(0, cl, LANES):
-        high, low = split(lax.rsqrt(dot_nn(target[first:first + LANES, :], source)))
-        out_ref[first:first + LANES, :] = high
+        rows = slice(first, first + LANES)
+        high, low = split(lax.rsqrt(dot_nn(target[rows, :], source)))
+        out_ref[rows, :] = high
         out_ref[cl + first:cl + first + LANES, :] = low
+        if symmetric:
+            parts.append(dot_nn(pieces[:, rows], high) + dot_nn(pieces[:, rows], low))
+        else:
+            parts.append(dot_nt(pieces, high) + dot_nt(pieces, low))
+    return sum(parts[1:], parts[0]) if symmetric else jnp.concatenate(parts, axis=1)
 
 
 def self_product(pieces, block_ref, cl):
@@ -243,15 +250,13 @@
         total_ref[...] = jnp.zeros_like(total_ref)
     else:
         for c in range(clusters):
-            targets_ref[c] = jnp.transpose(features_of(blocks[0], panels, c, cl, True)).astype(BF16)
-            near_block(targets_ref[c], sources_ref[c], own_ref.at[c])
-            total_ref[c] = self_product(pieces_ref[c], own_ref.at[c], cl)
+            target = jnp.transpose(features_of(blocks[0], panels, c, cl, True)).astype(BF16)
+            targets_ref[c] = target
+            total_ref[c] = near_block(target, sources_ref[c], pieces_ref[c], own_ref.at[c], True)
     def step(m, _):
         pairs = [pair_at(pairs_ref, which, group * m + w) for w in range(group)]
-        parts = []
-        for w, (c, j) in enumerate(pairs):
-            near_block(targets_ref[c], sources_ref[j], kept_ref.at[m, w])
-            parts.append(near_product(pieces_ref[j], kept_ref.at[m, w], cl))
+        loaded = [(targets_ref[c], sources_ref[j], pieces_ref[j]) for c, j in pairs]
+        parts = [near_block(*one, kept_ref.at[m, w], False) for w, one in enumerate(loaded)]
         for (c, j), part in zip(pairs, parts):
             total_ref[c] += part
         return 0

time: 49.6 us -> 53.2 us (1.073); the launches traced: 49 us -> 53.2 us
  Pallas kernels: 22.6 us -> 26.9 us
    pallas_call x9, Pallas kernels: 22.6 us -> 26.9 us  [call(): pl.pallas_call(kernel, out_shape=[pltpu.VMEM(*out) if m == 'p' else jax.S...]
  transfers between devices with their start and end apart: 11 -> 11, of which waited for: 5 -> 5; matrix products, arithmetic and copies ran while one was open for 0% -> 0% of each run, Pallas kernels for 31% -> 36%
where the time goes in v1:
time: 53.2 us
  Pallas kernels  26.9 us (51%)
  waiting for transfers between devices  15.4 us (29%)
  starting transfers between devices  10.1 us (19%)
  between operations  0.79 us (1%)
    pallas_call x9, Pallas kernels, call(): pl.pallas_call(kernel, out_shape=[pltpu.VMEM(*out) if m == 'p' else jax.S...  26.9 us
    ppermute x11, waiting for transfers between devices, move(): return lax.ppermute(value, 'clus', pairs)  15.4 us
    ppermute x11, starting transfers between devices, move(): return lax.ppermute(value, 'clus', pairs)  10.1 us
  transfers between devices with their start and end apart: 11, of which 5 were waited for; matrix products, arithmetic and copies ran while one was open for 0% of the time, Pallas kernels for 36%

profile of v1, /device:TPU:0, one launch (start us, length us, event | category | flops | bytes accessed | tf_op | source)
XLA Modules:
  0.0 53.2 jit_solution(15199242388551125301)
XLA Ops:
  0.6 1.8 %shard_map.86 = (f32[16,5632]{1,0:T(8,128)S(1)}, f32[16,4864]{1,0:T(8,128)S(1)}, f32[16,256]{1,0:T(8,128)S(1)}, f32[16,384]{1,0:T(8,128)S(1)}, s32[16,32]{1,0:T(...) custom-call(s32[1]{0:T(128)} %bitcast.position_ref, ...), custom_call_target="tpu_custom_call" | custom-call | flops 750000000 | bytes 5400000 | tf_op jit(solution)/shard_map/pallas_call | solution.py:454
  2.4 0.5 collective-permute-start
  3.0 0.7 %collective-permute-start.4 = (f32[16,4864]{1,0:T(8,128)S(1)}, f32[16,4864]{1,0:T(8,128)S(1)}, u32[]{:S(2)}, u32[]{:S(2)}) collective-permute-start(f32[16,4864]{1,0:T(8,128)S(1)} %get-tuple-element.30), channel_id=1, source_target_pairs={{1,2},{2,1},{3,4},{4,3},{5,6},{6,5},{7,8},{8,7},{9,10},{10,9},{11,... | collective-permute-start | bytes 933896 | tf_op jit(solution)/shard_map/ppermute | solution.py:484
  3.6 0.6 %collective-permute-done.refs_1_.refs_0_ = f32[16,5632]{1,0:T(8,128)S(1)} collective-permute-done((f32[16,5632]{1,0:T(8,128)S(1)}, f32[16,5632]{1,0:T(8,128)S(1)}, u32[]{:S(2)}, u32[]{:S(2)}) %collective-permute-start) | collective-permute-done | bytes 360480 | tf_op jit(solution)/shard_map/ppermute | solution.py:484
  4.3 4.8 %collective-permute-start.2 = (f32[16,1536]{1,0:T(8,128)S(1)}, f32[16,1536]{1,0:T(8,128)S(1)}, u32[]{:S(2)}, u32[]{:S(2)}) collective-permute-start(f32[16,1536]{1,0:T(8,128)S(1)} %pad_maximum_fusion.2), channel_id=1, source_target_pairs={{0,4},{1,13},{2,6},{3,15},{4,8},{5,1},{6,10},{7,3},{8,12},{9,5},{1... | collective-permute-start | bytes 294920 | tf_op jit(solution)/shard_map/ppermute | solution.py:484
  9.1 0.6 %collective-permute-start.1 = (f32[16,1536]{1,0:T(8,128)S(1)}, f32[16,1536]{1,0:T(8,128)S(1)}, u32[]{:S(2)}, u32[]{:S(2)}) collective-permute-start(f32[16,1536]{1,0:T(8,128)S(1)} %pad_maximum_fusion.2), channel_id=1, source_target_pairs={{0,2},{1,15},{2,4},{3,1},{4,6},{5,3},{6,8},{7,5},{8,10},{9,7},{10,... | collective-permute-start | bytes 294920 | tf_op jit(solution)/shard_map/ppermute | solution.py:484
  9.7 5.2 %shard_map.87 = (bf16[16,512,256]{2,1,0:T(8,128)(2,1)S(1)}, bf16[12,4,512,256]{3,2,1,0:T(8,128)(2,1)S(1)}, f32[16,4096]{1,0:T(8,128)S(1)}, bf16[16,256,80]{2,1,0:T(8,128)(2,1)S(1)}, f32[16,128]{1,0:T(8,128)S(1)}) custom-call(s32[8,128]{1,0:T(8,128)S(1)} %get-tuple-element.26.pairs_ref, f32[16,5632]{1,0:T(8,128)S(1)} %get-tuple-element.25.refs_0_, ...), custom_call_target="tpu_custom_call" | custom-call | flops 4000000000 | bytes 28800000 | tf_op jit(solution)/shard_map/pallas_call | solution.py:454
  14.9 3.9 %collective-permute-done.2.far_pair_ref = f32[16,1536]{1,0:T(8,128)S(1)} collective-permute-done((f32[16,1536]{1,0:T(8,128)S(1)}, f32[16,1536]{1,0:T(8,128)S(1)}, u32[]{:S(2)}, u32[]{:S(2)}) %collective-permute-start.2) | collective-permute-done | bytes 98336 | tf_op jit(solution)/shard_map/ppermute | solution.py:484
  18.8 0.0 collective-permute-done.1.near_pair_ref
  18.8 0.1 collective-permute-start.3
  18.9 0.0 collective-permute-done.4.refs_1_
  18.9 7.2 %shard_map.88 = (bf16[12,4,512,256]{3,2,1,0:T(8,128)(2,1)S(1)}, f32[16,4096]{1,0:T(8,128)S(1)}) custom-call(s32[8,128]{1,0:T(8,128)S(1)} %get-tuple-element.26.pairs_ref, f32[16,5632]{1,0:T(8,128)S(1)} %collective-permute-done.refs_1_.refs_0_, f32[16,4864]{1,0:T(8,128)S(1)} %collective-permute-done.4.refs_1_, ...), custom_call_target="tpu_custom_call" | custom-call | flops 2000000000 | bytes 14400000 | tf_op jit(solution)/shard_map/pallas_call | solution.py:454
  26.1 0.0 collective-permute-done.3.swapped_ref
  26.1 4.3 %shard_map.89 = (f32[16,4096]{1,0:T(8,128)S(1)}, f32[16,4736]{1,0:T(8,128)S(1)}, f32[16,4096]{1,0:T(8,128)S(1)}, bf16[16,64,1024]{2,1,0:T(8,128)(2,1)S(1)}) custom-call(s32[16,32]{1,0:T(8,128)S(1)} %get-tuple-element.24.at_ref, f32[16,1536]{1,0:T(8,128)S(1)} %collective-permute-done.1.near_pair_ref, f32[16,1536]{1,0:T(8,128)S(1)} %collective-permute-done.2.far_pair_ref, ...), custom_call_target="tpu_custom_call" | custom-call | flops 2249999872 | bytes 16200000 | tf_op jit(solution)/shard_map/pallas_call | solution.py:454
  30.4 0.1 collective-permute-start.5
  30.5 0.7 %collective-permute-start.10 = (f32[16,4096]{1,0:T(8,128)S(1)}, f32[16,4096]{1,0:T(8,128)S(1)}, u32[]{:S(2)}, u32[]{:S(2)}) collective-permute-start(f32[16,4096]{1,0:T(8,128)S(1)} %get-tuple-element.42), channel_id=1, source_target_pairs={{1,2},{2,1},{3,4},{4,3},{5,6},{6,5},{7,8},{8,7},{9,10},{10,9},{11,... | collective-permute-start | bytes 786440 | tf_op jit(solution)/shard_map/ppermute | solution.py:484
  31.2 0.9 %collective-permute-done.5.refs_1_.partner_ref.refs_0_ = f32[16,4736]{1,0:T(8,128)S(1)} collective-permute-done((f32[16,4736]{1,0:T(8,128)S(1)}, f32[16,4736]{1,0:T(8,128)S(1)}, u32[]{:S(2)}, u32[]{:S(2)}) %collective-permute-start.5) | collective-permute-done | bytes 303136 | tf_op jit(solution)/shard_map/ppermute | solution.py:484
  32.1 0.8 %collective-permute-start.7 = (f32[16,1280]{1,0:T(8,128)S(1)}, f32[16,1280]{1,0:T(8,128)S(1)}, u32[]{:S(2)}, u32[]{:S(2)}) collective-permute-start(f32[16,1280]{1,0:T(8,128)S(1)} %pad_maximum_fusion.3), channel_id=1, source_target_pairs={{0,4},{1,13},{2,6},{3,15},{4,8},{5,1},{6,10},{7,3},{8,12},{9,5},{1... | collective-permute-start | bytes 245768 | tf_op jit(solution)/shard_map/ppermute | solution.py:484
  32.9 1.8 %collective-permute-start.6 = (f32[16,1280]{1,0:T(8,128)S(1)}, f32[16,1280]{1,0:T(8,128)S(1)}, u32[]{:S(2)}, u32[]{:S(2)}) collective-permute-start(f32[16,1280]{1,0:T(8,128)S(1)} %pad_maximum_fusion.3), channel_id=1, source_target_pairs={{0,2},{1,15},{2,4},{3,1},{4,6},{5,3},{6,8},{7,5},{8,10},{9,7},{10,... | collective-permute-start | bytes 245768 | tf_op jit(solution)/shard_map/ppermute | solution.py:484
  34.7 2.3 %shard_map.90 = (f32[16,4096]{1,0:T(8,128)S(1)}, f32[16,128]{1,0:T(8,128)S(1)}) custom-call(s32[8,128]{1,0:T(8,128)S(1)} %get-tuple-element.26.pairs_ref, f32[16,4736]{1,0:T(8,128)S(1)} %get-tuple-element.37.refs_0_.payload_ref, f32[16,4736]{1,0:T(8,128)S(1)} %collective-permute-done.5.refs_1_.partner_ref.refs_0_, ...), custom_call_target="tpu_custom_call" | custom-call | flops 4000000000 | bytes 28800000 | tf_op jit(solution)/shard_map/pallas_call | solution.py:454
  37.0 7.6 %collective-permute-done.7.far_pair_ref = f32[16,1280]{1,0:T(8,128)S(1)} collective-permute-done((f32[16,1280]{1,0:T(8,128)S(1)}, f32[16,1280]{1,0:T(8,128)S(1)}, u32[]{:S(2)}, u32[]{:S(2)}) %collective-permute-start.7) | collective-permute-done | bytes 81952 | tf_op jit(solution)/shard_map/ppermute | solution.py:484
  44.6 0.0 collective-permute-done.6.near_pair_ref
  44.6 0.1 collective-permute-start.8
  44.7 0.0 collective-permute-done.10.refs_1_
  44.7 2.4 %shard_map.92.near_ref = f32[16,4096]{1,0:T(8,128)S(1)} custom-call(s32[8,128]{1,0:T(8,128)S(1)} %get-tuple-element.26.pairs_ref, f32[16,4736]{1,0:T(8,128)S(1)} %collective-permute-done.5.refs_1_.partner_ref.refs_0_, f32[16,4096]{1,0:T(8,128)S(1)} %collective-permute-done.10.refs_1_, f32[16,4096]{1,0:T(8,128)S(1)} %get-tuple-element.43.refs_2_, ...), custom_call_target="tpu_custom_call" | custom-call | flops 1000000000 | bytes 7200000 | tf_op jit(solution)/shard_map/pallas_call | solution.py:454
  47.1 0.0 collective-permute-done.8.swapped_ref
  47.1 0.3 shard_map.91.one_ref
  47.5 0.0 collective-permute-start.9
  47.5 2.1 %shard_map.93.again_ref = f32[16,4096]{1,0:T(8,128)S(1)} custom-call(s32[16,32]{1,0:T(8,128)S(1)} %get-tuple-element.24.at_ref, f32[16,1280]{1,0:T(8,128)S(1)} %collective-permute-done.6.near_pair_ref, f32[16,1280]{1,0:T(8,128)S(1)} %collective-permute-done.7.far_pair_ref, f32[16,2688]{1,0:T(8,128)S(1)} %collective-permute-done.8.swapped_ref, ...), custom_call_target="tpu_custom_call" | custom-call | flops 1000000000 | bytes 7200000 | tf_op jit(solution)/shard_map/pallas_call | solution.py:454
  49.6 2.4 %collective-permute-done.9.two_ref = f32[16,128]{1,0:T(8,128)S(1)} collective-permute-done((f32[16,128]{1,0:T(8,128)S(1)}, f32[16,128]{1,0:T(8,128)S(1)}, u32[]{:S(2)}, u32[]{:S(2)}) %collective-permute-start.9) | collective-permute-done | bytes 8224 | tf_op jit(solution)/shard_map/ppermute | solution.py:484
  52.0 1.2 %shard_map.94 = (f32[16,4096]{1,0:T(8,128)}, f32[16,4096]{1,0:T(8,128)}) custom-call(f32[16,128]{1,0:T(8,128)S(1)} %shard_map.91.one_ref, f32[16,128]{1,0:T(8,128)S(1)} %collective-permute-done.9.two_ref, f32[16,4096]{1,0:T(8,128)S(1)} %get-tuple-element.41.image_ref, f32[16,4096]{1,0:T(8,128)S(1)} %shard_map.93.again_ref, ...), custom_call_target="tpu_custom_call" | custom-call | flops 500000000 | bytes 3600000 | tf_op jit(solution)/shard_map/pallas_call | solution.py:454
  (8 shorter events, 0.1 us)
Async XLA Ops:
  2.4 1.8 %collective-permute-start = (f32[16,5632]{1,0:T(8,128)S(1)}, f32[16,5632]{1,0:T(8,128)S(1)}, u32[]{:S(2)}, u32[]{:S(2)}) collective-permute-start(f32[16,5632]{1,0:T(8,128)S(1)} %get-tuple-element.25.refs_0_), channel_id=1, source_target_pairs={{0,1},{1,0},{2,3},{3,2},{4,5},{5,4},{6,7},{7,6},{8,9},{9,8},{10,11... | collective-permute-start | bytes 1081352 | tf_op jit(solution)/shard_map/ppermute | solution.py:484
  3.0 15.9 %collective-permute-start.4 = (f32[16,4864]{1,0:T(8,128)S(1)}, f32[16,4864]{1,0:T(8,128)S(1)}, u32[]{:S(2)}, u32[]{:S(2)}) collective-permute-start(f32[16,4864]{1,0:T(8,128)S(1)} %get-tuple-element.30), channel_id=1, source_target_pairs={{1,2},{2,1},{3,4},{4,3},{5,6},{6,5},{7,8},{8,7},{9,10},{10,9},{11,... | collective-permute-start | bytes 933896 | tf_op jit(solution)/shard_map/ppermute | solution.py:484
  4.3 14.5 %collective-permute-start.2 = (f32[16,1536]{1,0:T(8,128)S(1)}, f32[16,1536]{1,0:T(8,128)S(1)}, u32[]{:S(2)}, u32[]{:S(2)}) collective-permute-start(f32[16,1536]{1,0:T(8,128)S(1)} %pad_maximum_fusion.2), channel_id=1, source_target_pairs={{0,4},{1,13},{2,6},{3,15},{4,8},{5,1},{6,10},{7,3},{8,12},{9,5},{1... | collective-permute-start | bytes 294920 | tf_op jit(solution)/shard_map/ppermute | solution.py:484
  9.1 9.7 %collective-permute-start.1 = (f32[16,1536]{1,0:T(8,128)S(1)}, f32[16,1536]{1,0:T(8,128)S(1)}, u32[]{:S(2)}, u32[]{:S(2)}) collective-permute-start(f32[16,1536]{1,0:T(8,128)S(1)} %pad_maximum_fusion.2), channel_id=1, source_target_pairs={{0,2},{1,15},{2,4},{3,1},{4,6},{5,3},{6,8},{7,5},{8,10},{9,7},{10,... | collective-permute-start | bytes 294920 | tf_op jit(solution)/shard_map/ppermute | solution.py:484
  18.8 7.3 %collective-permute-start.3 = (f32[16,3200]{1,0:T(8,128)S(1)}, f32[16,3200]{1,0:T(8,128)S(1)}, u32[]{:S(2)}, u32[]{:S(2)}) collective-permute-start(f32[16,3200]{1,0:T(8,128)S(1)} %pad_maximum_fusion), channel_id=1, source_target_pairs={{0,1},{1,0},{2,3},{3,2},{4,5},{5,4},{6,7},{7,6},{8,9},{9,8},{10,11... | collective-permute-start | bytes 614408 | tf_op jit(solution)/shard_map/ppermute | solution.py:484
  30.4 1.7 %collective-permute-start.5 = (f32[16,4736]{1,0:T(8,128)S(1)}, f32[16,4736]{1,0:T(8,128)S(1)}, u32[]{:S(2)}, u32[]{:S(2)}) collective-permute-start(f32[16,4736]{1,0:T(8,128)S(1)} %get-tuple-element.37.refs_0_.payload_ref), channel_id=1, source_target_pairs={{0,1},{1,0},{2,3},{3,2},{4,5},{5,4},{6,7},{7,6},{8,9},{9,8},{10,11... | collective-permute-start | bytes 909320 | tf_op jit(solution)/shard_map/ppermute | solution.py:484
  30.5 14.2 %collective-permute-start.10 = (f32[16,4096]{1,0:T(8,128)S(1)}, f32[16,4096]{1,0:T(8,128)S(1)}, u32[]{:S(2)}, u32[]{:S(2)}) collective-permute-start(f32[16,4096]{1,0:T(8,128)S(1)} %get-tuple-element.42), channel_id=1, source_target_pairs={{1,2},{2,1},{3,4},{4,3},{5,6},{6,5},{7,8},{8,7},{9,10},{10,9},{11,... | collective-permute-start | bytes 786440 | tf_op jit(solution)/shard_map/ppermute | solution.py:484
  32.1 12.5 %collective-permute-start.7 = (f32[16,1280]{1,0:T(8,128)S(1)}, f32[16,1280]{1,0:T(8,128)S(1)}, u32[]{:S(2)}, u32[]{:S(2)}) collective-permute-start(f32[16,1280]{1,0:T(8,128)S(1)} %pad_maximum_fusion.3), channel_id=1, source_target_pairs={{0,4},{1,13},{2,6},{3,15},{4,8},{5,1},{6,10},{7,3},{8,12},{9,5},{1... | collective-permute-start | bytes 245768 | tf_op jit(solution)/shard_map/ppermute | solution.py:484
  32.9 11.7 %collective-permute-start.6 = (f32[16,1280]{1,0:T(8,128)S(1)}, f32[16,1280]{1,0:T(8,128)S(1)}, u32[]{:S(2)}, u32[]{:S(2)}) collective-permute-start(f32[16,1280]{1,0:T(8,128)S(1)} %pad_maximum_fusion.3), channel_id=1, source_target_pairs={{0,2},{1,15},{2,4},{3,1},{4,6},{5,3},{6,8},{7,5},{8,10},{9,7},{10,... | collective-permute-start | bytes 245768 | tf_op jit(solution)/shard_map/ppermute | solution.py:484
  44.6 2.5 %collective-permute-start.8 = (f32[16,2688]{1,0:T(8,128)S(1)}, f32[16,2688]{1,0:T(8,128)S(1)}, u32[]{:S(2)}, u32[]{:S(2)}) collective-permute-start(f32[16,2688]{1,0:T(8,128)S(1)} %pad_maximum_fusion.1), channel_id=1, source_target_pairs={{0,1},{1,0},{2,3},{3,2},{4,5},{5,4},{6,7},{7,6},{8,9},{9,8},{10,11... | collective-permute-start | bytes 516104 | tf_op jit(solution)/shard_map/ppermute | solution.py:484
  47.5 4.6 %collective-permute-start.9 = (f32[16,128]{1,0:T(8,128)S(1)}, f32[16,128]{1,0:T(8,128)S(1)}, u32[]{:S(2)}, u32[]{:S(2)}) collective-permute-start(f32[16,128]{1,0:T(8,128)S(1)} %shard_map.91.one_ref), channel_id=1, source_target_pairs={{0,8},{1,9},{2,10},{3,11},{4,12},{5,13},{6,14},{7,15},{8,0},{9,1},... | collective-permute-start | bytes 24584 | tf_op jit(solution)/shard_map/ppermute | solution.py:484

commit v2 on v1

--- a/solution.py
+++ b/solution.py
@@ -43,6 +43,10 @@
 
 def dot_nt(left, right):
     return lax.dot_general(left, right, (((1,), (1,)), ((), ())), preferred_element_type=F32)
+
+
+def dot_tn(left, right):
+    return lax.dot_general(left, right, (((0,), (0,)), ((), ())), preferred_element_type=F32)
 
 
 def dot_nn(left, right):
@@ -199,27 +203,20 @@
     sources_ref[len(blocks) * clusters] = sources_ref[0]
 
 
-def near_block(target, source, pieces, out_ref, symmetric):
-    cl = target.shape[0]
+def near_block(source, target, pieces, out_ref):
+    cl = source.shape[1]
     parts = []
     for first in range(0, cl, LANES):
         rows = slice(first, first + LANES)
-        high, low = split(lax.rsqrt(dot_nn(target[rows, :], source)))
+        high, low = split(lax.rsqrt(dot_tn(source[:, rows], target)))
         out_ref[rows, :] = high
         out_ref[cl + first:cl + first + LANES, :] = low
-        if symmetric:
-            parts.append(dot_nn(pieces[:, rows], high) + dot_nn(pieces[:, rows], low))
-        else:
-            parts.append(dot_nt(pieces, high) + dot_nt(pieces, low))
-    return sum(parts[1:], parts[0]) if symmetric else jnp.concatenate(parts, axis=1)
-
-
-def self_product(pieces, block_ref, cl):
+        parts.append(dot_nn(pieces[:, rows], high) + dot_nn(pieces[:, rows], low))
+    return sum(parts[1:], parts[0])
+
+
+def near_product(pieces, block_ref, cl):
     return dot_nn(pieces, block_ref[0:cl, :]) + dot_nn(pieces, block_ref[cl:2 * cl, :])
-
-
-def near_product(pieces, block_ref, cl):
-    return dot_nt(pieces, block_ref[0:cl, :]) + dot_nt(pieces, block_ref[cl:2 * cl, :])
 
 
 def fill_charges(pieces_ref, blocks, clusters, cl):
@@ -250,13 +247,13 @@
         total_ref[...] = jnp.zeros_like(total_ref)
     else:
         for c in range(clusters):
-            target = jnp.transpose(features_of(blocks[0], panels, c, cl, True)).astype(BF16)
+            target = features_of(blocks[0], panels, c, cl, True).astype(BF16)
             targets_ref[c] = target
-            total_ref[c] = near_block(target, sources_ref[c], pieces_ref[c], own_ref.at[c], True)
+            total_ref[c] = near_block(sources_ref[c], target, pieces_ref[c], own_ref.at[c])
     def step(m, _):
         pairs = [pair_at(pairs_ref, which, group * m + w) for w in range(group)]
-        loaded = [(targets_ref[c], sources_ref[j], pieces_ref[j]) for c, j in pairs]
-        parts = [near_block(*one, kept_ref.at[m, w], False) for w, one in enumerate(loaded)]
+        loaded = [(sources_ref[j], targets_ref[c], pieces_ref[j]) for c, j in pairs]
+        parts = [near_block(*one, kept_ref.at[m, w]) for w, one in enumerate(loaded)]
         for (c, j), part in zip(pairs, parts):
             total_ref[c] += part
         return 0
@@ -282,7 +279,7 @@
         total_ref[...] = jnp.zeros_like(total_ref)
     else:
         for c in range(clusters):
-            total_ref[c] = self_product(pieces_ref[c], own_ref.at[c], cl)
+            total_ref[c] = near_product(pieces_ref[c], own_ref.at[c], cl)
 
     def step(m, _):
         pairs = [pair_at(pairs_ref, which, group * m + w) for w in range(group)]
@@ -531,7 +528,7 @@
 
     own_blocks, blocks, near, targets, tail = call(
         functools.partial(near_kernel, cl, 0, 1),
-        [own, kept, whole, ((clusters, cl, FEATURES), BF16), ((rhs, LANES), F32)],
+        [own, kept, whole, ((clusters, FEATURES, cl), BF16), ((rhs, LANES), F32)],
         [pieces(1), sources(1), total],
         "svv>ppvpv",
         pairs, payload, partner,

time: 53.2 us -> 47.7 us (0.90)
  Pallas kernels: 26.9 us -> 20.5 us
  starting transfers between devices: 10.1 us -> 12.1 us
  waiting for transfers between devices: 15.4 us -> 14.4 us
    pallas_call x9, Pallas kernels: 26.9 us -> 20.5 us  [call(): pl.pallas_call(kernel, out_shape=[pltpu.VMEM(*out) if m == 'p' else jax.S...]
    ppermute x11, starting transfers between devices: 10.1 us -> 12.1 us  [move(): return lax.ppermute(value, 'clus', pairs)]
    ppermute x11, waiting for transfers between devices: 15.4 us -> 14.4 us  [move(): return lax.ppermute(value, 'clus', pairs)]
  transfers between devices with their start and end apart: 11 -> 11, of which waited for: 5 -> 5; matrix products, arithmetic and copies ran while one was open for 0% -> 0% of each run, Pallas kernels for 36% -> 27%
where the time goes in v2:
time: 47.7 us; the launch traced here: 47.8 us
  Pallas kernels  20.5 us (43%)
  waiting for transfers between devices  14.4 us (30%)
  starting transfers between devices  12.1 us (25%)
  between operations  0.77 us (2%)
    pallas_call x9, Pallas kernels, call(): pl.pallas_call(kernel, out_shape=[pltpu.VMEM(*out) if m == 'p' else jax.S...  20.5 us
    ppermute x11, waiting for transfers between devices, move(): return lax.ppermute(value, 'clus', pairs)  14.4 us
    ppermute x11, starting transfers between devices, move(): return lax.ppermute(value, 'clus', pairs)  12.1 us
  transfers between devices with their start and end apart: 11, of which 5 were waited for; matrix products, arithmetic and copies ran while one was open for 0% of the time, Pallas kernels for 27%

profile of v2, /device:TPU:0, one launch (start us, length us, event | category | flops | bytes accessed | tf_op | source)
XLA Modules:
  0.0 47.8 jit_solution(14457897719747477203)
XLA Ops:
  0.6 1.8 %shard_map.86 = (f32[16,5632]{1,0:T(8,128)S(1)}, f32[16,4864]{1,0:T(8,128)S(1)}, f32[16,256]{1,0:T(8,128)S(1)}, f32[16,384]{1,0:T(8,128)S(1)}, s32[16,32]{1,0:T(...) custom-call(s32[1]{0:T(128)} %bitcast.position_ref, ...), custom_call_target="tpu_custom_call" | custom-call | flops 750000000 | bytes 5400000 | tf_op jit(solution)/shard_map/pallas_call | solution.py:451
  2.4 0.5 %collective-permute-start = (f32[16,5632]{1,0:T(8,128)S(1)}, f32[16,5632]{1,0:T(8,128)S(1)}, u32[]{:S(2)}, u32[]{:S(2)}) collective-permute-start(f32[16,5632]{1,0:T(8,128)S(1)} %get-tuple-element.25.refs_0_), channel_id=1, source_target_pairs={{0,1},{1,0},{2,3},{3,2},{4,5},{5,4},{6,7},{7,6},{8,9},{9,8},{10,11... | collective-permute-start | bytes 1081352 | tf_op jit(solution)/shard_map/ppermute | solution.py:481
  3.0 0.7 %collective-permute-start.4 = (f32[16,4864]{1,0:T(8,128)S(1)}, f32[16,4864]{1,0:T(8,128)S(1)}, u32[]{:S(2)}, u32[]{:S(2)}) collective-permute-start(f32[16,4864]{1,0:T(8,128)S(1)} %get-tuple-element.30), channel_id=1, source_target_pairs={{1,2},{2,1},{3,4},{4,3},{5,6},{6,5},{7,8},{8,7},{9,10},{10,9},{11,... | collective-permute-start | bytes 933896 | tf_op jit(solution)/shard_map/ppermute | solution.py:481
  3.6 0.6 %collective-permute-done.refs_1_.refs_0_ = f32[16,5632]{1,0:T(8,128)S(1)} collective-permute-done((f32[16,5632]{1,0:T(8,128)S(1)}, f32[16,5632]{1,0:T(8,128)S(1)}, u32[]{:S(2)}, u32[]{:S(2)}) %collective-permute-start) | collective-permute-done | bytes 360480 | tf_op jit(solution)/shard_map/ppermute | solution.py:481
  4.3 4.8 %collective-permute-start.2 = (f32[16,1536]{1,0:T(8,128)S(1)}, f32[16,1536]{1,0:T(8,128)S(1)}, u32[]{:S(2)}, u32[]{:S(2)}) collective-permute-start(f32[16,1536]{1,0:T(8,128)S(1)} %pad_maximum_fusion.2), channel_id=1, source_target_pairs={{0,4},{1,13},{2,6},{3,15},{4,8},{5,1},{6,10},{7,3},{8,12},{9,5},{1... | collective-permute-start | bytes 294920 | tf_op jit(solution)/shard_map/ppermute | solution.py:481
  9.1 0.6 %collective-permute-start.1 = (f32[16,1536]{1,0:T(8,128)S(1)}, f32[16,1536]{1,0:T(8,128)S(1)}, u32[]{:S(2)}, u32[]{:S(2)}) collective-permute-start(f32[16,1536]{1,0:T(8,128)S(1)} %pad_maximum_fusion.2), channel_id=1, source_target_pairs={{0,2},{1,15},{2,4},{3,1},{4,6},{5,3},{6,8},{7,5},{8,10},{9,7},{10,... | collective-permute-start | bytes 294920 | tf_op jit(solution)/shard_map/ppermute | solution.py:481
  9.7 3.9 %shard_map.87 = (bf16[16,512,256]{2,1,0:T(8,128)(2,1)S(1)}, bf16[12,4,512,256]{3,2,1,0:T(8,128)(2,1)S(1)}, f32[16,4096]{1,0:T(8,128)S(1)}, bf16[16,80,256]{2,1,0:T(8,128)(2,1)S(1)}, f32[16,128]{1,0:T(8,128)S(1)}) custom-call(s32[8,128]{1,0:T(8,128)S(1)} %get-tuple-element.26.pairs_ref, f32[16,5632]{1,0:T(8,128)S(1)} %get-tuple-element.25.refs_0_, ...), custom_call_target="tpu_custom_call" | custom-call | flops 4000000000 | bytes 28800000 | tf_op jit(solution)/shard_map/pallas_call | solution.py:451
  13.6 5.2 %collective-permute-done.2.far_pair_ref = f32[16,1536]{1,0:T(8,128)S(1)} collective-permute-done((f32[16,1536]{1,0:T(8,128)S(1)}, f32[16,1536]{1,0:T(8,128)S(1)}, u32[]{:S(2)}, u32[]{:S(2)}) %collective-permute-start.2) | collective-permute-done | bytes 98336 | tf_op jit(solution)/shard_map/ppermute | solution.py:481
  18.8 0.0 collective-permute-done.1.near_pair_ref
  18.8 0.1 collective-permute-start.3
  18.9 0.0 collective-permute-done.4.refs_1_
  18.9 2.9 %shard_map.88 = (bf16[12,4,512,256]{3,2,1,0:T(8,128)(2,1)S(1)}, f32[16,4096]{1,0:T(8,128)S(1)}) custom-call(s32[8,128]{1,0:T(8,128)S(1)} %get-tuple-element.26.pairs_ref, f32[16,5632]{1,0:T(8,128)S(1)} %collective-permute-done.refs_1_.refs_0_, f32[16,4864]{1,0:T(8,128)S(1)} %collective-permute-done.4.refs_1_, ...), custom_call_target="tpu_custom_call" | custom-call | flops 2000000000 | bytes 14400000 | tf_op jit(solution)/shard_map/pallas_call | solution.py:451
  21.8 0.0 collective-permute-done.3.swapped_ref
  21.8 4.3 %shard_map.89 = (f32[16,4096]{1,0:T(8,128)S(1)}, f32[16,4736]{1,0:T(8,128)S(1)}, f32[16,4096]{1,0:T(8,128)S(1)}, bf16[16,64,1024]{2,1,0:T(8,128)(2,1)S(1)}) custom-call(s32[16,32]{1,0:T(8,128)S(1)} %get-tuple-element.24.at_ref, f32[16,1536]{1,0:T(8,128)S(1)} %collective-permute-done.1.near_pair_ref, f32[16,1536]{1,0:T(8,128)S(1)} %collective-permute-done.2.far_pair_ref, ...), custom_call_target="tpu_custom_call" | custom-call | flops 2249999872 | bytes 16200000 | tf_op jit(solution)/shard_map/pallas_call | solution.py:451
  26.1 0.6 %collective-permute-start.5 = (f32[16,4736]{1,0:T(8,128)S(1)}, f32[16,4736]{1,0:T(8,128)S(1)}, u32[]{:S(2)}, u32[]{:S(2)}) collective-permute-start(f32[16,4736]{1,0:T(8,128)S(1)} %get-tuple-element.37.refs_0_.payload_ref), channel_id=1, source_target_pairs={{0,1},{1,0},{2,3},{3,2},{4,5},{5,4},{6,7},{7,6},{8,9},{9,8},{10,11... | collective-permute-start | bytes 909320 | tf_op jit(solution)/shard_map/ppermute | solution.py:481
  26.7 0.7 %collective-permute-start.10 = (f32[16,4096]{1,0:T(8,128)S(1)}, f32[16,4096]{1,0:T(8,128)S(1)}, u32[]{:S(2)}, u32[]{:S(2)}) collective-permute-start(f32[16,4096]{1,0:T(8,128)S(1)} %get-tuple-element.42), channel_id=1, source_target_pairs={{1,2},{2,1},{3,4},{4,3},{5,6},{6,5},{7,8},{8,7},{9,10},{10,9},{11,... | collective-permute-start | bytes 786440 | tf_op jit(solution)/shard_map/ppermute | solution.py:481
  27.3 0.5 %collective-permute-done.5.refs_1_.partner_ref.refs_0_ = f32[16,4736]{1,0:T(8,128)S(1)} collective-permute-done((f32[16,4736]{1,0:T(8,128)S(1)}, f32[16,4736]{1,0:T(8,128)S(1)}, u32[]{:S(2)}, u32[]{:S(2)}) %collective-permute-start.5) | collective-permute-done | bytes 303136 | tf_op jit(solution)/shard_map/ppermute | solution.py:481
  27.9 2.2 %collective-permute-start.7 = (f32[16,1280]{1,0:T(8,128)S(1)}, f32[16,1280]{1,0:T(8,128)S(1)}, u32[]{:S(2)}, u32[]{:S(2)}) collective-permute-start(f32[16,1280]{1,0:T(8,128)S(1)} %pad_maximum_fusion.3), channel_id=1, source_target_pairs={{0,4},{1,13},{2,6},{3,15},{4,8},{5,1},{6,10},{7,3},{8,12},{9,5},{1... | collective-permute-start | bytes 245768 | tf_op jit(solution)/shard_map/ppermute | solution.py:481
  30.1 1.4 %collective-permute-start.6 = (f32[16,1280]{1,0:T(8,128)S(1)}, f32[16,1280]{1,0:T(8,128)S(1)}, u32[]{:S(2)}, u32[]{:S(2)}) collective-permute-start(f32[16,1280]{1,0:T(8,128)S(1)} %pad_maximum_fusion.3), channel_id=1, source_target_pairs={{0,2},{1,15},{2,4},{3,1},{4,6},{5,3},{6,8},{7,5},{8,10},{9,7},{10,... | collective-permute-start | bytes 245768 | tf_op jit(solution)/shard_map/ppermute | solution.py:481
  31.6 2.3 %shard_map.90 = (f32[16,4096]{1,0:T(8,128)S(1)}, f32[16,128]{1,0:T(8,128)S(1)}) custom-call(s32[8,128]{1,0:T(8,128)S(1)} %get-tuple-element.26.pairs_ref, f32[16,4736]{1,0:T(8,128)S(1)} %get-tuple-element.37.refs_0_.payload_ref, f32[16,4736]{1,0:T(8,128)S(1)} %collective-permute-done.5.refs_1_.partner_ref.refs_0_, ...), custom_call_target="tpu_custom_call" | custom-call | flops 4000000000 | bytes 28800000 | tf_op jit(solution)/shard_map/pallas_call | solution.py:451
  33.9 6.1 %collective-permute-done.7.far_pair_ref = f32[16,1280]{1,0:T(8,128)S(1)} collective-permute-done((f32[16,1280]{1,0:T(8,128)S(1)}, f32[16,1280]{1,0:T(8,128)S(1)}, u32[]{:S(2)}, u32[]{:S(2)}) %collective-permute-start.7) | collective-permute-done | bytes 81952 | tf_op jit(solution)/shard_map/ppermute | solution.py:481
  40.0 0.0 collective-permute-done.6.near_pair_ref
  40.0 0.1 collective-permute-start.8
  40.1 0.0 collective-permute-done.10.refs_1_
  40.1 1.6 %shard_map.92.near_ref = f32[16,4096]{1,0:T(8,128)S(1)} custom-call(s32[8,128]{1,0:T(8,128)S(1)} %get-tuple-element.26.pairs_ref, f32[16,4736]{1,0:T(8,128)S(1)} %collective-permute-done.5.refs_1_.partner_ref.refs_0_, f32[16,4096]{1,0:T(8,128)S(1)} %collective-permute-done.10.refs_1_, f32[16,4096]{1,0:T(8,128)S(1)} %get-tuple-element.43.refs_2_, ...), custom_call_target="tpu_custom_call" | custom-call | flops 1000000000 | bytes 7200000 | tf_op jit(solution)/shard_map/pallas_call | solution.py:451
  41.7 0.0 collective-permute-done.8.swapped_ref
  41.7 0.3 shard_map.91.one_ref
  42.0 0.5 %collective-permute-start.9 = (f32[16,128]{1,0:T(8,128)S(1)}, f32[16,128]{1,0:T(8,128)S(1)}, u32[]{:S(2)}, u32[]{:S(2)}) collective-permute-start(f32[16,128]{1,0:T(8,128)S(1)} %shard_map.91.one_ref), channel_id=1, source_target_pairs={{0,8},{1,9},{2,10},{3,11},{4,12},{5,13},{6,14},{7,15},{8,0},{9,1},... | collective-permute-start | bytes 24584 | tf_op jit(solution)/shard_map/ppermute | solution.py:481
  42.6 2.1 %shard_map.93.again_ref = f32[16,4096]{1,0:T(8,128)S(1)} custom-call(s32[16,32]{1,0:T(8,128)S(1)} %get-tuple-element.24.at_ref, f32[16,1280]{1,0:T(8,128)S(1)} %collective-permute-done.6.near_pair_ref, f32[16,1280]{1,0:T(8,128)S(1)} %collective-permute-done.7.far_pair_ref, f32[16,2688]{1,0:T(8,128)S(1)} %collective-permute-done.8.swapped_ref, ...), custom_call_target="tpu_custom_call" | custom-call | flops 1000000000 | bytes 7200000 | tf_op jit(solution)/shard_map/pallas_call | solution.py:451
  44.7 1.9 %collective-permute-done.9.two_ref = f32[16,128]{1,0:T(8,128)S(1)} collective-permute-done((f32[16,128]{1,0:T(8,128)S(1)}, f32[16,128]{1,0:T(8,128)S(1)}, u32[]{:S(2)}, u32[]{:S(2)}) %collective-permute-start.9) | collective-permute-done | bytes 8224 | tf_op jit(solution)/shard_map/ppermute | solution.py:481
  46.6 1.2 %shard_map.94 = (f32[16,4096]{1,0:T(8,128)}, f32[16,4096]{1,0:T(8,128)}) custom-call(f32[16,128]{1,0:T(8,128)S(1)} %shard_map.91.one_ref, f32[16,128]{1,0:T(8,128)S(1)} %collective-permute-done.9.two_ref, f32[16,4096]{1,0:T(8,128)S(1)} %get-tuple-element.41.image_ref, f32[16,4096]{1,0:T(8,128)S(1)} %shard_map.93.again_ref, ...), custom_call_target="tpu_custom_call" | custom-call | flops 500000000 | bytes 3600000 | tf_op jit(solution)/shard_map/pallas_call | solution.py:451
  (8 shorter events, 0.1 us)
Async XLA Ops:
  2.4 1.8 %collective-permute-start = (f32[16,5632]{1,0:T(8,128)S(1)}, f32[16,5632]{1,0:T(8,128)S(1)}, u32[]{:S(2)}, u32[]{:S(2)}) collective-permute-start(f32[16,5632]{1,0:T(8,128)S(1)} %get-tuple-element.25.refs_0_), channel_id=1, source_target_pairs={{0,1},{1,0},{2,3},{3,2},{4,5},{5,4},{6,7},{7,6},{8,9},{9,8},{10,11... | collective-permute-start | bytes 1081352 | tf_op jit(solution)/shard_map/ppermute | solution.py:481
  3.0 15.9 %collective-permute-start.4 = (f32[16,4864]{1,0:T(8,128)S(1)}, f32[16,4864]{1,0:T(8,128)S(1)}, u32[]{:S(2)}, u32[]{:S(2)}) collective-permute-start(f32[16,4864]{1,0:T(8,128)S(1)} %get-tuple-element.30), channel_id=1, source_target_pairs={{1,2},{2,1},{3,4},{4,3},{5,6},{6,5},{7,8},{8,7},{9,10},{10,9},{11,... | collective-permute-start | bytes 933896 | tf_op jit(solution)/shard_map/ppermute | solution.py:481
  4.3 14.5 %collective-permute-start.2 = (f32[16,1536]{1,0:T(8,128)S(1)}, f32[16,1536]{1,0:T(8,128)S(1)}, u32[]{:S(2)}, u32[]{:S(2)}) collective-permute-start(f32[16,1536]{1,0:T(8,128)S(1)} %pad_maximum_fusion.2), channel_id=1, source_target_pairs={{0,4},{1,13},{2,6},{3,15},{4,8},{5,1},{6,10},{7,3},{8,12},{9,5},{1... | collective-permute-start | bytes 294920 | tf_op jit(solution)/shard_map/ppermute | solution.py:481
  9.1 9.7 %collective-permute-start.1 = (f32[16,1536]{1,0:T(8,128)S(1)}, f32[16,1536]{1,0:T(8,128)S(1)}, u32[]{:S(2)}, u32[]{:S(2)}) collective-permute-start(f32[16,1536]{1,0:T(8,128)S(1)} %pad_maximum_fusion.2), channel_id=1, source_target_pairs={{0,2},{1,15},{2,4},{3,1},{4,6},{5,3},{6,8},{7,5},{8,10},{9,7},{10,... | collective-permute-start | bytes 294920 | tf_op jit(solution)/shard_map/ppermute | solution.py:481
  18.8 3.0 %collective-permute-start.3 = (f32[16,3200]{1,0:T(8,128)S(1)}, f32[16,3200]{1,0:T(8,128)S(1)}, u32[]{:S(2)}, u32[]{:S(2)}) collective-permute-start(f32[16,3200]{1,0:T(8,128)S(1)} %pad_maximum_fusion), channel_id=1, source_target_pairs={{0,1},{1,0},{2,3},{3,2},{4,5},{5,4},{6,7},{7,6},{8,9},{9,8},{10,11... | collective-permute-start | bytes 614408 | tf_op jit(solution)/shard_map/ppermute | solution.py:481
  26.1 1.8 %collective-permute-start.5 = (f32[16,4736]{1,0:T(8,128)S(1)}, f32[16,4736]{1,0:T(8,128)S(1)}, u32[]{:S(2)}, u32[]{:S(2)}) collective-permute-start(f32[16,4736]{1,0:T(8,128)S(1)} %get-tuple-element.37.refs_0_.payload_ref), channel_id=1, source_target_pairs={{0,1},{1,0},{2,3},{3,2},{4,5},{5,4},{6,7},{7,6},{8,9},{9,8},{10,11... | collective-permute-start | bytes 909320 | tf_op jit(solution)/shard_map/ppermute | solution.py:481
  26.7 13.4 %collective-permute-start.10 = (f32[16,4096]{1,0:T(8,128)S(1)}, f32[16,4096]{1,0:T(8,128)S(1)}, u32[]{:S(2)}, u32[]{:S(2)}) collective-permute-start(f32[16,4096]{1,0:T(8,128)S(1)} %get-tuple-element.42), channel_id=1, source_target_pairs={{1,2},{2,1},{3,4},{4,3},{5,6},{6,5},{7,8},{8,7},{9,10},{10,9},{11,... | collective-permute-start | bytes 786440 | tf_op jit(solution)/shard_map/ppermute | solution.py:481
  27.9 12.1 %collective-permute-start.7 = (f32[16,1280]{1,0:T(8,128)S(1)}, f32[16,1280]{1,0:T(8,128)S(1)}, u32[]{:S(2)}, u32[]{:S(2)}) collective-permute-start(f32[16,1280]{1,0:T(8,128)S(1)} %pad_maximum_fusion.3), channel_id=1, source_target_pairs={{0,4},{1,13},{2,6},{3,15},{4,8},{5,1},{6,10},{7,3},{8,12},{9,5},{1... | collective-permute-start | bytes 245768 | tf_op jit(solution)/shard_map/ppermute | solution.py:481
  30.1 9.9 %collective-permute-start.6 = (f32[16,1280]{1,0:T(8,128)S(1)}, f32[16,1280]{1,0:T(8,128)S(1)}, u32[]{:S(2)}, u32[]{:S(2)}) collective-permute-start(f32[16,1280]{1,0:T(8,128)S(1)} %pad_maximum_fusion.3), channel_id=1, source_target_pairs={{0,2},{1,15},{2,4},{3,1},{4,6},{5,3},{6,8},{7,5},{8,10},{9,7},{10,... | collective-permute-start | bytes 245768 | tf_op jit(solution)/shard_map/ppermute | solution.py:481
  40.0 1.7 %collective-permute-start.8 = (f32[16,2688]{1,0:T(8,128)S(1)}, f32[16,2688]{1,0:T(8,128)S(1)}, u32[]{:S(2)}, u32[]{:S(2)}) collective-permute-start(f32[16,2688]{1,0:T(8,128)S(1)} %pad_maximum_fusion.1), channel_id=1, source_target_pairs={{0,1},{1,0},{2,3},{3,2},{4,5},{5,4},{6,7},{7,6},{8,9},{9,8},{10,11... | collective-permute-start | bytes 516104 | tf_op jit(solution)/shard_map/ppermute | solution.py:481
  42.0 4.6 %collective-permute-start.9 = (f32[16,128]{1,0:T(8,128)S(1)}, f32[16,128]{1,0:T(8,128)S(1)}, u32[]{:S(2)}, u32[]{:S(2)}) collective-permute-start(f32[16,128]{1,0:T(8,128)S(1)} %shard_map.91.one_ref), channel_id=1, source_target_pairs={{0,8},{1,9},{2,10},{3,11},{4,12},{5,13},{6,14},{7,15},{8,0},{9,1},... | collective-permute-start | bytes 24584 | tf_op jit(solution)/shard_map/ppermute | solution.py:481

commit v3 on v2

--- a/solution.py
+++ b/solution.py
@@ -98,12 +98,12 @@
     return out.astype(jnp.int32)
 
 
-def prepare_kernel(cl, vcl, rank, position_ref, vertices_hbm, corners_hbm, krylov_hbm, basis_hbm, far_hbm, near_hbm, offsets_hbm,
-                   payload_ref, heavy_ref, area_ref, center_ref, at_ref, pairs_ref, basis_ref, krylov_ref, offsets_ref,
+def prepare_kernel(cl, vcl, rank, position_ref, vertices_hbm, corners_hbm, krylov_hbm, basis_hbm, far_hbm, near_hbm, offsets_hbm, weights_hbm,
+                   payload_ref, table_ref, area_ref, center_ref, at_ref, pairs_ref, basis_ref, krylov_ref, offsets_ref, weights_ref,
                    vertices_ref, corners_ref, raw_ref, far_ref, near_ref, mesh_ref, local_ref, sems):
     moves = copies((
         (vertices_hbm, vertices_ref), (corners_hbm, corners_ref), (krylov_hbm, krylov_ref), (basis_hbm, raw_ref),
-        (far_hbm, far_ref), (near_hbm, near_ref), (offsets_hbm, offsets_ref),
+        (far_hbm, far_ref), (near_hbm, near_ref), (offsets_hbm, offsets_ref), (weights_hbm.at[position_ref[0]], weights_ref),
     ), sems)
     rhs, panels = krylov_ref.shape
     clusters = panels // cl
@@ -124,23 +124,21 @@
             middle = (corner[0][k] + corner[1][k] + corner[2][k]) / 3.0
             lanes = slice(panels + k * cl + h * LANES, panels + k * cl + (h + 1) * LANES)
             payload_ref[:, lanes] = middle
-            heavy_ref[:, lanes] = middle
             sums[k] = middle if h == 0 else sums[k] + middle
         one = [corner[1][k] - corner[0][k] for k in range(3)]
         two = [corner[2][k] - corner[0][k] for k in range(3)]
         normal = [one[1] * two[2] - one[2] * two[1], one[2] * two[0] - one[0] * two[2], one[0] * two[1] - one[1] * two[0]]
         area_ref[:, h * LANES:(h + 1) * LANES] = 0.5 * jnp.sqrt(normal[0] * normal[0] + normal[1] * normal[1] + normal[2] * normal[2])
     span = clusters * rank
-    table = panels + 3 * cl
     mine = lax.broadcasted_iota(jnp.int32, (clusters, span), 1) // rank == lax.broadcasted_iota(jnp.int32, (clusters, span), 0)
     half = span // 2
-    payload_ref[:, table + span:] = jnp.zeros_like(payload_ref[:, table + span:])
+    table_ref[:, span:] = jnp.zeros_like(table_ref[:, span:])
     for k in range(3):
         center = jnp.sum(sums[k], axis=1, keepdims=True) / cl
         center_ref[:, k * LANES:(k + 1) * LANES] = jnp.broadcast_to(center, (clusters, LANES))
         row = jnp.sum(jnp.where(mine, center, 0.0), axis=0, keepdims=True)
-        payload_ref[k:k + 1, table + span:] = row[:, 0:half]
-        payload_ref[8 + k:9 + k, table + span:] = row[:, half:]
+        table_ref[k:k + 1, span:] = row[:, 0:half]
+        table_ref[8 + k:9 + k, span:] = row[:, half:]
     moves[2].wait()
     moves[3].wait()
     for c in range(clusters):
@@ -148,8 +146,7 @@
         basis_ref[:, lanes] = stacked(raw_ref[:, lanes])
         charges = area_ref[c:c + 1, :] * krylov_ref[:, lanes]
         payload_ref[:, lanes] = charges
-        heavy_ref[:, lanes] = charges
-        payload_ref[:, table + c * rank:table + (c + 1) * rank] = moments_of(charges, basis_ref[:, lanes])
+        table_ref[:, c * rank:(c + 1) * rank] = moments_of(charges, basis_ref[:, lanes])
     moves[4].wait()
     far = far_ref[...]
     step = (lax.div(far, clusters) - position_ref[0]) * (1 - 2 * lax.rem(position_ref[0], 2))
@@ -160,6 +157,7 @@
     moves[5].wait()
     pairs_ref[...] = pair_list(near_ref[...], position_ref[0], clusters)
     moves[6].wait()
+    moves[7].wait()
 
 
 def features_of(payload_ref, panels, c, cl, target):
@@ -236,8 +234,8 @@
     if which:
         targets_ref, start_ref, kept_ref, near_out_ref, pieces_ref, sources_ref, total_ref = refs[number:]
     else:
-        _, own_ref, kept_ref, near_out_ref, targets_ref, tail_ref, pieces_ref, sources_ref, total_ref = refs[number:]
-        tail_ref[...] = blocks[0][:, blocks[0].shape[1] - tail_ref.shape[1]:]
+        table_ref, own_ref, kept_ref, near_out_ref, targets_ref, tail_ref, pieces_ref, sources_ref, total_ref = refs[number:]
+        tail_ref[...] = table_ref[:, table_ref.shape[1] - LANES:]
     panels = near_out_ref.shape[1]
     clusters = panels // cl
     group = kept_ref.shape[1]
@@ -270,8 +268,8 @@
     if which:
         start_ref, kept_ref, near_out_ref, pieces_ref, total_ref = refs[number:]
     else:
-        _, own_ref, kept_ref, near_out_ref, tail_ref, pieces_ref, total_ref = refs[number:]
-        tail_ref[...] = blocks[0][:, blocks[0].shape[1] - tail_ref.shape[1]:]
+        table_ref, own_ref, kept_ref, near_out_ref, tail_ref, pieces_ref, total_ref = refs[number:]
+        tail_ref[...] = table_ref[:, table_ref.shape[1] - LANES:]
     clusters = near_out_ref.shape[1] // cl
     group = kept_ref.shape[1]
     fill_charges(pieces_ref, blocks, clusters, cl)
@@ -313,9 +311,10 @@
                 middle_ref[s * count + at] = pltpu.roll(tile, s * rank, 1) if s else tile
 
 
-def six_tables(near_ref, far_ref, swapped_ref):
-    width = near_ref.shape[1] // 2
-    return (far_ref, 0), (far_ref, width), (near_ref, 0), (swapped_ref, width), (swapped_ref, 0), (swapped_ref, 3 * width)
+def six_tables(other_ref, far_ref, swapped_ref):
+    width = far_ref.shape[1] // 2
+    last = other_ref.shape[1] - width
+    return (far_ref, 0), (far_ref, width), (other_ref, last), (swapped_ref, 0), (swapped_ref, width), (swapped_ref, 3 * width)
 
 
 def pick(source_ref, at_ref, c, g, per, lane):
@@ -336,13 +335,13 @@
     return folded(dot_nn(fields_ref[c], basis))
 
 
-def image_kernel(cl, rank, at_ref, near_pair_ref, far_pair_ref, swapped_ref, center_ref, area_ref, near_ref, basis_ref, krylov_ref, offsets_ref,
-                 image_ref, payload_ref, heavy_ref, coupling_ref, pieces_ref, middle_ref, gathered_ref, fields_ref):
+def image_kernel(cl, rank, at_ref, other_ref, far_pair_ref, swapped_ref, center_ref, area_ref, near_ref, basis_ref, krylov_ref, offsets_ref,
+                 image_ref, payload_ref, table_ref, coupling_ref, pieces_ref, middle_ref, gathered_ref, fields_ref):
     rhs, panels = near_ref.shape
     clusters = panels // cl
     per = LANES // rank
     span = clusters * rank
-    load_window(six_tables(near_pair_ref, far_pair_ref, swapped_ref), clusters, rank, pieces_ref, middle_ref)
+    load_window(six_tables(other_ref, far_pair_ref, swapped_ref), clusters, rank, pieces_ref, middle_ref)
     lane = lax.broadcasted_iota(jnp.int32, (1, LANES), 1) // rank
     for c in range(clusters):
         mine = [offsets_ref[3, k:k + 1, :] - center_ref[c:c + 1, k * LANES:(k + 1) * LANES] for k in range(3)]
@@ -364,8 +363,7 @@
         charges = area * image
         image_ref[:, lanes] = image
         payload_ref[:, lanes] = charges
-        heavy_ref[:, lanes] = charges
-        payload_ref[:, panels + c * rank:panels + (c + 1) * rank] = moments_of(charges, basis)
+        table_ref[:, c * rank:(c + 1) * rank] = moments_of(charges, basis)
         krylov = krylov_ref[:, lanes]
         squared = squared + krylov * krylov
         correlation = correlation + krylov * image
@@ -373,14 +371,14 @@
     correlation = jnp.sum(correlation, axis=1, keepdims=True)
     local = ratio(correlation, squared)
     residual = image_ref[...] - local * krylov_ref[...]
-    payload_ref[:, panels + span:] = in_lanes(squared, correlation, jnp.sum(residual * residual, axis=1, keepdims=True), local)
-
-
-def far_again_kernel(cl, rank, at_ref, near_pair_ref, far_pair_ref, swapped_ref, near_ref, area_ref, coupling_ref, basis_ref,
+    table_ref[:, span:] = in_lanes(squared, correlation, jnp.sum(residual * residual, axis=1, keepdims=True), local)
+
+
+def far_again_kernel(cl, rank, at_ref, other_ref, far_pair_ref, swapped_ref, near_ref, area_ref, coupling_ref, basis_ref,
                      image_ref, pieces_ref, gathered_ref, fields_ref):
     clusters = near_ref.shape[1] // cl
     per = LANES // rank
-    load_window(six_tables(near_pair_ref, far_pair_ref, swapped_ref), clusters, rank, pieces_ref, None)
+    load_window(six_tables(other_ref, far_pair_ref, swapped_ref), clusters, rank, pieces_ref, None)
     lane = lax.broadcasted_iota(jnp.int32, (1, LANES), 1) // rank
     for c in range(clusters):
         for g in range(at_ref.shape[1] // per):
@@ -422,26 +420,61 @@
     return out
 
 
-def merged(groups):
-    squared = sum(group[:, 0:1] for group in groups)
-    correlation = sum(group[:, 1:2] for group in groups)
+def merged(groups, weights=None):
+    weights = weights or [1.0] * len(groups)
+    squared = sum(weight * group[:, 0:1] for group, weight in zip(groups, weights))
+    correlation = sum(weight * group[:, 1:2] for group, weight in zip(groups, weights))
     local = ratio(correlation, squared)
     energy = 0.0
-    for group in groups:
+    for group, weight in zip(groups, weights):
         gap = local - group[:, 3:4]
-        energy = energy + (group[:, 2:3] + gap * gap * group[:, 0:1])
+        energy = energy + weight * (group[:, 2:3] + gap * gap * group[:, 0:1])
     return squared, correlation, energy, local
 
 
-def window_sums_kernel(payload_ref, partner_ref, near_pair_ref, far_pair_ref, swapped_ref, out_ref):
-    width = near_pair_ref.shape[1] // 2
-    ends = [(payload_ref, payload_ref.shape[1]), (partner_ref, partner_ref.shape[1])]
-    ends += [(ref, end) for ref in (near_pair_ref, far_pair_ref, swapped_ref) for end in (width, 2 * width)]
-    out_ref[...] = in_lanes(*merged([ref[:, end - LANES:end] for ref, end in ends]))
-
-
 def merge_kernel(one_ref, two_ref, out_ref):
-    out_ref[...] = in_lanes(*merged([one_ref[...], two_ref[...]]))
+    out_ref[...] = in_lanes(*merged([ref[:, ref.shape[1] - LANES:] for ref in (one_ref, two_ref)]))
+
+
+def known_sums_kernel(weights_ref, own_ref, partner_ref, other_ref, far_ref, swapped_ref, *outs):
+    width = own_ref.shape[1]
+    last = other_ref.shape[1]
+    ends = [(own_ref, width), (partner_ref, width), (other_ref, last - width), (other_ref, last), (far_ref, width), (far_ref, 2 * width)]
+    ends += [(swapped_ref, width * i) for i in range(1, 5)]
+    groups = [ref[:, end - LANES:end] for ref, end in ends]
+    for side, out_ref in enumerate(outs):
+        weights = [weights_ref[0:1, 16 * side + i:16 * side + i + 1] for i in range(len(groups))]
+        out_ref[...] = in_lanes(*merged(groups, weights))
+
+
+def completing(devices, *moves):
+    partner, other, far = ({target: source for source, target in move} for move in moves)
+    slots = []
+    for i in range(devices):
+        near = [other[i], far[i], other[partner[i]], far[partner[i]]]
+        slots.append([i, partner[i]] + [device for one in near for device in (one, partner[one])])
+    known = [set(slot) for slot in slots]
+    everyone = set(range(devices))
+    target_of = {}
+
+    def matched(target, seen):
+        for source in range(devices):
+            if source not in seen and known[target] | known[source] == everyone:
+                seen.add(source)
+                if source not in target_of or matched(target_of[source], seen):
+                    target_of[source] = target
+                    return True
+        return False
+
+    if not all(matched(i, set()) for i in range(devices)):
+        return None
+    weights = np.zeros((devices, 8, LANES), np.float32)
+    for i in range(devices):
+        for at, device in enumerate(slots[i]):
+            if device not in slots[i][:at]:
+                weights[i, :, at] = 1.0
+                weights[i, :, 16 + at] = device not in known[target_of[i]]
+    return sorted(target_of.items()), weights
 
 
 def call(kernel, outs, scratch, memory, *args, limit=10, us=1.0):
@@ -476,28 +509,32 @@
     width = span + span // 2
     pairing = [(i, i + 1 - 2 * (i % 2)) for i in range(devices)]
     bridging = [(i, i - 1 + 2 * (i % 2)) for i in range(1, devices - 1)] + [(0, 0), (devices - 1, devices - 1)]
+    outward = [(i, i + 4 - 8 * (i % 2)) for i in range(devices)]
+    outward = [(i, j) for i, j in outward if 0 <= j < devices] + [(3, 0), (devices - 4, devices - 1)]
+    outward_once = outward + [(1, 2), (devices - 2, devices - 3)]
+    outward_around = outward + [(devices - 2, 2), (1, devices - 3)]
+    completion = completing(devices, pairing, bridging, outward_around)
+    weights = completion[1] if completion else np.zeros((devices, 8, LANES), np.float32)
 
     def move(value, pairs):
         return lax.ppermute(value, "clus", pairs)
 
-    def outward(value, steps):
-        return move(value, [(i, (i + steps * (1 - 2 * (i % 2))) % devices) for i in range(devices)])
-
-    def exchange(payload, heavy):
-        other = move(heavy, bridging)
-        partner = move(payload, pairing)
-        pair = jnp.concatenate([value[:, heavy.shape[1]:] for value in (payload, partner)], axis=1)
-        return partner, other, outward(pair, 2), outward(pair, 4)
-
-    def swapped(near_pair, far_pair, tail):
-        return move(jnp.concatenate([near_pair, far_pair, tail], axis=1), pairing)
+    def exchange(payload, table, away):
+        beside = move(table, pairing)
+        pair = jnp.concatenate([table, beside], axis=1)
+        other = move(jnp.concatenate([payload, pair], axis=1), bridging)
+        return beside, other, move(pair, away), move(payload, pairing)
+
+    def swapped(other, far_pair, tail):
+        pair = other[:, other.shape[1] - far_pair.shape[1]:]
+        return move(jnp.concatenate([pair, far_pair, tail], axis=1), pairing)
 
     whole = ((rhs, panels), F32)
-    payload, heavy, area, centers, at, pairs, basis, krylov, offsets = call(
+    payload, table, area, centers, at, pairs, basis, krylov, offsets, weights = call(
         functools.partial(prepare_kernel, cl, vcl, rank),
         [
-            ((rhs, panels + 3 * cl + width), F32), ((rhs, panels + 3 * cl), F32), ((clusters, cl), F32), ((clusters, 3 * LANES), F32),
-            (far_pairs.shape, jnp.int32), ((8, LANES), jnp.int32), ((2 * rank, panels), BF16), whole, (offsets.shape, F32),
+            ((rhs, panels + 3 * cl), F32), ((rhs, width), F32), ((clusters, cl), F32), ((clusters, 3 * LANES), F32),
+            (far_pairs.shape, jnp.int32), ((8, LANES), jnp.int32), ((2 * rank, panels), BF16), whole, (offsets.shape, F32), ((8, LANES), F32),
         ],
         [
             pltpu.VMEM(vertices.shape, F32),
@@ -507,13 +544,13 @@
             pltpu.VMEM((slots, clusters), jnp.int32),
             pltpu.VMEM((3 * clusters, vcl), F32),
             pltpu.VMEM((3 * panels // LANES, LANES), jnp.int32),
-            pltpu.SemaphoreType.DMA((7,)),
+            pltpu.SemaphoreType.DMA((8,)),
         ],
-        "shhhhhhh>vvvvvvppp",
-        position, vertices, panel_vertices, krylov, basis, far_pairs, near_pairs.T, offsets,
+        "shhhhhhhh>vvvvvvpppp",
+        position, vertices, panel_vertices, krylov, basis, far_pairs, near_pairs.T, offsets, jnp.asarray(weights),
         us=1.5,
     )
-    partner, other, near_pair, far_pair = exchange(payload, heavy)
+    beside, other, far_pair, partner = exchange(payload, table, outward_once)
     total = pltpu.VMEM((clusters, 2 * rhs, cl), F32)
 
     group = 4
@@ -531,10 +568,10 @@
         [own, kept, whole, ((clusters, FEATURES, cl), BF16), ((rhs, LANES), F32)],
         [pieces(1), sources(1), total],
         "svv>ppvpv",
-        pairs, payload, partner,
+        pairs, payload, beside,
         us=8.0,
     )
-    swap = swapped(near_pair, far_pair, tail)
+    swap = swapped(other, far_pair, tail)
     blocks_other, near = call(
         functools.partial(near_kernel, cl, 1, 2),
         [kept, whole],
@@ -547,24 +584,24 @@
     window = pltpu.VMEM((tiles, 2 * rhs, LANES), BF16)
     gathered = pltpu.VMEM((clusters, 2 * rhs, partners * rank), BF16)
     fields = pltpu.VMEM((clusters, 2 * rhs, 2 * rank), BF16)
-    image, payload, heavy, coupling = call(
+    image, payload, table, coupling = call(
         functools.partial(image_kernel, cl, rank),
-        [whole, ((rhs, panels + span + LANES), F32), whole, ((clusters, 2 * rank, partners * rank), BF16)],
+        [whole, whole, ((rhs, span + LANES), F32), ((clusters, 2 * rank, partners * rank), BF16)],
         [window, pltpu.VMEM((tiles, 8, LANES), F32), gathered, fields],
         "svvvvvvppp>vvvp",
-        at, near_pair, far_pair, swap, centers, area, near, basis, krylov, offsets,
+        at, other, far_pair, swap, centers, area, near, basis, krylov, offsets,
         us=4.5,
     )
-    partner, other, near_pair, far_pair = exchange(payload, heavy)
+    beside, other, far_pair, partner = exchange(payload, table, outward_around)
     near, tail = call(
         functools.partial(near_again_kernel, cl, 0, 1),
         [whole, ((rhs, LANES), F32)],
         [pieces(1), total],
         "svvpp>vv",
-        pairs, payload, partner, own_blocks, blocks,
+        pairs, payload, beside, own_blocks, blocks,
         us=8.0,
     )
-    swap = swapped(near_pair, far_pair, tail)
+    swap = swapped(other, far_pair, tail)
     (near,) = call(
         functools.partial(near_again_kernel, cl, 1, 2),
         [whole],
@@ -574,19 +611,21 @@
         us=2.0,
     )
     sums_shape = ((rhs, LANES), F32)
-    (one,) = call(window_sums_kernel, [sums_shape], [], "vvvvv>v", payload, partner, near_pair, far_pair, swap, us=0.3)
-    size = 8
-    many = outward(one, size)
-    while 2 * size < devices:
-        (one,) = call(merge_kernel, [sums_shape], [], "vv>v", one, many, us=0.3)
-        size = 2 * size
-        many = outward(one, size)
+    if completion:
+        one, many = call(known_sums_kernel, [sums_shape] * 2, [], "pvvvvv>vv", weights, table, beside, other, far_pair, swap, us=0.3)
+        many = move(many, completion[0])
+    else:
+        one, many, size = table, beside, 2
+        while size < devices:
+            (one,) = call(merge_kernel, [sums_shape], [], "vv>v", one, many, us=0.3)
+            many = move(one, [(i, (i + size) % devices) for i in range(devices)])
+            size = 2 * size
     (again,) = call(
         functools.partial(far_again_kernel, cl, rank),
         [whole],
         [window, gathered, fields],
         "svvvvvpp>v",
-        at, near_pair, far_pair, swap, near, area, coupling, basis,
+        at, other, far_pair, swap, near, area, coupling, basis,
         us=2.0,
     )
     here = pltpu.VMEM((rhs, panels), F32)

time: 47.7 us -> 51.5 us (1.080)
  starting transfers between devices: 12.1 us -> 27.8 us
  waiting for transfers between devices: 14.4 us -> 1.62 us
    ppermute x11, starting transfers between devices: 12.1 us -> 27.8 us  [move(): return lax.ppermute(value, 'clus', pairs)]
    ppermute x11, waiting for transfers between devices: 14.4 us -> 1.62 us  [move(): return lax.ppermute(value, 'clus', pairs)]
  transfers between devices with their start and end apart: 11 -> 11, of which waited for: 5 -> 2; matrix products, arithmetic and copies ran while one was open for 0% -> 0% of each run, Pallas kernels for 27% -> 25%
where the time goes in v3:
time: 51.5 us; the launch traced here: 51.2 us
  starting transfers between devices  27.8 us (54%)
  Pallas kernels  20.9 us (41%)
  waiting for transfers between devices  1.62 us (3%)
  between operations  0.8 us (2%)
    ppermute x11, starting transfers between devices, move(): return lax.ppermute(value, 'clus', pairs)  27.8 us
    pallas_call x9, Pallas kernels, call(): pl.pallas_call(kernel, out_shape=[pltpu.VMEM(*out) if m == 'p' else jax.S...  20.9 us
    ppermute x11, waiting for transfers between devices, move(): return lax.ppermute(value, 'clus', pairs)  1.62 us
  transfers between devices with their start and end apart: 11, of which 2 were waited for; matrix products, arithmetic and copies ran while one was open for 0% of the time, Pallas kernels for 25%

profile of v3, /device:TPU:0, one launch (start us, length us, event | category | flops | bytes accessed | tf_op | source)
XLA Modules:
  0.0 51.2 jit_solution(7194809785932471453)
XLA Ops:
  0.6 1.8 %shard_map.95 = (f32[16,4864]{1,0:T(8,128)S(1)}, f32[16,768]{1,0:T(8,128)S(1)}, f32[16,256]{1,0:T(8,128)S(1)}, f32[16,384]{1,0:T(8,128)S(1)}, s32[16,32]{1,0:T(8...) custom-call(s32[1]{0:T(128)} %bitcast.position_ref, ...), custom_call_target="tpu_custom_call" | custom-call | flops 750000000 | bytes 5400000 | tf_op jit(solution)/shard_map/pallas_call | solution.py:484
  2.5 0.5 %collective-permute-start = (f32[16,768]{1,0:T(8,128)S(1)}, f32[16,768]{1,0:T(8,128)S(1)}, u32[]{:S(2)}, u32[]{:S(2)}) collective-permute-start(f32[16,768]{1,0:T(8,128)S(1)} %get-tuple-element.30), channel_id=1, source_target_pairs={{0,1},{1,0},{2,3},{3,2},{4,5},{5,4},{6,7},{7,6},{8,9},{9,8},{10,11... | collective-permute-start | bytes 147464 | tf_op jit(solution)/shard_map/ppermute | solution.py:520
  3.0 0.1 collective-permute-start.4
  3.0 0.8 %collective-permute-done.refs_1_ = f32[16,768]{1,0:T(8,128)S(1)} collective-permute-done((f32[16,768]{1,0:T(8,128)S(1)}, f32[16,768]{1,0:T(8,128)S(1)}, u32[]{:S(2)}, u32[]{:S(2)}) %collective-permute-start) | collective-permute-done | bytes 49184 | tf_op jit(solution)/shard_map/ppermute | solution.py:520
  3.9 0.7 %collective-permute-start.1 = (f32[16,6400]{1,0:T(8,128)S(1)}, f32[16,6400]{1,0:T(8,128)S(1)}, u32[]{:S(2)}, u32[]{:S(2)}) collective-permute-start(f32[16,6400]{1,0:T(8,128)S(1)} %pad_maximum_fusion), channel_id=1, source_target_pairs={{1,2},{2,1},{3,4},{4,3},{5,6},{6,5},{7,8},{8,7},{9,10},{10,9},{11,... | collective-permute-start | bytes 1228808 | tf_op jit(solution)/shard_map/ppermute | solution.py:520
  4.6 5.4 %collective-permute-start.2 = (f32[16,1536]{1,0:T(8,128)S(1)}, f32[16,1536]{1,0:T(8,128)S(1)}, u32[]{:S(2)}, u32[]{:S(2)}) collective-permute-start(f32[16,1536]{1,0:T(8,128)S(1)} %pad_maximum_fusion.4), channel_id=1, source_target_pairs={{0,4},{2,6},{4,8},{5,1},{6,10},{7,3},{8,12},{9,5},{10,14},{11,7},{... | collective-permute-start | bytes 294920 | tf_op jit(solution)/shard_map/ppermute | solution.py:520
  10.0 3.9 %shard_map.96 = (bf16[16,512,256]{2,1,0:T(8,128)(2,1)S(1)}, bf16[12,4,512,256]{3,2,1,0:T(8,128)(2,1)S(1)}, f32[16,4096]{1,0:T(8,128)S(1)}, bf16[16,80,256]{2,1,0:T(8,128)(2,1)S(1)}, f32[16,128]{1,0:T(8,128)S(1)}) custom-call(s32[8,128]{1,0:T(8,128)S(1)} %get-tuple-element.31.pairs_ref, f32[16,4864]{1,0:T(8,128)S(1)} %get-tuple-element.29.refs_0_, ...), custom_call_target="tpu_custom_call" | custom-call | flops 4000000000 | bytes 28800000 | tf_op jit(solution)/shard_map/pallas_call | solution.py:484
  13.8 0.0 collective-permute-done.1.refs_1_.other_ref
  13.9 0.0 collective-permute-done.2.far_pair_ref
  13.9 5.3 %collective-permute-start.3 = (f32[16,3200]{1,0:T(8,128)S(1)}, f32[16,3200]{1,0:T(8,128)S(1)}, u32[]{:S(2)}, u32[]{:S(2)}) collective-permute-start(f32[16,3200]{1,0:T(8,128)S(1)} %pad_maximum_fusion.2), channel_id=1, source_target_pairs={{0,1},{1,0},{2,3},{3,2},{4,5},{5,4},{6,7},{7,6},{8,9},{9,8},{10,11... | collective-permute-start | bytes 614408 | tf_op jit(solution)/shard_map/ppermute | solution.py:520
  19.2 0.0 collective-permute-done.4.refs_0_
  19.2 2.9 %shard_map.97 = (bf16[12,4,512,256]{3,2,1,0:T(8,128)(2,1)S(1)}, f32[16,4096]{1,0:T(8,128)S(1)}) custom-call(s32[8,128]{1,0:T(8,128)S(1)} %get-tuple-element.31.pairs_ref, f32[16,4864]{1,0:T(8,128)S(1)} %collective-permute-done.4.refs_0_, f32[16,6400]{1,0:T(8,128)S(1)} %collective-permute-done.1.refs_1_.other_ref, ...), custom_call_target="tpu_custom_call" | custom-call | flops 2000000000 | bytes 14400000 | tf_op jit(solution)/shard_map/pallas_call | solution.py:484
  22.1 0.0 collective-permute-done.3.swapped_ref
  22.1 4.3 %shard_map.98 = (f32[16,4096]{1,0:T(8,128)S(1)}, f32[16,4096]{1,0:T(8,128)S(1)}, f32[16,640]{1,0:T(8,128)S(1)}, bf16[16,64,1024]{2,1,0:T(8,128)(2,1)S(1)}) custom-call(s32[16,32]{1,0:T(8,128)S(1)} %get-tuple-element.28.at_ref, f32[16,6400]{1,0:T(8,128)S(1)} %collective-permute-done.1.refs_1_.other_ref, f32[16,1536]{1,0:T(8,128)S(1)} %collective-permute-done.2.far_pair_ref, ...), custom_call_target="tpu_custom_call" | custom-call | flops 2249999872 | bytes 16200000 | tf_op jit(solution)/shard_map/pallas_call | solution.py:484
  26.4 0.7 %collective-permute-start.5 = (f32[16,640]{1,0:T(8,128)S(1)}, f32[16,640]{1,0:T(8,128)S(1)}, u32[]{:S(2)}, u32[]{:S(2)}) collective-permute-start(f32[16,640]{1,0:T(8,128)S(1)} %get-tuple-element.41.own_ref), channel_id=1, source_target_pairs={{0,1},{1,0},{2,3},{3,2},{4,5},{5,4},{6,7},{7,6},{8,9},{9,8},{10,11... | collective-permute-start | bytes 122888 | tf_op jit(solution)/shard_map/ppermute | solution.py:520
  27.1 0.1 collective-permute-start.10
  27.1 0.8 %collective-permute-done.5.refs_1_.partner_ref = f32[16,640]{1,0:T(8,128)S(1)} collective-permute-done((f32[16,640]{1,0:T(8,128)S(1)}, f32[16,640]{1,0:T(8,128)S(1)}, u32[]{:S(2)}, u32[]{:S(2)}) %collective-permute-start.5) | collective-permute-done | bytes 40992 | tf_op jit(solution)/shard_map/ppermute | solution.py:520
  27.9 2.5 %collective-permute-start.7 = (f32[16,1280]{1,0:T(8,128)S(1)}, f32[16,1280]{1,0:T(8,128)S(1)}, u32[]{:S(2)}, u32[]{:S(2)}) collective-permute-start(f32[16,1280]{1,0:T(8,128)S(1)} %pad_maximum_fusion.5), channel_id=1, source_target_pairs={{0,4},{2,6},{4,8},{5,1},{6,10},{7,3},{8,12},{9,5},{10,14},{11,7},{... | collective-permute-start | bytes 245768 | tf_op jit(solution)/shard_map/ppermute | solution.py:520
  30.4 0.7 %collective-permute-start.6 = (f32[16,5376]{1,0:T(8,128)S(1)}, f32[16,5376]{1,0:T(8,128)S(1)}, u32[]{:S(2)}, u32[]{:S(2)}) collective-permute-start(f32[16,5376]{1,0:T(8,128)S(1)} %pad_maximum_fusion.1), channel_id=1, source_target_pairs={{1,2},{2,1},{3,4},{4,3},{5,6},{6,5},{7,8},{8,7},{9,10},{10,9},{11,... | collective-permute-start | bytes 1032200 | tf_op jit(solution)/shard_map/ppermute | solution.py:520
  31.1 2.3 %shard_map.99 = (f32[16,4096]{1,0:T(8,128)S(1)}, f32[16,128]{1,0:T(8,128)S(1)}) custom-call(s32[8,128]{1,0:T(8,128)S(1)} %get-tuple-element.31.pairs_ref, f32[16,4096]{1,0:T(8,128)S(1)} %get-tuple-element.42.refs_0_, f32[16,640]{1,0:T(8,128)S(1)} %collective-permute-done.5.refs_1_.partner_ref, bf16[16,512,256]{2,1,0:T(8,128)(2,1)S(1)} %get-tuple-element.43.refs_2_, ...), custom_call_target="tpu_custom_call" | custom-call | flops 4000000000 | bytes 28800000 | tf_op jit(solution)/shard_map/pallas_call | solution.py:484
  33.5 0.0 collective-permute-done.6.other_ref.refs_1_
  33.5 0.0 collective-permute-done.7.far_ref.far_pair_ref
  33.5 9.0 %collective-permute-start.8 = (f32[16,2688]{1,0:T(8,128)S(1)}, f32[16,2688]{1,0:T(8,128)S(1)}, u32[]{:S(2)}, u32[]{:S(2)}) collective-permute-start(f32[16,2688]{1,0:T(8,128)S(1)} %pad_maximum_fusion.3), channel_id=1, source_target_pairs={{0,1},{1,0},{2,3},{3,2},{4,5},{5,4},{6,7},{7,6},{8,9},{9,8},{10,11... | collective-permute-start | bytes 516104 | tf_op jit(solution)/shard_map/ppermute | solution.py:520
  42.5 0.0 collective-permute-done.10.refs_0_
  42.5 1.6 %shard_map.101.near_ref = f32[16,4096]{1,0:T(8,128)S(1)} custom-call(s32[8,128]{1,0:T(8,128)S(1)} %get-tuple-element.31.pairs_ref, f32[16,4096]{1,0:T(8,128)S(1)} %collective-permute-done.10.refs_0_, f32[16,5376]{1,0:T(8,128)S(1)} %collective-permute-done.6.other_ref.refs_1_, f32[16,4096]{1,0:T(8,128)S(1)} %get-tuple-element.49.refs_2_, ...), custom_call_target="tpu_custom_call" | custom-call | flops 1000000000 | bytes 7200000 | tf_op jit(solution)/shard_map/pallas_call | solution.py:484
  44.1 0.0 collective-permute-done.8.swapped_ref
  44.2 0.7 %shard_map.100 = (f32[16,128]{1,0:T(8,128)S(1)}, f32[16,128]{1,0:T(8,128)S(1)}) custom-call(f32[8,128]{1,0:T(8,128)S(1)} %get-tuple-element.27.weights_ref, f32[16,640]{1,0:T(8,128)S(1)} %get-tuple-element.41.own_ref, f32[16,640]{1,0:T(8,128)S(1)} %collective-permute-done.5.refs_1_.partner_ref, f32[16,5376]{1,0:T(8,128)S(1)} %collective-permute-done.6.other_ref.refs_1_, ...), custom_call_target="tpu_custom_call" | custom-call | flops 150000000 | bytes 1080000 | tf_op jit(solution)/shard_map/pallas_call | solution.py:484
  44.9 3.0 %collective-permute-start.9 = (f32[16,128]{1,0:T(8,128)S(1)}, f32[16,128]{1,0:T(8,128)S(1)}, u32[]{:S(2)}, u32[]{:S(2)}) collective-permute-start(f32[16,128]{1,0:T(8,128)S(1)} %get-tuple-element.47), channel_id=1, source_target_pairs={{0,11},{1,10},{2,9},{3,8},{4,15},{5,14},{6,13},{7,12},{8,3},{9,2},... | collective-permute-start | bytes 24584 | tf_op jit(solution)/shard_map/ppermute | solution.py:520
  47.9 2.1 %shard_map.102.again_ref = f32[16,4096]{1,0:T(8,128)S(1)} custom-call(s32[16,32]{1,0:T(8,128)S(1)} %get-tuple-element.28.at_ref, f32[16,5376]{1,0:T(8,128)S(1)} %collective-permute-done.6.other_ref.refs_1_, f32[16,1280]{1,0:T(8,128)S(1)} %collective-permute-done.7.far_ref.far_pair_ref, f32[16,2688]{1,0:T(8,128)S(1)} %collective-permute-done.8.swapped_ref, ...), custom_call_target="tpu_custom_call" | custom-call | flops 1000000000 | bytes 7200000 | tf_op jit(solution)/shard_map/pallas_call | solution.py:484
  50.0 0.0 collective-permute-done.9.two_ref
  50.0 1.2 %shard_map.103 = (f32[16,4096]{1,0:T(8,128)}, f32[16,4096]{1,0:T(8,128)}) custom-call(f32[16,128]{1,0:T(8,128)S(1)} %get-tuple-element.46.one_ref, f32[16,128]{1,0:T(8,128)S(1)} %collective-permute-done.9.two_ref, f32[16,4096]{1,0:T(8,128)S(1)} %get-tuple-element.48.image_ref, f32[16,4096]{1,0:T(8,128)S(1)} %shard_map.102.again_ref, ...), custom_call_target="tpu_custom_call" | custom-call | flops 500000000 | bytes 3600000 | tf_op jit(solution)/shard_map/pallas_call | solution.py:484
  (8 shorter events, 0.1 us)
Async XLA Ops:
  2.5 1.4 %collective-permute-start = (f32[16,768]{1,0:T(8,128)S(1)}, f32[16,768]{1,0:T(8,128)S(1)}, u32[]{:S(2)}, u32[]{:S(2)}) collective-permute-start(f32[16,768]{1,0:T(8,128)S(1)} %get-tuple-element.30), channel_id=1, source_target_pairs={{0,1},{1,0},{2,3},{3,2},{4,5},{5,4},{6,7},{7,6},{8,9},{9,8},{10,11... | collective-permute-start | bytes 147464 | tf_op jit(solution)/shard_map/ppermute | solution.py:520
  3.0 16.2 %collective-permute-start.4 = (f32[16,4864]{1,0:T(8,128)S(1)}, f32[16,4864]{1,0:T(8,128)S(1)}, u32[]{:S(2)}, u32[]{:S(2)}) collective-permute-start(f32[16,4864]{1,0:T(8,128)S(1)} %get-tuple-element.29.refs_0_), channel_id=1, source_target_pairs={{0,1},{1,0},{2,3},{3,2},{4,5},{5,4},{6,7},{7,6},{8,9},{9,8},{10,11... | collective-permute-start | bytes 933896 | tf_op jit(solution)/shard_map/ppermute | solution.py:520
  3.9 10.0 %collective-permute-start.1 = (f32[16,6400]{1,0:T(8,128)S(1)}, f32[16,6400]{1,0:T(8,128)S(1)}, u32[]{:S(2)}, u32[]{:S(2)}) collective-permute-start(f32[16,6400]{1,0:T(8,128)S(1)} %pad_maximum_fusion), channel_id=1, source_target_pairs={{1,2},{2,1},{3,4},{4,3},{5,6},{6,5},{7,8},{8,7},{9,10},{10,9},{11,... | collective-permute-start | bytes 1228808 | tf_op jit(solution)/shard_map/ppermute | solution.py:520
  4.6 9.3 %collective-permute-start.2 = (f32[16,1536]{1,0:T(8,128)S(1)}, f32[16,1536]{1,0:T(8,128)S(1)}, u32[]{:S(2)}, u32[]{:S(2)}) collective-permute-start(f32[16,1536]{1,0:T(8,128)S(1)} %pad_maximum_fusion.4), channel_id=1, source_target_pairs={{0,4},{2,6},{4,8},{5,1},{6,10},{7,3},{8,12},{9,5},{10,14},{11,7},{... | collective-permute-start | bytes 294920 | tf_op jit(solution)/shard_map/ppermute | solution.py:520
  13.9 8.2 %collective-permute-start.3 = (f32[16,3200]{1,0:T(8,128)S(1)}, f32[16,3200]{1,0:T(8,128)S(1)}, u32[]{:S(2)}, u32[]{:S(2)}) collective-permute-start(f32[16,3200]{1,0:T(8,128)S(1)} %pad_maximum_fusion.2), channel_id=1, source_target_pairs={{0,1},{1,0},{2,3},{3,2},{4,5},{5,4},{6,7},{7,6},{8,9},{9,8},{10,11... | collective-permute-start | bytes 614408 | tf_op jit(solution)/shard_map/ppermute | solution.py:520
  26.4 1.6 %collective-permute-start.5 = (f32[16,640]{1,0:T(8,128)S(1)}, f32[16,640]{1,0:T(8,128)S(1)}, u32[]{:S(2)}, u32[]{:S(2)}) collective-permute-start(f32[16,640]{1,0:T(8,128)S(1)} %get-tuple-element.41.own_ref), channel_id=1, source_target_pairs={{0,1},{1,0},{2,3},{3,2},{4,5},{5,4},{6,7},{7,6},{8,9},{9,8},{10,11... | collective-permute-start | bytes 122888 | tf_op jit(solution)/shard_map/ppermute | solution.py:520
  27.1 15.5 %collective-permute-start.10 = (f32[16,4096]{1,0:T(8,128)S(1)}, f32[16,4096]{1,0:T(8,128)S(1)}, u32[]{:S(2)}, u32[]{:S(2)}) collective-permute-start(f32[16,4096]{1,0:T(8,128)S(1)} %get-tuple-element.42.refs_0_), channel_id=1, source_target_pairs={{0,1},{1,0},{2,3},{3,2},{4,5},{5,4},{6,7},{7,6},{8,9},{9,8},{10,11... | collective-permute-start | bytes 786440 | tf_op jit(solution)/shard_map/ppermute | solution.py:520
  27.9 5.6 %collective-permute-start.7 = (f32[16,1280]{1,0:T(8,128)S(1)}, f32[16,1280]{1,0:T(8,128)S(1)}, u32[]{:S(2)}, u32[]{:S(2)}) collective-permute-start(f32[16,1280]{1,0:T(8,128)S(1)} %pad_maximum_fusion.5), channel_id=1, source_target_pairs={{0,4},{2,6},{4,8},{5,1},{6,10},{7,3},{8,12},{9,5},{10,14},{11,7},{... | collective-permute-start | bytes 245768 | tf_op jit(solution)/shard_map/ppermute | solution.py:520
  30.4 3.0 %collective-permute-start.6 = (f32[16,5376]{1,0:T(8,128)S(1)}, f32[16,5376]{1,0:T(8,128)S(1)}, u32[]{:S(2)}, u32[]{:S(2)}) collective-permute-start(f32[16,5376]{1,0:T(8,128)S(1)} %pad_maximum_fusion.1), channel_id=1, source_target_pairs={{1,2},{2,1},{3,4},{4,3},{5,6},{6,5},{7,8},{8,7},{9,10},{10,9},{11,... | collective-permute-start | bytes 1032200 | tf_op jit(solution)/shard_map/ppermute | solution.py:520
  33.5 10.6 %collective-permute-start.8 = (f32[16,2688]{1,0:T(8,128)S(1)}, f32[16,2688]{1,0:T(8,128)S(1)}, u32[]{:S(2)}, u32[]{:S(2)}) collective-permute-start(f32[16,2688]{1,0:T(8,128)S(1)} %pad_maximum_fusion.3), channel_id=1, source_target_pairs={{0,1},{1,0},{2,3},{3,2},{4,5},{5,4},{6,7},{7,6},{8,9},{9,8},{10,11... | collective-permute-start | bytes 516104 | tf_op jit(solution)/shard_map/ppermute | solution.py:520
  44.9 5.1 %collective-permute-start.9 = (f32[16,128]{1,0:T(8,128)S(1)}, f32[16,128]{1,0:T(8,128)S(1)}, u32[]{:S(2)}, u32[]{:S(2)}) collective-permute-start(f32[16,128]{1,0:T(8,128)S(1)} %get-tuple-element.47), channel_id=1, source_target_pairs={{0,11},{1,10},{2,9},{3,8},{4,15},{5,14},{6,13},{7,12},{8,3},{9,2},... | collective-permute-start | bytes 24584 | tf_op jit(solution)/shard_map/ppermute | solution.py:520

commit v4 on v2

--- a/solution.py
+++ b/solution.py
@@ -72,8 +72,8 @@
 
 def pair_list(near, position, clusters):
     block = lax.div(near, clusters) - position
-    partner = block * (1 - 2 * lax.rem(position, 2)) > 0
-    place = (lax.rem(near, clusters) + jnp.where((block != 0) & ~partner, clusters, 0)).astype(F32)
+    side = block * (1 - 2 * lax.rem(position, 2))
+    place = lax.rem(near, clusters).astype(F32)
     across = lax.broadcasted_iota(jnp.int32, (clusters, clusters), 1)
     down = lax.broadcasted_iota(jnp.int32, (clusters, clusters), 0)
     upright = lambda value: jnp.sum(jnp.where(across == down, value, 0.0), axis=1, keepdims=True)
@@ -81,9 +81,8 @@
     target = lax.broadcasted_iota(jnp.int32, (clusters, 1), 0).astype(F32)
     rows = lax.broadcasted_iota(jnp.int32, (8, LANES), 0)
     out = jnp.zeros((8, LANES), F32)
-    for which in range(2):
-        here = block != 0 if which else block == 0
-        live = jnp.where(here & (near >= 0), 1.0, 0.0)
+    for which in range(3):
+        live = jnp.where((side == (0, 1, -1)[which]) & (near >= 0), 1.0, 0.0)
         counts = sum(live[k:k + 1] for k in range(1, near.shape[0]))
         first = jnp.sum(jnp.where(across < down, counts, 0.0), axis=1, keepdims=True)
         found = jnp.zeros((clusters, LANES), F32)
@@ -93,8 +92,8 @@
             found = found + hit * (target * 64 + upright(place[k:k + 1]))
             first = first + alive
         count = jnp.sum(counts, axis=1, keepdims=True)
-        found = jnp.where(row[0:1] < count, jnp.sum(found, axis=0, keepdims=True), (1.0 + which) * clusters)
-        out = jnp.where(rows == which, found, jnp.where(rows == 2 + which, count, out))
+        found = jnp.where(row[0:1] < count, jnp.sum(found, axis=0, keepdims=True), 1.0 * clusters)
+        out = jnp.where(rows == which, found, jnp.where(rows == 3 + which, count, out))
     return out.astype(jnp.int32)
 
 
@@ -195,12 +194,11 @@
     return jnp.concatenate([first, *combos, last], axis=0)
 
 
-def fill_features(sources_ref, blocks, panels, cl):
+def fill_features(sources_ref, payload_ref, panels, cl):
     clusters = panels // cl
-    for b, ref in enumerate(blocks):
-        for c in range(clusters):
-            sources_ref[b * clusters + c] = features_of(ref, panels, c, cl, False).astype(BF16)
-    sources_ref[len(blocks) * clusters] = sources_ref[0]
+    for c in range(clusters):
+        sources_ref[c] = features_of(payload_ref, panels, c, cl, False).astype(BF16)
+    sources_ref[clusters] = sources_ref[0]
 
 
 def near_block(source, target, pieces, out_ref):
@@ -219,11 +217,10 @@
     return dot_nn(pieces, block_ref[0:cl, :]) + dot_nn(pieces, block_ref[cl:2 * cl, :])
 
 
-def fill_charges(pieces_ref, blocks, clusters, cl):
-    for b, ref in enumerate(blocks):
-        for c in range(clusters):
-            pieces_ref[b * clusters + c] = stacked(ref[:, c * cl:(c + 1) * cl])
-    pieces_ref[len(blocks) * clusters] = jnp.zeros_like(pieces_ref[0])
+def fill_charges(pieces_ref, payload_ref, clusters, cl):
+    for c in range(clusters):
+        pieces_ref[c] = stacked(payload_ref[:, c * cl:(c + 1) * cl])
+    pieces_ref[clusters] = jnp.zeros_like(pieces_ref[0])
 
 
 def pair_at(pairs_ref, which, i):
@@ -231,25 +228,25 @@
     return lax.shift_right_logical(pair, 6), lax.bitwise_and(pair, 63)
 
 
-def near_kernel(cl, which, number, pairs_ref, *refs):
-    blocks = refs[:number]
+def near_kernel(cl, which, pairs_ref, payload_ref, table_ref, *refs):
     if which:
-        targets_ref, start_ref, kept_ref, near_out_ref, pieces_ref, sources_ref, total_ref = refs[number:]
+        targets_ref, start_ref, kept_ref, near_out_ref, tail_ref, pieces_ref, sources_ref, total_ref = refs
     else:
-        _, own_ref, kept_ref, near_out_ref, targets_ref, tail_ref, pieces_ref, sources_ref, total_ref = refs[number:]
-        tail_ref[...] = blocks[0][:, blocks[0].shape[1] - tail_ref.shape[1]:]
+        own_ref, kept_ref, near_out_ref, targets_ref, tail_ref, pieces_ref, sources_ref, total_ref = refs
+    tail_ref[...] = table_ref[:, table_ref.shape[1] - tail_ref.shape[1]:]
     panels = near_out_ref.shape[1]
     clusters = panels // cl
     group = kept_ref.shape[1]
-    fill_charges(pieces_ref, blocks, clusters, cl)
-    fill_features(sources_ref, blocks, panels, cl)
+    fill_charges(pieces_ref, payload_ref, clusters, cl)
+    fill_features(sources_ref, payload_ref, panels, cl)
     if which:
         total_ref[...] = jnp.zeros_like(total_ref)
     else:
         for c in range(clusters):
-            target = features_of(blocks[0], panels, c, cl, True).astype(BF16)
+            target = features_of(payload_ref, panels, c, cl, True).astype(BF16)
             targets_ref[c] = target
             total_ref[c] = near_block(sources_ref[c], target, pieces_ref[c], own_ref.at[c])
+
     def step(m, _):
         pairs = [pair_at(pairs_ref, which, group * m + w) for w in range(group)]
         loaded = [(sources_ref[j], targets_ref[c], pieces_ref[j]) for c, j in pairs]
@@ -258,23 +255,22 @@
             total_ref[c] += part
         return 0
 
-    lax.fori_loop(0, (pairs_ref[2 + which, 0] + group - 1) // group, step, 0)
+    lax.fori_loop(0, (pairs_ref[3 + which, 0] + group - 1) // group, step, 0)
     for c in range(clusters):
         lanes = slice(c * cl, (c + 1) * cl)
         near = folded(total_ref[c])
         near_out_ref[:, lanes] = start_ref[:, lanes] + near if which else near
 
 
-def near_again_kernel(cl, which, number, pairs_ref, *refs):
-    blocks = refs[:number]
+def near_again_kernel(cl, which, pairs_ref, payload_ref, table_ref, *refs):
     if which:
-        start_ref, kept_ref, near_out_ref, pieces_ref, total_ref = refs[number:]
+        start_ref, kept_ref, near_out_ref, tail_ref, pieces_ref, total_ref = refs
     else:
-        _, own_ref, kept_ref, near_out_ref, tail_ref, pieces_ref, total_ref = refs[number:]
-        tail_ref[...] = blocks[0][:, blocks[0].shape[1] - tail_ref.shape[1]:]
+        own_ref, kept_ref, near_out_ref, tail_ref, pieces_ref, total_ref = refs
+    tail_ref[...] = table_ref[:, table_ref.shape[1] - tail_ref.shape[1]:]
     clusters = near_out_ref.shape[1] // cl
     group = kept_ref.shape[1]
-    fill_charges(pieces_ref, blocks, clusters, cl)
+    fill_charges(pieces_ref, payload_ref, clusters, cl)
     if which:
         total_ref[...] = jnp.zeros_like(total_ref)
     else:
@@ -288,7 +284,7 @@
             total_ref[c] += part
         return 0
 
-    lax.fori_loop(0, (pairs_ref[2 + which, 0] + group - 1) // group, step, 0)
+    lax.fori_loop(0, (pairs_ref[3 + which, 0] + group - 1) // group, step, 0)
     for c in range(clusters):
         lanes = slice(c * cl, (c + 1) * cl)
         near = folded(total_ref[c])
@@ -483,11 +479,12 @@
     def outward(value, steps):
         return move(value, [(i, (i + steps * (1 - 2 * (i % 2))) % devices) for i in range(devices)])
 
-    def exchange(payload, heavy):
-        other = move(heavy, bridging)
-        partner = move(payload, pairing)
-        pair = jnp.concatenate([value[:, heavy.shape[1]:] for value in (payload, partner)], axis=1)
-        return partner, other, outward(pair, 2), outward(pair, 4)
+    def neighbours(payload, heavy):
+        return move(payload, pairing), move(heavy, bridging)
+
+    def pairs_away(tail, partner):
+        pair = jnp.concatenate([tail, partner[:, partner.shape[1] - tail.shape[1]:]], axis=1)
+        return outward(pair, 2), outward(pair, 4)
 
     def swapped(near_pair, far_pair, tail):
         return move(jnp.concatenate([near_pair, far_pair, tail], axis=1), pairing)
@@ -513,34 +510,38 @@
         position, vertices, panel_vertices, krylov, basis, far_pairs, near_pairs.T, offsets,
         us=1.5,
     )
-    partner, other, near_pair, far_pair = exchange(payload, heavy)
-    total = pltpu.VMEM((clusters, 2 * rhs, cl), F32)
-
+    partner, other = neighbours(payload, heavy)
     group = 4
     own = ((clusters, 2 * cl, cl), BF16)
     kept = ((clusters * (slots - 1) // group, group, 2 * cl, cl), BF16)
-
-    def pieces(number):
-        return pltpu.VMEM((number * clusters + 1, 2 * rhs, cl), BF16)
-
-    def sources(number):
-        return pltpu.VMEM((number * clusters + 1, FEATURES, cl), BF16)
-
+    sums_shape = ((rhs, LANES), F32)
+    total = pltpu.VMEM((clusters, 2 * rhs, cl), F32)
+    pieces = pltpu.VMEM((clusters + 1, 2 * rhs, cl), BF16)
+    sources = pltpu.VMEM((clusters + 1, FEATURES, cl), BF16)
     own_blocks, blocks, near, targets, tail = call(
-        functools.partial(near_kernel, cl, 0, 1),
-        [own, kept, whole, ((clusters, FEATURES, cl), BF16), ((rhs, LANES), F32)],
-        [pieces(1), sources(1), total],
+        functools.partial(near_kernel, cl, 0),
+        [own, kept, whole, ((clusters, FEATURES, cl), BF16), ((rhs, width), F32)],
+        [pieces, sources, total],
         "svv>ppvpv",
-        pairs, payload, partner,
+        pairs, payload, payload,
         us=8.0,
     )
+    near_pair, far_pair = pairs_away(tail, partner)
+    blocks_partner, near, tail = call(
+        functools.partial(near_kernel, cl, 1),
+        [kept, whole, sums_shape],
+        [pieces, sources, total],
+        "svvpv>pvv",
+        pairs, partner, payload, targets, near,
+        us=4.0,
+    )
     swap = swapped(near_pair, far_pair, tail)
-    blocks_other, near = call(
-        functools.partial(near_kernel, cl, 1, 2),
-        [kept, whole],
-        [pieces(2), sources(2), total],
-        "svvpv>pv",
-        pairs, partner, other, targets, near,
+    blocks_other, near, _ = call(
+        functools.partial(near_kernel, cl, 2),
+        [kept, whole, sums_shape],
+        [pieces, sources, total],
+        "svvpv>pvv",
+        pairs, other, payload, targets, near,
         us=4.0,
     )
     tiles = 6 * per * span // LANES
@@ -555,25 +556,33 @@
         at, near_pair, far_pair, swap, centers, area, near, basis, krylov, offsets,
         us=4.5,
     )
-    partner, other, near_pair, far_pair = exchange(payload, heavy)
+    partner, other = neighbours(payload, heavy)
     near, tail = call(
-        functools.partial(near_again_kernel, cl, 0, 1),
-        [whole, ((rhs, LANES), F32)],
-        [pieces(1), total],
+        functools.partial(near_again_kernel, cl, 0),
+        [whole, ((rhs, span + LANES), F32)],
+        [pieces, total],
         "svvpp>vv",
-        pairs, payload, partner, own_blocks, blocks,
+        pairs, payload, payload, own_blocks, blocks,
         us=8.0,
     )
+    near_pair, far_pair = pairs_away(tail, partner)
+    near, tail = call(
+        functools.partial(near_again_kernel, cl, 1),
+        [whole, sums_shape],
+        [pieces, total],
+        "svvvp>vv",
+        pairs, partner, payload, near, blocks_partner,
+        us=4.0,
+    )
     swap = swapped(near_pair, far_pair, tail)
-    (near,) = call(
-        functools.partial(near_again_kernel, cl, 1, 2),
-        [whole],
-        [pieces(2), total],
-        "svvvp>v",
-        pairs, partner, other, near, blocks_other,
-        us=2.0,
-    )
-    sums_shape = ((rhs, LANES), F32)
+    near, _ = call(
+        functools.partial(near_again_kernel, cl, 2),
+        [whole, sums_shape],
+        [pieces, total],
+        "svvvp>vv",
+        pairs, other, payload, near, blocks_other,
+        us=4.0,
+    )
     (one,) = call(window_sums_kernel, [sums_shape], [], "vvvvv>v", payload, partner, near_pair, far_pair, swap, us=0.3)
     size = 8
     many = outward(one, size)

time: 47.7 us -> 47.4 us (level)
  waiting for transfers between devices: 14.4 us -> 8.23 us
  starting transfers between devices: 12.1 us -> 17.7 us
    ppermute x11, waiting for transfers between devices: 14.4 us -> 8.23 us  [move(): return lax.ppermute(value, 'clus', pairs)]
    ppermute x11, starting transfers between devices: 12.1 us -> 17.7 us  [move(): return lax.ppermute(value, 'clus', pairs)]
    pallas_call x9 -> x11, Pallas kernels: 20.5 us -> 20.3 us  [call(): pl.pallas_call(kernel, out_shape=[pltpu.VMEM(*out) if m == 'p' else jax.S...]
  transfers between devices with their start and end apart: 11 -> 11, of which waited for: 5 -> 6; matrix products, arithmetic and copies ran while one was open for 0% -> 0% of each run, Pallas kernels for 27% -> 27%
where the time goes in v4:
time: 47.4 us; the launch traced here: 47.1 us
  Pallas kernels  20.3 us (43%)
  starting transfers between devices  17.7 us (37%)
  waiting for transfers between devices  8.23 us (17%)
  between operations  0.79 us (2%)
    pallas_call x11, Pallas kernels, call(): pl.pallas_call(kernel, out_shape=[pltpu.VMEM(*out) if m == 'p' else jax.S...  20.3 us
    ppermute x11, starting transfers between devices, move(): return lax.ppermute(value, 'clus', pairs)  17.7 us
    ppermute x11, waiting for transfers between devices, move(): return lax.ppermute(value, 'clus', pairs)  8.23 us
  transfers between devices with their start and end apart: 11, of which 6 were waited for; matrix products, arithmetic and copies ran while one was open for 0% of the time, Pallas kernels for 27%

profile of v4, /device:TPU:0, one launch (start us, length us, event | category | flops | bytes accessed | tf_op | source)
XLA Modules:
  0.0 47.1 jit_solution(15341207592064760430)
XLA Ops:
  0.6 1.8 %shard_map.86 = (f32[16,5632]{1,0:T(8,128)S(1)}, f32[16,4864]{1,0:T(8,128)S(1)}, f32[16,256]{1,0:T(8,128)S(1)}, f32[16,384]{1,0:T(8,128)S(1)}, s32[16,32]{1,0:T(...) custom-call(s32[1]{0:T(128)} %bitcast.position_ref, ...), custom_call_target="tpu_custom_call" | custom-call | flops 750000000 | bytes 5400000 | tf_op jit(solution)/shard_map/pallas_call | solution.py:447
  2.4 0.7 %collective-permute-start.4 = (f32[16,4864]{1,0:T(8,128)S(1)}, f32[16,4864]{1,0:T(8,128)S(1)}, u32[]{:S(2)}, u32[]{:S(2)}) collective-permute-start(f32[16,4864]{1,0:T(8,128)S(1)} %get-tuple-element.39), channel_id=1, source_target_pairs={{1,2},{2,1},{3,4},{4,3},{5,6},{6,5},{7,8},{8,7},{9,10},{10,9},{11,... | collective-permute-start | bytes 933896 | tf_op jit(solution)/shard_map/ppermute | solution.py:477
  3.1 4.4 %collective-permute-start = (f32[16,5632]{1,0:T(8,128)S(1)}, f32[16,5632]{1,0:T(8,128)S(1)}, u32[]{:S(2)}, u32[]{:S(2)}) collective-permute-start(f32[16,5632]{1,0:T(8,128)S(1)} %get-tuple-element.32.payload_ref.table_ref), channel_id=1, source_target_pairs={{0,1},{1,0},{2,3},{3,2},{4,5},{5,4},{6,7},{7,6},{8,9},{9,8},{10,11... | collective-permute-start | bytes 1081352 | tf_op jit(solution)/shard_map/ppermute | solution.py:477
  7.5 2.7 %shard_map.87 = (bf16[16,512,256]{2,1,0:T(8,128)(2,1)S(1)}, bf16[12,4,512,256]{3,2,1,0:T(8,128)(2,1)S(1)}, f32[16,4096]{1,0:T(8,128)S(1)}, bf16[16,80,256]{2,1,0:T(8,128)(2,1)S(1)}, f32[16,768]{1,0:T(8,128)S(1)}) custom-call(s32[8,128]{1,0:T(8,128)S(1)} %get-tuple-element.31.pairs_ref, f32[16,5632]{1,0:T(8,128)S(1)} %get-tuple-element.32.payload_ref.table_ref, ...), custom_call_target="tpu_custom_call" | custom-call | flops 4000000000 | bytes 28800000 | tf_op jit(solution)/shard_map/pallas_call | solution.py:447
  10.2 0.0 collective-permute-done.payload_ref
  10.2 2.2 %collective-permute-start.2 = (f32[16,1536]{1,0:T(8,128)S(1)}, f32[16,1536]{1,0:T(8,128)S(1)}, u32[]{:S(2)}, u32[]{:S(2)}) collective-permute-start(f32[16,1536]{1,0:T(8,128)S(1)} %pad_maximum_fusion.2), channel_id=1, source_target_pairs={{0,4},{1,13},{2,6},{3,15},{4,8},{5,1},{6,10},{7,3},{8,12},{9,5},{1... | collective-permute-start | bytes 294920 | tf_op jit(solution)/shard_map/ppermute | solution.py:477
  12.5 0.9 %collective-permute-start.1 = (f32[16,1536]{1,0:T(8,128)S(1)}, f32[16,1536]{1,0:T(8,128)S(1)}, u32[]{:S(2)}, u32[]{:S(2)}) collective-permute-start(f32[16,1536]{1,0:T(8,128)S(1)} %pad_maximum_fusion.2), channel_id=1, source_target_pairs={{0,2},{1,15},{2,4},{3,1},{4,6},{5,3},{6,8},{7,5},{8,10},{9,7},{10,... | collective-permute-start | bytes 294920 | tf_op jit(solution)/shard_map/ppermute | solution.py:477
  13.4 2.1 %shard_map.88 = (bf16[12,4,512,256]{3,2,1,0:T(8,128)(2,1)S(1)}, f32[16,4096]{1,0:T(8,128)S(1)}, f32[16,128]{1,0:T(8,128)S(1)}) custom-call(s32[8,128]{1,0:T(8,128)S(1)} %get-tuple-element.31.pairs_ref, f32[16,5632]{1,0:T(8,128)S(1)} %collective-permute-done.payload_ref, f32[16,5632]{1,0:T(8,128)S(1)} %get-tuple-element.32.payload_ref.table_ref, ...), custom_call_target="tpu_custom_call" | custom-call | flops 2000000000 | bytes 14400000 | tf_op jit(solution)/shard_map/pallas_call | solution.py:447
  15.5 2.3 %collective-permute-done.2.far_pair_ref = f32[16,1536]{1,0:T(8,128)S(1)} collective-permute-done((f32[16,1536]{1,0:T(8,128)S(1)}, f32[16,1536]{1,0:T(8,128)S(1)}, u32[]{:S(2)}, u32[]{:S(2)}) %collective-permute-start.2) | collective-permute-done | bytes 98336 | tf_op jit(solution)/shard_map/ppermute | solution.py:477
  17.8 2.0 %collective-permute-done.1.near_pair_ref = f32[16,1536]{1,0:T(8,128)S(1)} collective-permute-done((f32[16,1536]{1,0:T(8,128)S(1)}, f32[16,1536]{1,0:T(8,128)S(1)}, u32[]{:S(2)}, u32[]{:S(2)}) %collective-permute-start.1) | collective-permute-done | bytes 98336 | tf_op jit(solution)/shard_map/ppermute | solution.py:477
  19.8 0.1 collective-permute-start.3
  19.9 0.0 collective-permute-done.4.payload_ref
  19.9 1.5 %shard_map.89 = (bf16[12,4,512,256]{3,2,1,0:T(8,128)(2,1)S(1)}, f32[16,4096]{1,0:T(8,128)S(1)}, f32[16,128]{1,0:T(8,128)}) custom-call(s32[8,128]{1,0:T(8,128)S(1)} %get-tuple-element.31.pairs_ref, f32[16,4864]{1,0:T(8,128)S(1)} %collective-permute-done.4.payload_ref, f32[16,5632]{1,0:T(8,128)S(1)} %get-tuple-element.32.payload_ref.table_ref, ...), custom_call_target="tpu_custom_call" | custom-call | flops 2000000000 | bytes 14400000 | tf_op jit(solution)/shard_map/pallas_call | solution.py:447
  21.4 0.0 collective-permute-done.3.swapped_ref
  21.4 4.3 %shard_map.90 = (f32[16,4096]{1,0:T(8,128)S(1)}, f32[16,4736]{1,0:T(8,128)S(1)}, f32[16,4096]{1,0:T(8,128)S(1)}, bf16[16,64,1024]{2,1,0:T(8,128)(2,1)S(1)}) custom-call(s32[16,32]{1,0:T(8,128)S(1)} %get-tuple-element.30.at_ref, f32[16,1536]{1,0:T(8,128)S(1)} %collective-permute-done.1.near_pair_ref, f32[16,1536]{1,0:T(8,128)S(1)} %collective-permute-done.2.far_pair_ref, ...), custom_call_target="tpu_custom_call" | custom-call | flops 2249999872 | bytes 16200000 | tf_op jit(solution)/shard_map/pallas_call | solution.py:447
  25.6 0.7 %collective-permute-start.10 = (f32[16,4096]{1,0:T(8,128)S(1)}, f32[16,4096]{1,0:T(8,128)S(1)}, u32[]{:S(2)}, u32[]{:S(2)}) collective-permute-start(f32[16,4096]{1,0:T(8,128)S(1)} %get-tuple-element.53), channel_id=1, source_target_pairs={{1,2},{2,1},{3,4},{4,3},{5,6},{6,5},{7,8},{8,7},{9,10},{10,9},{11,... | collective-permute-start | bytes 786440 | tf_op jit(solution)/shard_map/ppermute | solution.py:477
  26.3 2.4 %collective-permute-start.5 = (f32[16,4736]{1,0:T(8,128)S(1)}, f32[16,4736]{1,0:T(8,128)S(1)}, u32[]{:S(2)}, u32[]{:S(2)}) collective-permute-start(f32[16,4736]{1,0:T(8,128)S(1)} %get-tuple-element.45.payload_ref.table_ref), channel_id=1, source_target_pairs={{0,1},{1,0},{2,3},{3,2},{4,5},{5,4},{6,7},{7,6},{8,9},{9,8},{10,11... | collective-permute-start | bytes 909320 | tf_op jit(solution)/shard_map/ppermute | solution.py:477
  28.7 1.8 %shard_map.91 = (f32[16,4096]{1,0:T(8,128)S(1)}, f32[16,640]{1,0:T(8,128)S(1)}) custom-call(s32[8,128]{1,0:T(8,128)S(1)} %get-tuple-element.31.pairs_ref, f32[16,4736]{1,0:T(8,128)S(1)} %get-tuple-element.45.payload_ref.table_ref, f32[16,4736]{1,0:T(8,128)S(1)} %get-tuple-element.45.payload_ref.table_ref, ...), custom_call_target="tpu_custom_call" | custom-call | flops 4000000000 | bytes 28800000 | tf_op jit(solution)/shard_map/pallas_call | solution.py:447
  30.5 0.0 collective-permute-done.5.payload_ref.partner_ref
  30.5 1.8 %collective-permute-start.7 = (f32[16,1280]{1,0:T(8,128)S(1)}, f32[16,1280]{1,0:T(8,128)S(1)}, u32[]{:S(2)}, u32[]{:S(2)}) collective-permute-start(f32[16,1280]{1,0:T(8,128)S(1)} %pad_maximum_fusion.3), channel_id=1, source_target_pairs={{0,4},{1,13},{2,6},{3,15},{4,8},{5,1},{6,10},{7,3},{8,12},{9,5},{1... | collective-permute-start | bytes 245768 | tf_op jit(solution)/shard_map/ppermute | solution.py:477
  32.3 2.6 %collective-permute-start.6 = (f32[16,1280]{1,0:T(8,128)S(1)}, f32[16,1280]{1,0:T(8,128)S(1)}, u32[]{:S(2)}, u32[]{:S(2)}) collective-permute-start(f32[16,1280]{1,0:T(8,128)S(1)} %pad_maximum_fusion.3), channel_id=1, source_target_pairs={{0,2},{1,15},{2,4},{3,1},{4,6},{5,3},{6,8},{7,5},{8,10},{9,7},{10,... | collective-permute-start | bytes 245768 | tf_op jit(solution)/shard_map/ppermute | solution.py:477
  35.0 1.3 %shard_map.92 = (f32[16,4096]{1,0:T(8,128)S(1)}, f32[16,128]{1,0:T(8,128)S(1)}) custom-call(s32[8,128]{1,0:T(8,128)S(1)} %get-tuple-element.31.pairs_ref, f32[16,4736]{1,0:T(8,128)S(1)} %collective-permute-done.5.payload_ref.partner_ref, f32[16,4736]{1,0:T(8,128)S(1)} %get-tuple-element.45.payload_ref.table_ref, f32[16,4096]{1,0:T(8,128)S(1)} %get-tuple-element.49.refs_0_, ...), custom_call_target="tpu_custom_call" | custom-call | flops 2000000000 | bytes 14400000 | tf_op jit(solution)/shard_map/pallas_call | solution.py:447
  36.3 1.3 %collective-permute-done.7.far_pair_ref = f32[16,1280]{1,0:T(8,128)S(1)} collective-permute-done((f32[16,1280]{1,0:T(8,128)S(1)}, f32[16,1280]{1,0:T(8,128)S(1)}, u32[]{:S(2)}, u32[]{:S(2)}) %collective-permute-start.7) | collective-permute-done | bytes 81952 | tf_op jit(solution)/shard_map/ppermute | solution.py:477
  37.6 1.9 %collective-permute-done.6.near_pair_ref = f32[16,1280]{1,0:T(8,128)S(1)} collective-permute-done((f32[16,1280]{1,0:T(8,128)S(1)}, f32[16,1280]{1,0:T(8,128)S(1)}, u32[]{:S(2)}, u32[]{:S(2)}) %collective-permute-start.6) | collective-permute-done | bytes 81952 | tf_op jit(solution)/shard_map/ppermute | solution.py:477
  39.5 0.1 collective-permute-start.8
  39.5 0.0 collective-permute-done.10.payload_ref
  39.6 1.3 %shard_map.94 = (f32[16,4096]{1,0:T(8,128)S(1)}, f32[16,128]{1,0:T(8,128)}) custom-call(s32[8,128]{1,0:T(8,128)S(1)} %get-tuple-element.31.pairs_ref, f32[16,4096]{1,0:T(8,128)S(1)} %collective-permute-done.10.payload_ref, f32[16,4736]{1,0:T(8,128)S(1)} %get-tuple-element.45.payload_ref.table_ref, f32[16,4096]{1,0:T(8,128)S(1)} %get-tuple-element.54.refs_0_, ...), custom_call_target="tpu_custom_call" | custom-call | flops 2000000000 | bytes 14400000 | tf_op jit(solution)/shard_map/pallas_call | solution.py:447
  40.8 0.1 collective-permute-done.8.swapped_ref
  40.9 0.3 shard_map.93.one_ref
  41.2 1.9 %collective-permute-start.9 = (f32[16,128]{1,0:T(8,128)S(1)}, f32[16,128]{1,0:T(8,128)S(1)}, u32[]{:S(2)}, u32[]{:S(2)}) collective-permute-start(f32[16,128]{1,0:T(8,128)S(1)} %shard_map.93.one_ref), channel_id=1, source_target_pairs={{0,8},{1,9},{2,10},{3,11},{4,12},{5,13},{6,14},{7,15},{8,0},{9,1},... | collective-permute-start | bytes 24584 | tf_op jit(solution)/shard_map/ppermute | solution.py:477
  43.1 2.1 %shard_map.95.again_ref = f32[16,4096]{1,0:T(8,128)S(1)} custom-call(s32[16,32]{1,0:T(8,128)S(1)} %get-tuple-element.30.at_ref, f32[16,1280]{1,0:T(8,128)S(1)} %collective-permute-done.6.near_pair_ref, f32[16,1280]{1,0:T(8,128)S(1)} %collective-permute-done.7.far_pair_ref, f32[16,2688]{1,0:T(8,128)S(1)} %collective-permute-done.8.swapped_ref, ...), custom_call_target="tpu_custom_call" | custom-call | flops 1000000000 | bytes 7200000 | tf_op jit(solution)/shard_map/pallas_call | solution.py:447
  45.3 0.6 %collective-permute-done.9.two_ref = f32[16,128]{1,0:T(8,128)S(1)} collective-permute-done((f32[16,128]{1,0:T(8,128)S(1)}, f32[16,128]{1,0:T(8,128)S(1)}, u32[]{:S(2)}, u32[]{:S(2)}) %collective-permute-start.9) | collective-permute-done | bytes 8224 | tf_op jit(solution)/shard_map/ppermute | solution.py:477
  45.9 1.2 %shard_map.96 = (f32[16,4096]{1,0:T(8,128)}, f32[16,4096]{1,0:T(8,128)}) custom-call(f32[16,128]{1,0:T(8,128)S(1)} %shard_map.93.one_ref, f32[16,128]{1,0:T(8,128)S(1)} %collective-permute-done.9.two_ref, f32[16,4096]{1,0:T(8,128)S(1)} %get-tuple-element.52.image_ref, f32[16,4096]{1,0:T(8,128)S(1)} %shard_map.95.again_ref, ...), custom_call_target="tpu_custom_call" | custom-call | flops 500000000 | bytes 3600000 | tf_op jit(solution)/shard_map/pallas_call | solution.py:447
  (6 shorter events, 0.1 us)
Async XLA Ops:
  2.4 17.4 %collective-permute-start.4 = (f32[16,4864]{1,0:T(8,128)S(1)}, f32[16,4864]{1,0:T(8,128)S(1)}, u32[]{:S(2)}, u32[]{:S(2)}) collective-permute-start(f32[16,4864]{1,0:T(8,128)S(1)} %get-tuple-element.39), channel_id=1, source_target_pairs={{1,2},{2,1},{3,4},{4,3},{5,6},{6,5},{7,8},{8,7},{9,10},{10,9},{11,... | collective-permute-start | bytes 933896 | tf_op jit(solution)/shard_map/ppermute | solution.py:477
  3.1 7.1 %collective-permute-start = (f32[16,5632]{1,0:T(8,128)S(1)}, f32[16,5632]{1,0:T(8,128)S(1)}, u32[]{:S(2)}, u32[]{:S(2)}) collective-permute-start(f32[16,5632]{1,0:T(8,128)S(1)} %get-tuple-element.32.payload_ref.table_ref), channel_id=1, source_target_pairs={{0,1},{1,0},{2,3},{3,2},{4,5},{5,4},{6,7},{7,6},{8,9},{9,8},{10,11... | collective-permute-start | bytes 1081352 | tf_op jit(solution)/shard_map/ppermute | solution.py:477
  10.2 7.5 %collective-permute-start.2 = (f32[16,1536]{1,0:T(8,128)S(1)}, f32[16,1536]{1,0:T(8,128)S(1)}, u32[]{:S(2)}, u32[]{:S(2)}) collective-permute-start(f32[16,1536]{1,0:T(8,128)S(1)} %pad_maximum_fusion.2), channel_id=1, source_target_pairs={{0,4},{1,13},{2,6},{3,15},{4,8},{5,1},{6,10},{7,3},{8,12},{9,5},{1... | collective-permute-start | bytes 294920 | tf_op jit(solution)/shard_map/ppermute | solution.py:477
  12.5 7.3 %collective-permute-start.1 = (f32[16,1536]{1,0:T(8,128)S(1)}, f32[16,1536]{1,0:T(8,128)S(1)}, u32[]{:S(2)}, u32[]{:S(2)}) collective-permute-start(f32[16,1536]{1,0:T(8,128)S(1)} %pad_maximum_fusion.2), channel_id=1, source_target_pairs={{0,2},{1,15},{2,4},{3,1},{4,6},{5,3},{6,8},{7,5},{8,10},{9,7},{10,... | collective-permute-start | bytes 294920 | tf_op jit(solution)/shard_map/ppermute | solution.py:477
  19.8 1.6 %collective-permute-start.3 = (f32[16,3200]{1,0:T(8,128)S(1)}, f32[16,3200]{1,0:T(8,128)S(1)}, u32[]{:S(2)}, u32[]{:S(2)}) collective-permute-start(f32[16,3200]{1,0:T(8,128)S(1)} %pad_maximum_fusion), channel_id=1, source_target_pairs={{0,1},{1,0},{2,3},{3,2},{4,5},{5,4},{6,7},{7,6},{8,9},{9,8},{10,11... | collective-permute-start | bytes 614408 | tf_op jit(solution)/shard_map/ppermute | solution.py:477
  25.6 13.9 %collective-permute-start.10 = (f32[16,4096]{1,0:T(8,128)S(1)}, f32[16,4096]{1,0:T(8,128)S(1)}, u32[]{:S(2)}, u32[]{:S(2)}) collective-permute-start(f32[16,4096]{1,0:T(8,128)S(1)} %get-tuple-element.53), channel_id=1, source_target_pairs={{1,2},{2,1},{3,4},{4,3},{5,6},{6,5},{7,8},{8,7},{9,10},{10,9},{11,... | collective-permute-start | bytes 786440 | tf_op jit(solution)/shard_map/ppermute | solution.py:477
  26.3 4.1 %collective-permute-start.5 = (f32[16,4736]{1,0:T(8,128)S(1)}, f32[16,4736]{1,0:T(8,128)S(1)}, u32[]{:S(2)}, u32[]{:S(2)}) collective-permute-start(f32[16,4736]{1,0:T(8,128)S(1)} %get-tuple-element.45.payload_ref.table_ref), channel_id=1, source_target_pairs={{0,1},{1,0},{2,3},{3,2},{4,5},{5,4},{6,7},{7,6},{8,9},{9,8},{10,11... | collective-permute-start | bytes 909320 | tf_op jit(solution)/shard_map/ppermute | solution.py:477
  30.5 7.1 %collective-permute-start.7 = (f32[16,1280]{1,0:T(8,128)S(1)}, f32[16,1280]{1,0:T(8,128)S(1)}, u32[]{:S(2)}, u32[]{:S(2)}) collective-permute-start(f32[16,1280]{1,0:T(8,128)S(1)} %pad_maximum_fusion.3), channel_id=1, source_target_pairs={{0,4},{1,13},{2,6},{3,15},{4,8},{5,1},{6,10},{7,3},{8,12},{9,5},{1... | collective-permute-start | bytes 245768 | tf_op jit(solution)/shard_map/ppermute | solution.py:477
  32.3 7.1 %collective-permute-start.6 = (f32[16,1280]{1,0:T(8,128)S(1)}, f32[16,1280]{1,0:T(8,128)S(1)}, u32[]{:S(2)}, u32[]{:S(2)}) collective-permute-start(f32[16,1280]{1,0:T(8,128)S(1)} %pad_maximum_fusion.3), channel_id=1, source_target_pairs={{0,2},{1,15},{2,4},{3,1},{4,6},{5,3},{6,8},{7,5},{8,10},{9,7},{10,... | collective-permute-start | bytes 245768 | tf_op jit(solution)/shard_map/ppermute | solution.py:477
  39.5 1.5 %collective-permute-start.8 = (f32[16,2688]{1,0:T(8,128)S(1)}, f32[16,2688]{1,0:T(8,128)S(1)}, u32[]{:S(2)}, u32[]{:S(2)}) collective-permute-start(f32[16,2688]{1,0:T(8,128)S(1)} %pad_maximum_fusion.1), channel_id=1, source_target_pairs={{0,1},{1,0},{2,3},{3,2},{4,5},{5,4},{6,7},{7,6},{8,9},{9,8},{10,11... | collective-permute-start | bytes 516104 | tf_op jit(solution)/shard_map/ppermute | solution.py:477
  41.2 4.6 %collective-permute-start.9 = (f32[16,128]{1,0:T(8,128)S(1)}, f32[16,128]{1,0:T(8,128)S(1)}, u32[]{:S(2)}, u32[]{:S(2)}) collective-permute-start(f32[16,128]{1,0:T(8,128)S(1)} %shard_map.93.one_ref), channel_id=1, source_target_pairs={{0,8},{1,9},{2,10},{3,11},{4,12},{5,13},{6,14},{7,15},{8,0},{9,1},... | collective-permute-start | bytes 24584 | tf_op jit(solution)/shard_map/ppermute | solution.py:477

commit v5 on v4

--- a/solution.py
+++ b/solution.py
@@ -98,7 +98,7 @@
 
 
 def prepare_kernel(cl, vcl, rank, position_ref, vertices_hbm, corners_hbm, krylov_hbm, basis_hbm, far_hbm, near_hbm, offsets_hbm,
-                   payload_ref, heavy_ref, area_ref, center_ref, at_ref, pairs_ref, basis_ref, krylov_ref, offsets_ref,
+                   payload_ref, table_ref, area_ref, center_ref, at_ref, pairs_ref, basis_ref, krylov_ref, offsets_ref,
                    vertices_ref, corners_ref, raw_ref, far_ref, near_ref, mesh_ref, local_ref, sems):
     moves = copies((
         (vertices_hbm, vertices_ref), (corners_hbm, corners_ref), (krylov_hbm, krylov_ref), (basis_hbm, raw_ref),
@@ -123,23 +123,21 @@
             middle = (corner[0][k] + corner[1][k] + corner[2][k]) / 3.0
             lanes = slice(panels + k * cl + h * LANES, panels + k * cl + (h + 1) * LANES)
             payload_ref[:, lanes] = middle
-            heavy_ref[:, lanes] = middle
             sums[k] = middle if h == 0 else sums[k] + middle
         one = [corner[1][k] - corner[0][k] for k in range(3)]
         two = [corner[2][k] - corner[0][k] for k in range(3)]
         normal = [one[1] * two[2] - one[2] * two[1], one[2] * two[0] - one[0] * two[2], one[0] * two[1] - one[1] * two[0]]
         area_ref[:, h * LANES:(h + 1) * LANES] = 0.5 * jnp.sqrt(normal[0] * normal[0] + normal[1] * normal[1] + normal[2] * normal[2])
     span = clusters * rank
-    table = panels + 3 * cl
     mine = lax.broadcasted_iota(jnp.int32, (clusters, span), 1) // rank == lax.broadcasted_iota(jnp.int32, (clusters, span), 0)
     half = span // 2
-    payload_ref[:, table + span:] = jnp.zeros_like(payload_ref[:, table + span:])
+    table_ref[:, span:] = jnp.zeros_like(table_ref[:, span:])
     for k in range(3):
         center = jnp.sum(sums[k], axis=1, keepdims=True) / cl
         center_ref[:, k * LANES:(k + 1) * LANES] = jnp.broadcast_to(center, (clusters, LANES))
         row = jnp.sum(jnp.where(mine, center, 0.0), axis=0, keepdims=True)
-        payload_ref[k:k + 1, table + span:] = row[:, 0:half]
-        payload_ref[8 + k:9 + k, table + span:] = row[:, half:]
+        table_ref[k:k + 1, span:] = row[:, 0:half]
+        table_ref[8 + k:9 + k, span:] = row[:, half:]
     moves[2].wait()
     moves[3].wait()
     for c in range(clusters):
@@ -147,8 +145,7 @@
         basis_ref[:, lanes] = stacked(raw_ref[:, lanes])
         charges = area_ref[c:c + 1, :] * krylov_ref[:, lanes]
         payload_ref[:, lanes] = charges
-        heavy_ref[:, lanes] = charges
-        payload_ref[:, table + c * rank:table + (c + 1) * rank] = moments_of(charges, basis_ref[:, lanes])
+        table_ref[:, c * rank:(c + 1) * rank] = moments_of(charges, basis_ref[:, lanes])
     moves[4].wait()
     far = far_ref[...]
     step = (lax.div(far, clusters) - position_ref[0]) * (1 - 2 * lax.rem(position_ref[0], 2))
@@ -228,24 +225,8 @@
     return lax.shift_right_logical(pair, 6), lax.bitwise_and(pair, 63)
 
 
-def near_kernel(cl, which, pairs_ref, payload_ref, table_ref, *refs):
-    if which:
-        targets_ref, start_ref, kept_ref, near_out_ref, tail_ref, pieces_ref, sources_ref, total_ref = refs
-    else:
-        own_ref, kept_ref, near_out_ref, targets_ref, tail_ref, pieces_ref, sources_ref, total_ref = refs
-    tail_ref[...] = table_ref[:, table_ref.shape[1] - tail_ref.shape[1]:]
-    panels = near_out_ref.shape[1]
-    clusters = panels // cl
+def build_list(which, pairs_ref, targets_ref, kept_ref, pieces_ref, sources_ref, total_ref):
     group = kept_ref.shape[1]
-    fill_charges(pieces_ref, payload_ref, clusters, cl)
-    fill_features(sources_ref, payload_ref, panels, cl)
-    if which:
-        total_ref[...] = jnp.zeros_like(total_ref)
-    else:
-        for c in range(clusters):
-            target = features_of(payload_ref, panels, c, cl, True).astype(BF16)
-            targets_ref[c] = target
-            total_ref[c] = near_block(sources_ref[c], target, pieces_ref[c], own_ref.at[c])
 
     def step(m, _):
         pairs = [pair_at(pairs_ref, which, group * m + w) for w in range(group)]
@@ -256,26 +237,10 @@
         return 0
 
     lax.fori_loop(0, (pairs_ref[3 + which, 0] + group - 1) // group, step, 0)
-    for c in range(clusters):
-        lanes = slice(c * cl, (c + 1) * cl)
-        near = folded(total_ref[c])
-        near_out_ref[:, lanes] = start_ref[:, lanes] + near if which else near
-
-
-def near_again_kernel(cl, which, pairs_ref, payload_ref, table_ref, *refs):
-    if which:
-        start_ref, kept_ref, near_out_ref, tail_ref, pieces_ref, total_ref = refs
-    else:
-        own_ref, kept_ref, near_out_ref, tail_ref, pieces_ref, total_ref = refs
-    tail_ref[...] = table_ref[:, table_ref.shape[1] - tail_ref.shape[1]:]
-    clusters = near_out_ref.shape[1] // cl
+
+
+def apply_list(which, pairs_ref, kept_ref, pieces_ref, total_ref, cl):
     group = kept_ref.shape[1]
-    fill_charges(pieces_ref, payload_ref, clusters, cl)
-    if which:
-        total_ref[...] = jnp.zeros_like(total_ref)
-    else:
-        for c in range(clusters):
-            total_ref[c] = near_product(pieces_ref[c], own_ref.at[c], cl)
 
     def step(m, _):
         pairs = [pair_at(pairs_ref, which, group * m + w) for w in range(group)]
@@ -285,10 +250,113 @@
         return 0
 
     lax.fori_loop(0, (pairs_ref[3 + which, 0] + group - 1) // group, step, 0)
-    for c in range(clusters):
+
+
+def put_total(cl, total_ref, start_ref, out_ref):
+    for c in range(total_ref.shape[0]):
         lanes = slice(c * cl, (c + 1) * cl)
         near = folded(total_ref[c])
-        near_out_ref[:, lanes] = start_ref[:, lanes] + near if which else near
+        out_ref[:, lanes] = near if start_ref is None else start_ref[:, lanes] + near
+
+
+def own_kernel(cl, pairs_ref, payload_ref, beside_ref, own_ref, kept_ref, near_out_ref, targets_ref, tail_ref, pieces_ref, sources_ref, total_ref):
+    tail_ref[...] = beside_ref[:, beside_ref.shape[1] - LANES:]
+    panels = near_out_ref.shape[1]
+    clusters = panels // cl
+    fill_charges(pieces_ref, payload_ref, clusters, cl)
+    fill_features(sources_ref, payload_ref, panels, cl)
+    for c in range(clusters):
+        target = features_of(payload_ref, panels, c, cl, True).astype(BF16)
+        targets_ref[c] = target
+        total_ref[c] = near_block(sources_ref[c], target, pieces_ref[c], own_ref.at[c])
+    build_list(0, pairs_ref, targets_ref, kept_ref, pieces_ref, sources_ref, total_ref)
+    put_total(cl, total_ref, None, near_out_ref)
+
+
+def partner_kernel(cl, pairs_ref, payload_ref, targets_ref, start_ref, kept_ref, near_out_ref, pieces_ref, sources_ref, total_ref):
+    panels = near_out_ref.shape[1]
+    fill_charges(pieces_ref, payload_ref, panels // cl, cl)
+    fill_features(sources_ref, payload_ref, panels, cl)
+    total_ref[...] = jnp.zeros_like(total_ref)
+    build_list(1, pairs_ref, targets_ref, kept_ref, pieces_ref, sources_ref, total_ref)
+    put_total(cl, total_ref, start_ref, near_out_ref)
+
+
+def image_kernel(cl, rank, pairs_ref, payload_ref, targets_ref, start_ref, area_ref, krylov_ref, basis_ref,
+                 kept_ref, image_ref, charges_ref, table_ref, pieces_ref, sources_ref, total_ref):
+    rhs, panels = image_ref.shape
+    clusters = panels // cl
+    span = clusters * rank
+    fill_charges(pieces_ref, payload_ref, clusters, cl)
+    fill_features(sources_ref, payload_ref, panels, cl)
+    total_ref[...] = jnp.zeros_like(total_ref)
+    build_list(2, pairs_ref, targets_ref, kept_ref, pieces_ref, sources_ref, total_ref)
+    squared = correlation = jnp.zeros((rhs, cl), F32)
+    for c in range(clusters):
+        lanes = slice(c * cl, (c + 1) * cl)
+        area = area_ref[c:c + 1, :]
+        image = COULOMB * area * (start_ref[:, lanes] + folded(total_ref[c]))
+        charges = area * image
+        image_ref[:, lanes] = image
+        charges_ref[:, lanes] = charges
+        table_ref[:, c * rank:(c + 1) * rank] = moments_of(charges, basis_ref[:, lanes])
+        krylov = krylov_ref[:, lanes]
+        squared = squared + krylov * krylov
+        correlation = correlation + krylov * image
+    squared = jnp.sum(squared, axis=1, keepdims=True)
+    correlation = jnp.sum(correlation, axis=1, keepdims=True)
+    local = ratio(correlation, squared)
+    energy = jnp.zeros((rhs, cl), F32)
+    for c in range(clusters):
+        lanes = slice(c * cl, (c + 1) * cl)
+        residual = image_ref[:, lanes] - local * krylov_ref[:, lanes]
+        energy = energy + residual * residual
+    table_ref[:, span:] = in_lanes(squared, correlation, jnp.sum(energy, axis=1, keepdims=True), local)
+
+
+def own_again_kernel(cl, pairs_ref, payload_ref, beside_ref, own_ref, kept_ref, near_out_ref, tail_ref, pieces_ref, total_ref):
+    tail_ref[...] = beside_ref[:, beside_ref.shape[1] - LANES:]
+    clusters = near_out_ref.shape[1] // cl
+    fill_charges(pieces_ref, payload_ref, clusters, cl)
+    for c in range(clusters):
+        total_ref[c] = near_product(pieces_ref[c], own_ref.at[c], cl)
+    apply_list(0, pairs_ref, kept_ref, pieces_ref, total_ref, cl)
+    put_total(cl, total_ref, None, near_out_ref)
+
+
+def partner_again_kernel(cl, pairs_ref, payload_ref, start_ref, kept_ref, near_out_ref, pieces_ref, total_ref):
+    fill_charges(pieces_ref, payload_ref, near_out_ref.shape[1] // cl, cl)
+    total_ref[...] = jnp.zeros_like(total_ref)
+    apply_list(1, pairs_ref, kept_ref, pieces_ref, total_ref, cl)
+    put_total(cl, total_ref, start_ref, near_out_ref)
+
+
+def finish_kernel(cl, total, pairs_ref, payload_ref, start_ref, kept_ref, area_ref, image_ref, krylov_ref, one_ref, two_ref,
+                  next_hbm, second_hbm, pieces_ref, total_ref, next_ref, second_ref, sems):
+    panels = image_ref.shape[1]
+    clusters = panels // cl
+    squared, correlation, energy, local = merged([one_ref[...], two_ref[...]])
+    projection = correlation / (squared + 1e-06)
+    gap = projection - local
+    scaling = 1.0 / jnp.sqrt((energy + gap * gap * squared) / total + 1e-06)
+    for c in range(clusters):
+        lanes = slice(c * cl, (c + 1) * cl)
+        next_ref[:, lanes] = (image_ref[:, lanes] - projection * krylov_ref[:, lanes]) * scaling
+    moves = copies(((next_ref, next_hbm),), sems)
+    fill_charges(pieces_ref, payload_ref, clusters, cl)
+    total_ref[...] = jnp.zeros_like(total_ref)
+    apply_list(2, pairs_ref, kept_ref, pieces_ref, total_ref, cl)
+    parts = 2
+    for h in range(parts):
+        for c in range(h * clusters // parts, (h + 1) * clusters // parts):
+            lanes = slice(c * cl, (c + 1) * cl)
+            again = COULOMB * area_ref[c:c + 1, :] * (start_ref[:, lanes] + folded(total_ref[c]))
+            second_ref[:, lanes] = (again - projection * image_ref[:, lanes]) * scaling
+        lanes = slice(h * panels // parts, (h + 1) * panels // parts)
+        moves.append(pltpu.make_async_copy(second_ref.at[:, lanes], second_hbm.at[:, lanes], sems.at[1 + h]))
+        moves[-1].start()
+    for move in moves:
+        move.wait()
 
 
 def load_window(tables, clusters, rank, pieces_ref, middle_ref):
@@ -332,12 +400,10 @@
     return folded(dot_nn(fields_ref[c], basis))
 
 
-def image_kernel(cl, rank, at_ref, near_pair_ref, far_pair_ref, swapped_ref, center_ref, area_ref, near_ref, basis_ref, krylov_ref, offsets_ref,
-                 image_ref, payload_ref, heavy_ref, coupling_ref, pieces_ref, middle_ref, gathered_ref, fields_ref):
-    rhs, panels = near_ref.shape
-    clusters = panels // cl
+def far_kernel(cl, rank, at_ref, near_pair_ref, far_pair_ref, swapped_ref, center_ref, near_ref, basis_ref, offsets_ref,
+               out_ref, coupling_ref, pieces_ref, middle_ref, gathered_ref, fields_ref):
+    clusters = near_ref.shape[1] // cl
     per = LANES // rank
-    span = clusters * rank
     load_window(six_tables(near_pair_ref, far_pair_ref, swapped_ref), clusters, rank, pieces_ref, middle_ref)
     lane = lax.broadcasted_iota(jnp.int32, (1, LANES), 1) // rank
     for c in range(clusters):
@@ -351,29 +417,13 @@
             coupling_ref[c, 0:rank, lanes] = high
             coupling_ref[c, rank:2 * rank, lanes] = low
     far_fields(gathered_ref, coupling_ref, fields_ref)
-    squared = correlation = jnp.zeros((rhs, cl), F32)
     for c in range(clusters):
         lanes = slice(c * cl, (c + 1) * cl)
-        basis = basis_ref[:, lanes]
-        area = area_ref[c:c + 1, :]
-        image = COULOMB * area * (near_ref[:, lanes] + far_potential(fields_ref, c, basis))
-        charges = area * image
-        image_ref[:, lanes] = image
-        payload_ref[:, lanes] = charges
-        heavy_ref[:, lanes] = charges
-        payload_ref[:, panels + c * rank:panels + (c + 1) * rank] = moments_of(charges, basis)
-        krylov = krylov_ref[:, lanes]
-        squared = squared + krylov * krylov
-        correlation = correlation + krylov * image
-    squared = jnp.sum(squared, axis=1, keepdims=True)
-    correlation = jnp.sum(correlation, axis=1, keepdims=True)
-    local = ratio(correlation, squared)
-    residual = image_ref[...] - local * krylov_ref[...]
-    payload_ref[:, panels + span:] = in_lanes(squared, correlation, jnp.sum(residual * residual, axis=1, keepdims=True), local)
-
-
-def far_again_kernel(cl, rank, at_ref, near_pair_ref, far_pair_ref, swapped_ref, near_ref, area_ref, coupling_ref, basis_ref,
-                     image_ref, pieces_ref, gathered_ref, fields_ref):
+        out_ref[:, lanes] = near_ref[:, lanes] + far_potential(fields_ref, c, basis_ref[:, lanes])
+
+
+def far_again_kernel(cl, rank, at_ref, near_pair_ref, far_pair_ref, swapped_ref, near_ref, coupling_ref, basis_ref,
+                     out_ref, pieces_ref, gathered_ref, fields_ref):
     clusters = near_ref.shape[1] // cl
     per = LANES // rank
     load_window(six_tables(near_pair_ref, far_pair_ref, swapped_ref), clusters, rank, pieces_ref, None)
@@ -384,26 +434,7 @@
     far_fields(gathered_ref, coupling_ref, fields_ref)
     for c in range(clusters):
         lanes = slice(c * cl, (c + 1) * cl)
-        image_ref[:, lanes] = COULOMB * area_ref[c:c + 1, :] * (near_ref[:, lanes] + far_potential(fields_ref, c, basis_ref[:, lanes]))
-
-
-def finish_kernel(total, one_ref, two_ref, image_ref, again_ref, krylov_ref, next_hbm, second_hbm, next_ref, second_ref, sems):
-    squared, correlation, energy, local = merged([one_ref[...], two_ref[...]])
-    projection = correlation / (squared + 1e-06)
-    gap = projection - local
-    scaling = 1.0 / jnp.sqrt((energy + gap * gap * squared) / total + 1e-06)
-    moves = []
-    part = next_ref.shape[1] // 4
-    for h in range(4):
-        lanes = slice(h * part, (h + 1) * part)
-        image = image_ref[:, lanes]
-        next_ref[:, lanes] = (image - projection * krylov_ref[:, lanes]) * scaling
-        second_ref[:, lanes] = (again_ref[:, lanes] - projection * image) * scaling
-        for held, hbm in ((next_ref, next_hbm), (second_ref, second_hbm)):
-            moves.append(pltpu.make_async_copy(held.at[:, lanes], hbm.at[:, lanes], sems.at[len(moves)]))
-            moves[-1].start()
-    for move in moves:
-        move.wait()
+        out_ref[:, lanes] = near_ref[:, lanes] + far_potential(fields_ref, c, basis_ref[:, lanes])
 
 
 def ratio(correlation, squared):
@@ -479,21 +510,21 @@
     def outward(value, steps):
         return move(value, [(i, (i + steps * (1 - 2 * (i % 2))) % devices) for i in range(devices)])
 
-    def neighbours(payload, heavy):
-        return move(payload, pairing), move(heavy, bridging)
-
-    def pairs_away(tail, partner):
-        pair = jnp.concatenate([tail, partner[:, partner.shape[1] - tail.shape[1]:]], axis=1)
-        return outward(pair, 2), outward(pair, 4)
+    def exchange(payload, table):
+        beside = move(table, pairing)
+        pair = jnp.concatenate([table, beside], axis=1)
+        near_pair, far_pair = outward(pair, 2), outward(pair, 4)
+        last = move(jnp.concatenate([payload, beside[:, beside.shape[1] - LANES:]], axis=1), bridging)
+        return beside, near_pair, far_pair, last, move(payload, pairing)
 
     def swapped(near_pair, far_pair, tail):
         return move(jnp.concatenate([near_pair, far_pair, tail], axis=1), pairing)
 
     whole = ((rhs, panels), F32)
-    payload, heavy, area, centers, at, pairs, basis, krylov, offsets = call(
+    payload, table, area, centers, at, pairs, basis, krylov, offsets = call(
         functools.partial(prepare_kernel, cl, vcl, rank),
         [
-            ((rhs, panels + 3 * cl + width), F32), ((rhs, panels + 3 * cl), F32), ((clusters, cl), F32), ((clusters, 3 * LANES), F32),
+            ((rhs, panels + 3 * cl), F32), ((rhs, width), F32), ((clusters, cl), F32), ((clusters, 3 * LANES), F32),
             (far_pairs.shape, jnp.int32), ((8, LANES), jnp.int32), ((2 * rank, panels), BF16), whole, (offsets.shape, F32),
         ],
         [
@@ -510,7 +541,7 @@
         position, vertices, panel_vertices, krylov, basis, far_pairs, near_pairs.T, offsets,
         us=1.5,
     )
-    partner, other = neighbours(payload, heavy)
+    beside, near_pair, far_pair, other, partner = exchange(payload, table)
     group = 4
     own = ((clusters, 2 * cl, cl), BF16)
     kept = ((clusters * (slots - 1) // group, group, 2 * cl, cl), BF16)
@@ -519,92 +550,83 @@
     pieces = pltpu.VMEM((clusters + 1, 2 * rhs, cl), BF16)
     sources = pltpu.VMEM((clusters + 1, FEATURES, cl), BF16)
     own_blocks, blocks, near, targets, tail = call(
-        functools.partial(near_kernel, cl, 0),
-        [own, kept, whole, ((clusters, FEATURES, cl), BF16), ((rhs, width), F32)],
+        functools.partial(own_kernel, cl),
+        [own, kept, whole, ((clusters, FEATURES, cl), BF16), sums_shape],
         [pieces, sources, total],
         "svv>ppvpv",
-        pairs, payload, payload,
+        pairs, payload, beside,
         us=8.0,
     )
-    near_pair, far_pair = pairs_away(tail, partner)
-    blocks_partner, near, tail = call(
-        functools.partial(near_kernel, cl, 1),
-        [kept, whole, sums_shape],
+    swap = swapped(near_pair, far_pair, tail)
+    blocks_partner, near = call(
+        functools.partial(partner_kernel, cl),
+        [kept, whole],
         [pieces, sources, total],
-        "svvpv>pvv",
-        pairs, partner, payload, targets, near,
-        us=4.0,
-    )
-    swap = swapped(near_pair, far_pair, tail)
-    blocks_other, near, _ = call(
-        functools.partial(near_kernel, cl, 2),
-        [kept, whole, sums_shape],
-        [pieces, sources, total],
-        "svvpv>pvv",
-        pairs, other, payload, targets, near,
+        "svpv>pv",
+        pairs, partner, targets, near,
         us=4.0,
     )
     tiles = 6 * per * span // LANES
     window = pltpu.VMEM((tiles, 2 * rhs, LANES), BF16)
     gathered = pltpu.VMEM((clusters, 2 * rhs, partners * rank), BF16)
     fields = pltpu.VMEM((clusters, 2 * rhs, 2 * rank), BF16)
-    image, payload, heavy, coupling = call(
+    near, coupling = call(
+        functools.partial(far_kernel, cl, rank),
+        [whole, ((clusters, 2 * rank, partners * rank), BF16)],
+        [window, pltpu.VMEM((tiles, 8, LANES), F32), gathered, fields],
+        "svvvvvpp>vp",
+        at, near_pair, far_pair, swap, centers, near, basis, offsets,
+        us=4.0,
+    )
+    blocks_other, image, payload, table = call(
         functools.partial(image_kernel, cl, rank),
-        [whole, ((rhs, panels + span + LANES), F32), whole, ((clusters, 2 * rank, partners * rank), BF16)],
-        [window, pltpu.VMEM((tiles, 8, LANES), F32), gathered, fields],
-        "svvvvvvppp>vvvp",
-        at, near_pair, far_pair, swap, centers, area, near, basis, krylov, offsets,
-        us=4.5,
-    )
-    partner, other = neighbours(payload, heavy)
+        [kept, whole, whole, ((rhs, span + LANES), F32)],
+        [pieces, sources, total],
+        "svpvvpp>pvvv",
+        pairs, other, targets, near, area, krylov, basis,
+        us=4.0,
+    )
+    beside, near_pair, far_pair, other, partner = exchange(payload, table)
     near, tail = call(
-        functools.partial(near_again_kernel, cl, 0),
-        [whole, ((rhs, span + LANES), F32)],
+        functools.partial(own_again_kernel, cl),
+        [whole, sums_shape],
         [pieces, total],
         "svvpp>vv",
-        pairs, payload, payload, own_blocks, blocks,
+        pairs, payload, beside, own_blocks, blocks,
         us=8.0,
     )
-    near_pair, far_pair = pairs_away(tail, partner)
-    near, tail = call(
-        functools.partial(near_again_kernel, cl, 1),
-        [whole, sums_shape],
+    swap = swapped(near_pair, far_pair, tail)
+    (near,) = call(
+        functools.partial(partner_again_kernel, cl),
+        [whole],
         [pieces, total],
-        "svvvp>vv",
-        pairs, partner, payload, near, blocks_partner,
+        "svvp>v",
+        pairs, partner, near, blocks_partner,
         us=4.0,
     )
-    swap = swapped(near_pair, far_pair, tail)
-    near, _ = call(
-        functools.partial(near_again_kernel, cl, 2),
-        [whole, sums_shape],
-        [pieces, total],
-        "svvvp>vv",
-        pairs, other, payload, near, blocks_other,
-        us=4.0,
-    )
-    (one,) = call(window_sums_kernel, [sums_shape], [], "vvvvv>v", payload, partner, near_pair, far_pair, swap, us=0.3)
+    (one,) = call(window_sums_kernel, [sums_shape], [], "vvvvv>v", table, beside, near_pair, far_pair, swap, us=0.3)
     size = 8
     many = outward(one, size)
     while 2 * size < devices:
         (one,) = call(merge_kernel, [sums_shape], [], "vv>v", one, many, us=0.3)
         size = 2 * size
         many = outward(one, size)
-    (again,) = call(
+    (near,) = call(
         functools.partial(far_again_kernel, cl, rank),
         [whole],
         [window, gathered, fields],
-        "svvvvvpp>v",
-        at, near_pair, far_pair, swap, near, area, coupling, basis,
-        us=2.0,
+        "svvvvpp>v",
+        at, near_pair, far_pair, swap, near, coupling, basis,
+        us=4.0,
     )
     here = pltpu.VMEM((rhs, panels), F32)
     return tuple(call(
-        functools.partial(finish_kernel, panels * devices),
+        functools.partial(finish_kernel, cl, panels * devices),
         [whole, whole],
-        [here, here, pltpu.SemaphoreType.DMA((8,))],
-        "vvvvp>hh",
-        one, many, image, again, krylov,
+        [pieces, total, here, here, pltpu.SemaphoreType.DMA((3,))],
+        "svvpvvpvv>hh",
+        pairs, other, near, blocks_other, area, image, krylov, one, many,
+        us=3.0,
     ))
 
 

time: 47.4 us -> 46.6 us (0.983); the launches traced: 47.1 us -> 46.8 us
  waiting for transfers between devices: 8.23 us -> 10.7 us
  Pallas kernels: 20.3 us -> 18.4 us
  starting transfers between devices: 17.7 us -> 16.9 us
    ppermute x11 -> x13, waiting for transfers between devices: 8.23 us -> 10.7 us  [move(): return lax.ppermute(value, 'clus', pairs)]
    pallas_call x11 -> x10, Pallas kernels: 20.3 us -> 18.4 us  [call(): pl.pallas_call(kernel, out_shape=[pltpu.VMEM(*out) if m == 'p' else jax.S...]
    ppermute x11 -> x13, starting transfers between devices: 17.7 us -> 16.9 us  [move(): return lax.ppermute(value, 'clus', pairs)]
  transfers between devices with their start and end apart: 11 -> 13, of which waited for: 6 -> 7; matrix products, arithmetic and copies ran while one was open for 0% -> 0% of each run, Pallas kernels for 27% -> 29%
where the time goes in v5:
time: 46.6 us; the launch traced here: 46.8 us
  Pallas kernels  18.4 us (39%)
  starting transfers between devices  16.9 us (36%)
  waiting for transfers between devices  10.7 us (23%)
  between operations  0.76 us (2%)
    pallas_call x10, Pallas kernels, call(): pl.pallas_call(kernel, out_shape=[pltpu.VMEM(*out) if m == 'p' else jax.S...  18.4 us
    ppermute x13, starting transfers between devices, move(): return lax.ppermute(value, 'clus', pairs)  16.9 us
    ppermute x13, waiting for transfers between devices, move(): return lax.ppermute(value, 'clus', pairs)  10.7 us
  transfers between devices with their start and end apart: 13, of which 7 were waited for; matrix products, arithmetic and copies ran while one was open for 0% of the time, Pallas kernels for 29%

profile of v5, /device:TPU:0, one launch (start us, length us, event | category | flops | bytes accessed | tf_op | source)
XLA Modules:
  0.0 46.8 jit_solution(9632301492663005773)
XLA Ops:
  0.6 1.8 %shard_map.86 = (f32[16,4864]{1,0:T(8,128)S(1)}, f32[16,768]{1,0:T(8,128)S(1)}, f32[16,256]{1,0:T(8,128)S(1)}, f32[16,384]{1,0:T(8,128)S(1)}, s32[16,32]{1,0:T(8...) custom-call(s32[1]{0:T(128)} %bitcast.position_ref, ...), custom_call_target="tpu_custom_call" | custom-call | flops 750000000 | bytes 5400000 | tf_op jit(solution)/shard_map/pallas_call | solution.py:478
  2.4 0.5 %collective-permute-start = (f32[16,768]{1,0:T(8,128)S(1)}, f32[16,768]{1,0:T(8,128)S(1)}, u32[]{:S(2)}, u32[]{:S(2)}) collective-permute-start(f32[16,768]{1,0:T(8,128)S(1)} %get-tuple-element.28), channel_id=1, source_target_pairs={{0,1},{1,0},{2,3},{3,2},{4,5},{5,4},{6,7},{7,6},{8,9},{9,8},{10,11... | collective-permute-start | bytes 147464 | tf_op jit(solution)/shard_map/ppermute | solution.py:508
  3.0 0.1 collective-permute-start.5
  3.0 0.8 %collective-permute-done.beside_ref = f32[16,768]{1,0:T(8,128)S(1)} collective-permute-done((f32[16,768]{1,0:T(8,128)S(1)}, f32[16,768]{1,0:T(8,128)S(1)}, u32[]{:S(2)}, u32[]{:S(2)}) %collective-permute-start) | collective-permute-done | bytes 49184 | tf_op jit(solution)/shard_map/ppermute | solution.py:508
  3.9 2.9 %collective-permute-start.3 = (f32[16,1536]{1,0:T(8,128)S(1)}, f32[16,1536]{1,0:T(8,128)S(1)}, u32[]{:S(2)}, u32[]{:S(2)}) collective-permute-start(f32[16,1536]{1,0:T(8,128)S(1)} %constant_dynamic-update-slice_fusion), channel_id=1, source_target_pairs={{0,4},{1,13},{2,6},{3,15},{4,8},{5,1},{6,10},{7,3},{8,12},{9,5},{1... | collective-permute-start | bytes 294920 | tf_op jit(solution)/shard_map/ppermute | solution.py:508
  6.8 1.5 %collective-permute-start.2 = (f32[16,1536]{1,0:T(8,128)S(1)}, f32[16,1536]{1,0:T(8,128)S(1)}, u32[]{:S(2)}, u32[]{:S(2)}) collective-permute-start(f32[16,1536]{1,0:T(8,128)S(1)} %constant_dynamic-update-slice_fusion), channel_id=1, source_target_pairs={{0,2},{1,15},{2,4},{3,1},{4,6},{5,3},{6,8},{7,5},{8,10},{9,7},{10,... | collective-permute-start | bytes 294920 | tf_op jit(solution)/shard_map/ppermute | solution.py:508
  8.3 2.7 %shard_map.87 = (bf16[16,512,256]{2,1,0:T(8,128)(2,1)S(1)}, bf16[12,4,512,256]{3,2,1,0:T(8,128)(2,1)S(1)}, f32[16,4096]{1,0:T(8,128)S(1)}, bf16[16,80,256]{2,1,0:T(8,128)(2,1)S(1)}, f32[16,128]{1,0:T(8,128)S(1)}) custom-call(s32[8,128]{1,0:T(8,128)S(1)} %get-tuple-element.26.pairs_ref, f32[16,4864]{1,0:T(8,128)S(1)} %get-tuple-element.27.payload_ref, ...), custom_call_target="tpu_custom_call" | custom-call | flops 4000000000 | bytes 28800000 | tf_op jit(solution)/shard_map/pallas_call | solution.py:478
  11.0 1.4 %collective-permute-done.3.far_pair_ref = f32[16,1536]{1,0:T(8,128)S(1)} collective-permute-done((f32[16,1536]{1,0:T(8,128)S(1)}, f32[16,1536]{1,0:T(8,128)S(1)}, u32[]{:S(2)}, u32[]{:S(2)}) %collective-permute-start.3) | collective-permute-done | bytes 98336 | tf_op jit(solution)/shard_map/ppermute | solution.py:508
  12.3 1.7 %collective-permute-done.2.near_pair_ref = f32[16,1536]{1,0:T(8,128)S(1)} collective-permute-done((f32[16,1536]{1,0:T(8,128)S(1)}, f32[16,1536]{1,0:T(8,128)S(1)}, u32[]{:S(2)}, u32[]{:S(2)}) %collective-permute-start.2) | collective-permute-done | bytes 98336 | tf_op jit(solution)/shard_map/ppermute | solution.py:508
  14.1 0.3 collective-permute-start.4
  14.4 0.7 %collective-permute-start.1 = (f32[16,4992]{1,0:T(8,128)S(1)}, f32[16,4992]{1,0:T(8,128)S(1)}, u32[]{:S(2)}, u32[]{:S(2)}) collective-permute-start(f32[16,4992]{1,0:T(8,128)S(1)} %pad_maximum_fusion), channel_id=1, source_target_pairs={{1,2},{2,1},{3,4},{4,3},{5,6},{6,5},{7,8},{8,7},{9,10},{10,9},{11,... | collective-permute-start | bytes 958472 | tf_op jit(solution)/shard_map/ppermute | solution.py:508
  15.1 0.0 collective-permute-done.5.payload_ref
  15.1 2.1 %shard_map.88 = (bf16[12,4,512,256]{3,2,1,0:T(8,128)(2,1)S(1)}, f32[16,4096]{1,0:T(8,128)S(1)}) custom-call(s32[8,128]{1,0:T(8,128)S(1)} %get-tuple-element.26.pairs_ref, f32[16,4864]{1,0:T(8,128)S(1)} %collective-permute-done.5.payload_ref, bf16[16,80,256]{2,1,0:T(8,128)(2,1)S(1)} %get-tuple-element.29.targets_ref, f32[16,4096]{1,0:T(8,128)S(1)} %get-tuple-element.33.start_ref), custom_call_target="tpu_custom_call" | custom-call | flops 2000000000 | bytes 14400000 | tf_op jit(solution)/shard_map/pallas_call | solution.py:478
  17.2 0.0 collective-permute-done.4.swapped_ref
  17.2 3.2 %shard_map.89 = (f32[16,4096]{1,0:T(8,128)S(1)}, bf16[16,64,1024]{2,1,0:T(8,128)(2,1)S(1)}) custom-call(s32[16,32]{1,0:T(8,128)S(1)} %get-tuple-element.30.at_ref, f32[16,1536]{1,0:T(8,128)S(1)} %collective-permute-done.2.near_pair_ref, f32[16,1536]{1,0:T(8,128)S(1)} %collective-permute-done.3.far_pair_ref, ...), custom_call_target="tpu_custom_call" | custom-call | flops 2000000000 | bytes 14400000 | tf_op jit(solution)/shard_map/pallas_call | solution.py:478
  20.5 0.0 collective-permute-done.1.payload_ref
  20.5 1.3 %shard_map.90 = (bf16[12,4,512,256]{3,2,1,0:T(8,128)(2,1)S(1)}, f32[16,4096]{1,0:T(8,128)S(1)}, f32[16,4096]{1,0:T(8,128)S(1)}, f32[16,640]{1,0:T(8,128)S(1)}) custom-call(s32[8,128]{1,0:T(8,128)S(1)} %get-tuple-element.26.pairs_ref, f32[16,4992]{1,0:T(8,128)S(1)} %collective-permute-done.1.payload_ref, ...), custom_call_target="tpu_custom_call" | custom-call | flops 2000000000 | bytes 14400000 | tf_op jit(solution)/shard_map/pallas_call | solution.py:478
  21.8 4.9 %collective-permute-start.6 = (f32[16,640]{1,0:T(8,128)S(1)}, f32[16,640]{1,0:T(8,128)S(1)}, u32[]{:S(2)}, u32[]{:S(2)}) collective-permute-start(f32[16,640]{1,0:T(8,128)S(1)} %get-tuple-element.41.payload_ref), channel_id=1, source_target_pairs={{0,1},{1,0},{2,3},{3,2},{4,5},{5,4},{6,7},{7,6},{8,9},{9,8},{10,11... | collective-permute-start | bytes 122888 | tf_op jit(solution)/shard_map/ppermute | solution.py:508
  26.7 0.1 collective-permute-start.11
  26.8 0.8 %collective-permute-done.6.beside_ref.partner_ref = f32[16,640]{1,0:T(8,128)S(1)} collective-permute-done((f32[16,640]{1,0:T(8,128)S(1)}, f32[16,640]{1,0:T(8,128)S(1)}, u32[]{:S(2)}, u32[]{:S(2)}) %collective-permute-start.6) | collective-permute-done | bytes 40992 | tf_op jit(solution)/shard_map/ppermute | solution.py:508
  27.5 1.7 %collective-permute-start.9 = (f32[16,1280]{1,0:T(8,128)S(1)}, f32[16,1280]{1,0:T(8,128)S(1)}, u32[]{:S(2)}, u32[]{:S(2)}) collective-permute-start(f32[16,1280]{1,0:T(8,128)S(1)} %constant_dynamic-update-slice_fusion.2), channel_id=1, source_target_pairs={{0,4},{1,13},{2,6},{3,15},{4,8},{5,1},{6,10},{7,3},{8,12},{9,5},{1... | collective-permute-start | bytes 245768 | tf_op jit(solution)/shard_map/ppermute | solution.py:508
  29.2 1.4 %collective-permute-start.8 = (f32[16,1280]{1,0:T(8,128)S(1)}, f32[16,1280]{1,0:T(8,128)S(1)}, u32[]{:S(2)}, u32[]{:S(2)}) collective-permute-start(f32[16,1280]{1,0:T(8,128)S(1)} %constant_dynamic-update-slice_fusion.2), channel_id=1, source_target_pairs={{0,2},{1,15},{2,4},{3,1},{4,6},{5,3},{6,8},{7,5},{8,10},{9,7},{10,... | collective-permute-start | bytes 245768 | tf_op jit(solution)/shard_map/ppermute | solution.py:508
  30.7 0.7 %collective-permute-start.7 = (f32[16,4224]{1,0:T(8,128)S(1)}, f32[16,4224]{1,0:T(8,128)S(1)}, u32[]{:S(2)}, u32[]{:S(2)}) collective-permute-start(f32[16,4224]{1,0:T(8,128)S(1)} %pad_maximum_fusion.1), channel_id=1, source_target_pairs={{1,2},{2,1},{3,4},{4,3},{5,6},{6,5},{7,8},{8,7},{9,10},{10,9},{11,... | collective-permute-start | bytes 811016 | tf_op jit(solution)/shard_map/ppermute | solution.py:508
  31.4 1.7 %shard_map.91 = (f32[16,4096]{1,0:T(8,128)S(1)}, f32[16,128]{1,0:T(8,128)S(1)}) custom-call(s32[8,128]{1,0:T(8,128)S(1)} %get-tuple-element.26.pairs_ref, f32[16,4096]{1,0:T(8,128)S(1)} %get-tuple-element.40.payload_ref, f32[16,640]{1,0:T(8,128)S(1)} %collective-permute-done.6.beside_ref.partner_ref, bf16[16,512,256]{2,1,0:T(8,128)(2,1)S(1)} %get-tuple-element.42.own_ref, ...), custom_call_target="tpu_custom_call" | custom-call | flops 4000000000 | bytes 28800000 | tf_op jit(solution)/shard_map/pallas_call | solution.py:478
  33.1 2.0 %collective-permute-done.9.far_pair_ref = f32[16,1280]{1,0:T(8,128)S(1)} collective-permute-done((f32[16,1280]{1,0:T(8,128)S(1)}, f32[16,1280]{1,0:T(8,128)S(1)}, u32[]{:S(2)}, u32[]{:S(2)}) %collective-permute-start.9) | collective-permute-done | bytes 81952 | tf_op jit(solution)/shard_map/ppermute | solution.py:508
  35.1 1.6 %collective-permute-done.8.near_pair_ref = f32[16,1280]{1,0:T(8,128)S(1)} collective-permute-done((f32[16,1280]{1,0:T(8,128)S(1)}, f32[16,1280]{1,0:T(8,128)S(1)}, u32[]{:S(2)}, u32[]{:S(2)}) %collective-permute-start.8) | collective-permute-done | bytes 81952 | tf_op jit(solution)/shard_map/ppermute | solution.py:508
  36.7 2.1 %collective-permute-start.10 = (f32[16,2688]{1,0:T(8,128)S(1)}, f32[16,2688]{1,0:T(8,128)S(1)}, u32[]{:S(2)}, u32[]{:S(2)}) collective-permute-start(f32[16,2688]{1,0:T(8,128)S(1)} %pad_maximum_fusion.3), channel_id=1, source_target_pairs={{0,1},{1,0},{2,3},{3,2},{4,5},{5,4},{6,7},{7,6},{8,9},{9,8},{10,11... | collective-permute-start | bytes 516104 | tf_op jit(solution)/shard_map/ppermute | solution.py:508
  38.8 0.0 collective-permute-done.11.payload_ref
  38.8 1.3 %shard_map.92.near_ref = f32[16,4096]{1,0:T(8,128)S(1)} custom-call(s32[8,128]{1,0:T(8,128)S(1)} %get-tuple-element.26.pairs_ref, f32[16,4096]{1,0:T(8,128)S(1)} %collective-permute-done.11.payload_ref, f32[16,4096]{1,0:T(8,128)S(1)} %get-tuple-element.45.start_ref, bf16[12,4,512,256]{3,2,1,0:T(8,128)(2,1)S(1)} %get-tuple-element.46.kept_ref), custom_call_target="tpu_custom_call" | custom-call | flops 2000000000 | bytes 14400000 | tf_op jit(solution)/shard_map/pallas_call | solution.py:478
  40.1 0.0 collective-permute-done.10.swapped_ref
  40.1 0.3 shard_map.94.one_ref
  40.4 0.0 collective-permute-start.12
  40.5 2.1 %shard_map.93.start_ref = f32[16,4096]{1,0:T(8,128)S(1)} custom-call(s32[16,32]{1,0:T(8,128)S(1)} %get-tuple-element.30.at_ref, f32[16,1280]{1,0:T(8,128)S(1)} %collective-permute-done.8.near_pair_ref, f32[16,1280]{1,0:T(8,128)S(1)} %collective-permute-done.9.far_pair_ref, f32[16,2688]{1,0:T(8,128)S(1)} %collective-permute-done.10.swapped_ref, ...), custom_call_target="tpu_custom_call" | custom-call | flops 2000000000 | bytes 14400000 | tf_op jit(solution)/shard_map/pallas_call | solution.py:478
  42.6 2.4 %collective-permute-done.12.two_ref = f32[16,128]{1,0:T(8,128)S(1)} collective-permute-done((f32[16,128]{1,0:T(8,128)S(1)}, f32[16,128]{1,0:T(8,128)S(1)}, u32[]{:S(2)}, u32[]{:S(2)}) %collective-permute-start.12) | collective-permute-done | bytes 8224 | tf_op jit(solution)/shard_map/ppermute | solution.py:508
  45.0 0.0 collective-permute-done.7.payload_ref
  45.0 1.8 %shard_map.95 = (f32[16,4096]{1,0:T(8,128)}, f32[16,4096]{1,0:T(8,128)}) custom-call(s32[8,128]{1,0:T(8,128)S(1)} %get-tuple-element.26.pairs_ref, f32[16,4224]{1,0:T(8,128)S(1)} %collective-permute-done.7.payload_ref, f32[16,4096]{1,0:T(8,128)S(1)} %shard_map.93.start_ref, bf16[12,4,512,256]{3,2,1,0:T(8,128)(2,1)S(1)} %get-tuple-element.48.kept_ref, ...), custom_call_target="tpu_custom_call" | custom-call | flops 1500000000 | bytes 10800000 | tf_op jit(solution)/shard_map/pallas_call | solution.py:478
  (10 shorter events, 0.1 us)
Async XLA Ops:
  2.4 1.4 %collective-permute-start = (f32[16,768]{1,0:T(8,128)S(1)}, f32[16,768]{1,0:T(8,128)S(1)}, u32[]{:S(2)}, u32[]{:S(2)}) collective-permute-start(f32[16,768]{1,0:T(8,128)S(1)} %get-tuple-element.28), channel_id=1, source_target_pairs={{0,1},{1,0},{2,3},{3,2},{4,5},{5,4},{6,7},{7,6},{8,9},{9,8},{10,11... | collective-permute-start | bytes 147464 | tf_op jit(solution)/shard_map/ppermute | solution.py:508
  3.0 12.2 %collective-permute-start.5 = (f32[16,4864]{1,0:T(8,128)S(1)}, f32[16,4864]{1,0:T(8,128)S(1)}, u32[]{:S(2)}, u32[]{:S(2)}) collective-permute-start(f32[16,4864]{1,0:T(8,128)S(1)} %get-tuple-element.27.payload_ref), channel_id=1, source_target_pairs={{0,1},{1,0},{2,3},{3,2},{4,5},{5,4},{6,7},{7,6},{8,9},{9,8},{10,11... | collective-permute-start | bytes 933896 | tf_op jit(solution)/shard_map/ppermute | solution.py:508
  3.9 8.5 %collective-permute-start.3 = (f32[16,1536]{1,0:T(8,128)S(1)}, f32[16,1536]{1,0:T(8,128)S(1)}, u32[]{:S(2)}, u32[]{:S(2)}) collective-permute-start(f32[16,1536]{1,0:T(8,128)S(1)} %constant_dynamic-update-slice_fusion), channel_id=1, source_target_pairs={{0,4},{1,13},{2,6},{3,15},{4,8},{5,1},{6,10},{7,3},{8,12},{9,5},{1... | collective-permute-start | bytes 294920 | tf_op jit(solution)/shard_map/ppermute | solution.py:508
  6.8 7.3 %collective-permute-start.2 = (f32[16,1536]{1,0:T(8,128)S(1)}, f32[16,1536]{1,0:T(8,128)S(1)}, u32[]{:S(2)}, u32[]{:S(2)}) collective-permute-start(f32[16,1536]{1,0:T(8,128)S(1)} %constant_dynamic-update-slice_fusion), channel_id=1, source_target_pairs={{0,2},{1,15},{2,4},{3,1},{4,6},{5,3},{6,8},{7,5},{8,10},{9,7},{10,... | collective-permute-start | bytes 294920 | tf_op jit(solution)/shard_map/ppermute | solution.py:508
  14.1 3.1 %collective-permute-start.4 = (f32[16,3200]{1,0:T(8,128)S(1)}, f32[16,3200]{1,0:T(8,128)S(1)}, u32[]{:S(2)}, u32[]{:S(2)}) collective-permute-start(f32[16,3200]{1,0:T(8,128)S(1)} %pad_maximum_fusion.2), channel_id=1, source_target_pairs={{0,1},{1,0},{2,3},{3,2},{4,5},{5,4},{6,7},{7,6},{8,9},{9,8},{10,11... | collective-permute-start | bytes 614408 | tf_op jit(solution)/shard_map/ppermute | solution.py:508
  14.4 6.0 %collective-permute-start.1 = (f32[16,4992]{1,0:T(8,128)S(1)}, f32[16,4992]{1,0:T(8,128)S(1)}, u32[]{:S(2)}, u32[]{:S(2)}) collective-permute-start(f32[16,4992]{1,0:T(8,128)S(1)} %pad_maximum_fusion), channel_id=1, source_target_pairs={{1,2},{2,1},{3,4},{4,3},{5,6},{6,5},{7,8},{8,7},{9,10},{10,9},{11,... | collective-permute-start | bytes 958472 | tf_op jit(solution)/shard_map/ppermute | solution.py:508
  21.8 5.7 %collective-permute-start.6 = (f32[16,640]{1,0:T(8,128)S(1)}, f32[16,640]{1,0:T(8,128)S(1)}, u32[]{:S(2)}, u32[]{:S(2)}) collective-permute-start(f32[16,640]{1,0:T(8,128)S(1)} %get-tuple-element.41.payload_ref), channel_id=1, source_target_pairs={{0,1},{1,0},{2,3},{3,2},{4,5},{5,4},{6,7},{7,6},{8,9},{9,8},{10,11... | collective-permute-start | bytes 122888 | tf_op jit(solution)/shard_map/ppermute | solution.py:508
  26.7 12.1 %collective-permute-start.11 = (f32[16,4096]{1,0:T(8,128)S(1)}, f32[16,4096]{1,0:T(8,128)S(1)}, u32[]{:S(2)}, u32[]{:S(2)}) collective-permute-start(f32[16,4096]{1,0:T(8,128)S(1)} %get-tuple-element.40.payload_ref), channel_id=1, source_target_pairs={{0,1},{1,0},{2,3},{3,2},{4,5},{5,4},{6,7},{7,6},{8,9},{9,8},{10,11... | collective-permute-start | bytes 786440 | tf_op jit(solution)/shard_map/ppermute | solution.py:508
  27.5 7.6 %collective-permute-start.9 = (f32[16,1280]{1,0:T(8,128)S(1)}, f32[16,1280]{1,0:T(8,128)S(1)}, u32[]{:S(2)}, u32[]{:S(2)}) collective-permute-start(f32[16,1280]{1,0:T(8,128)S(1)} %constant_dynamic-update-slice_fusion.2), channel_id=1, source_target_pairs={{0,4},{1,13},{2,6},{3,15},{4,8},{5,1},{6,10},{7,3},{8,12},{9,5},{1... | collective-permute-start | bytes 245768 | tf_op jit(solution)/shard_map/ppermute | solution.py:508
  29.2 7.5 %collective-permute-start.8 = (f32[16,1280]{1,0:T(8,128)S(1)}, f32[16,1280]{1,0:T(8,128)S(1)}, u32[]{:S(2)}, u32[]{:S(2)}) collective-permute-start(f32[16,1280]{1,0:T(8,128)S(1)} %constant_dynamic-update-slice_fusion.2), channel_id=1, source_target_pairs={{0,2},{1,15},{2,4},{3,1},{4,6},{5,3},{6,8},{7,5},{8,10},{9,7},{10,... | collective-permute-start | bytes 245768 | tf_op jit(solution)/shard_map/ppermute | solution.py:508
  30.7 14.3 %collective-permute-start.7 = (f32[16,4224]{1,0:T(8,128)S(1)}, f32[16,4224]{1,0:T(8,128)S(1)}, u32[]{:S(2)}, u32[]{:S(2)}) collective-permute-start(f32[16,4224]{1,0:T(8,128)S(1)} %pad_maximum_fusion.1), channel_id=1, source_target_pairs={{1,2},{2,1},{3,4},{4,3},{5,6},{6,5},{7,8},{8,7},{9,10},{10,9},{11,... | collective-permute-start | bytes 811016 | tf_op jit(solution)/shard_map/ppermute | solution.py:508
  36.7 3.4 %collective-permute-start.10 = (f32[16,2688]{1,0:T(8,128)S(1)}, f32[16,2688]{1,0:T(8,128)S(1)}, u32[]{:S(2)}, u32[]{:S(2)}) collective-permute-start(f32[16,2688]{1,0:T(8,128)S(1)} %pad_maximum_fusion.3), channel_id=1, source_target_pairs={{0,1},{1,0},{2,3},{3,2},{4,5},{5,4},{6,7},{7,6},{8,9},{9,8},{10,11... | collective-permute-start | bytes 516104 | tf_op jit(solution)/shard_map/ppermute | solution.py:508
  40.4 4.6 %collective-permute-start.12 = (f32[16,128]{1,0:T(8,128)S(1)}, f32[16,128]{1,0:T(8,128)S(1)}, u32[]{:S(2)}, u32[]{:S(2)}) collective-permute-start(f32[16,128]{1,0:T(8,128)S(1)} %shard_map.94.one_ref), channel_id=1, source_target_pairs={{0,8},{1,9},{2,10},{3,11},{4,12},{5,13},{6,14},{7,15},{8,0},{9,1},... | collective-permute-start | bytes 24584 | tf_op jit(solution)/shard_map/ppermute | solution.py:508

commit v6 on v5

--- a/solution.py
+++ b/solution.py
@@ -392,12 +392,13 @@
 
 def far_fields(gathered_ref, coupling_ref, fields_ref):
     for c in range(gathered_ref.shape[0]):
-        field = quartered(dot_nt(gathered_ref[c], coupling_ref[c]))
-        fields_ref[c] = stacked(jnp.concatenate([field, field], axis=1))
+        field = quartered(dot_nt(coupling_ref[c], gathered_ref[c]))
+        field = jnp.concatenate(split(field), axis=1)
+        fields_ref[c] = jnp.concatenate([field, field], axis=0)
 
 
 def far_potential(fields_ref, c, basis):
-    return folded(dot_nn(fields_ref[c], basis))
+    return folded(dot_tn(fields_ref[c], basis))
 
 
 def far_kernel(cl, rank, at_ref, near_pair_ref, far_pair_ref, swapped_ref, center_ref, near_ref, basis_ref, offsets_ref,
@@ -514,8 +515,8 @@
         beside = move(table, pairing)
         pair = jnp.concatenate([table, beside], axis=1)
         near_pair, far_pair = outward(pair, 2), outward(pair, 4)
-        last = move(jnp.concatenate([payload, beside[:, beside.shape[1] - LANES:]], axis=1), bridging)
-        return beside, near_pair, far_pair, last, move(payload, pairing)
+        sent = jnp.concatenate([payload, beside[:, beside.shape[1] - LANES:]], axis=1)
+        return sent, beside, near_pair, far_pair, move(sent, bridging), move(payload, pairing)
 
     def swapped(near_pair, far_pair, tail):
         return move(jnp.concatenate([near_pair, far_pair, tail], axis=1), pairing)
@@ -541,7 +542,7 @@
         position, vertices, panel_vertices, krylov, basis, far_pairs, near_pairs.T, offsets,
         us=1.5,
     )
-    beside, near_pair, far_pair, other, partner = exchange(payload, table)
+    sent, beside, near_pair, far_pair, other, partner = exchange(payload, table)
     group = 4
     own = ((clusters, 2 * cl, cl), BF16)
     kept = ((clusters * (slots - 1) // group, group, 2 * cl, cl), BF16)
@@ -554,7 +555,7 @@
         [own, kept, whole, ((clusters, FEATURES, cl), BF16), sums_shape],
         [pieces, sources, total],
         "svv>ppvpv",
-        pairs, payload, beside,
+        pairs, sent, beside,
         us=8.0,
     )
     swap = swapped(near_pair, far_pair, tail)
@@ -564,19 +565,19 @@
         [pieces, sources, total],
         "svpv>pv",
         pairs, partner, targets, near,
-        us=4.0,
+        us=0.2,
     )
     tiles = 6 * per * span // LANES
     window = pltpu.VMEM((tiles, 2 * rhs, LANES), BF16)
     gathered = pltpu.VMEM((clusters, 2 * rhs, partners * rank), BF16)
-    fields = pltpu.VMEM((clusters, 2 * rhs, 2 * rank), BF16)
+    fields = pltpu.VMEM((clusters, 2 * rank, 2 * rhs), BF16)
     near, coupling = call(
         functools.partial(far_kernel, cl, rank),
         [whole, ((clusters, 2 * rank, partners * rank), BF16)],
         [window, pltpu.VMEM((tiles, 8, LANES), F32), gathered, fields],
         "svvvvvpp>vp",
         at, near_pair, far_pair, swap, centers, near, basis, offsets,
-        us=4.0,
+        us=0.2,
     )
     blocks_other, image, payload, table = call(
         functools.partial(image_kernel, cl, rank),
@@ -586,13 +587,13 @@
         pairs, other, targets, near, area, krylov, basis,
         us=4.0,
     )
-    beside, near_pair, far_pair, other, partner = exchange(payload, table)
+    sent, beside, near_pair, far_pair, other, partner = exchange(payload, table)
     near, tail = call(
         functools.partial(own_again_kernel, cl),
         [whole, sums_shape],
         [pieces, total],
         "svvpp>vv",
-        pairs, payload, beside, own_blocks, blocks,
+        pairs, sent, beside, own_blocks, blocks,
         us=8.0,
     )
     swap = swapped(near_pair, far_pair, tail)

time: 46.6 us -> 43 us (0.923); the launches traced: 46.8 us -> 42.7 us
  waiting for transfers between devices: 10.7 us -> 5.59 us
  Pallas kernels: 18.4 us -> 20.5 us
  starting transfers between devices: 16.9 us -> 15.8 us
    ppermute x13, waiting for transfers between devices: 10.7 us -> 5.59 us  [move(): return lax.ppermute(value, 'clus', pairs)]
    pallas_call x10, Pallas kernels: 18.4 us -> 20.5 us  [call(): pl.pallas_call(kernel, out_shape=[pltpu.VMEM(*out) if m == 'p' else jax.S...]
    ppermute x13, starting transfers between devices: 16.9 us -> 15.8 us  [move(): return lax.ppermute(value, 'clus', pairs)]
  transfers between devices with their start and end apart: 13 -> 13, of which waited for: 7 -> 5; matrix products, arithmetic and copies ran while one was open for 0% -> 0% of each run, Pallas kernels for 29% -> 36%
where the time goes in v6:
time: 43 us; the launch traced here: 42.7 us
  Pallas kernels  20.5 us (48%)
  starting transfers between devices  15.8 us (37%)
  waiting for transfers between devices  5.59 us (13%)
  between operations  0.75 us (2%)
    pallas_call x10, Pallas kernels, call(): pl.pallas_call(kernel, out_shape=[pltpu.VMEM(*out) if m == 'p' else jax.S...  20.5 us
    ppermute x13, starting transfers between devices, move(): return lax.ppermute(value, 'clus', pairs)  15.8 us
    ppermute x13, waiting for transfers between devices, move(): return lax.ppermute(value, 'clus', pairs)  5.59 us
  transfers between devices with their start and end apart: 13, of which 5 were waited for; matrix products, arithmetic and copies ran while one was open for 0% of the time, Pallas kernels for 36%

profile of v6, /device:TPU:0, one launch (start us, length us, event | category | flops | bytes accessed | tf_op | source)
XLA Modules:
  0.0 42.7 jit_solution(12239729702610265198)
XLA Ops:
  0.6 1.8 %shard_map.86 = (f32[16,4864]{1,0:T(8,128)S(1)}, f32[16,768]{1,0:T(8,128)S(1)}, f32[16,256]{1,0:T(8,128)S(1)}, f32[16,384]{1,0:T(8,128)S(1)}, s32[16,32]{1,0:T(8...) custom-call(s32[1]{0:T(128)} %bitcast.position_ref, ...), custom_call_target="tpu_custom_call" | custom-call | flops 750000000 | bytes 5400000 | tf_op jit(solution)/shard_map/pallas_call | solution.py:479
  2.4 0.5 %collective-permute-start = (f32[16,768]{1,0:T(8,128)S(1)}, f32[16,768]{1,0:T(8,128)S(1)}, u32[]{:S(2)}, u32[]{:S(2)}) collective-permute-start(f32[16,768]{1,0:T(8,128)S(1)} %get-tuple-element.28), channel_id=1, source_target_pairs={{0,1},{1,0},{2,3},{3,2},{4,5},{5,4},{6,7},{7,6},{8,9},{9,8},{10,11... | collective-permute-start | bytes 147464 | tf_op jit(solution)/shard_map/ppermute | solution.py:509
  3.0 0.1 collective-permute-start.5
  3.0 0.8 %collective-permute-done.beside_ref = f32[16,768]{1,0:T(8,128)S(1)} collective-permute-done((f32[16,768]{1,0:T(8,128)S(1)}, f32[16,768]{1,0:T(8,128)S(1)}, u32[]{:S(2)}, u32[]{:S(2)}) %collective-permute-start) | collective-permute-done | bytes 49184 | tf_op jit(solution)/shard_map/ppermute | solution.py:509
  3.9 2.9 %collective-permute-start.3 = (f32[16,1536]{1,0:T(8,128)S(1)}, f32[16,1536]{1,0:T(8,128)S(1)}, u32[]{:S(2)}, u32[]{:S(2)}) collective-permute-start(f32[16,1536]{1,0:T(8,128)S(1)} %constant_dynamic-update-slice_fusion), channel_id=1, source_target_pairs={{0,4},{1,13},{2,6},{3,15},{4,8},{5,1},{6,10},{7,3},{8,12},{9,5},{1... | collective-permute-start | bytes 294920 | tf_op jit(solution)/shard_map/ppermute | solution.py:509
  6.8 1.5 %collective-permute-start.2 = (f32[16,1536]{1,0:T(8,128)S(1)}, f32[16,1536]{1,0:T(8,128)S(1)}, u32[]{:S(2)}, u32[]{:S(2)}) collective-permute-start(f32[16,1536]{1,0:T(8,128)S(1)} %constant_dynamic-update-slice_fusion), channel_id=1, source_target_pairs={{0,2},{1,15},{2,4},{3,1},{4,6},{5,3},{6,8},{7,5},{8,10},{9,7},{10,... | collective-permute-start | bytes 294920 | tf_op jit(solution)/shard_map/ppermute | solution.py:509
  8.3 0.7 %collective-permute-start.1 = (f32[16,4992]{1,0:T(8,128)S(1)}, f32[16,4992]{1,0:T(8,128)S(1)}, u32[]{:S(2)}, u32[]{:S(2)}) collective-permute-start(f32[16,4992]{1,0:T(8,128)S(1)} %pad_maximum_fusion.payload_ref), channel_id=1, source_target_pairs={{1,2},{2,1},{3,4},{4,3},{5,6},{6,5},{7,8},{8,7},{9,10},{10,9},{11,... | collective-permute-start | bytes 958472 | tf_op jit(solution)/shard_map/ppermute | solution.py:509
  9.0 3.9 %shard_map.87 = (bf16[16,512,256]{2,1,0:T(8,128)(2,1)S(1)}, bf16[12,4,512,256]{3,2,1,0:T(8,128)(2,1)S(1)}, f32[16,4096]{1,0:T(8,128)S(1)}, bf16[16,80,256]{2,1,0:T(8,128)(2,1)S(1)}, f32[16,128]{1,0:T(8,128)S(1)}) custom-call(s32[8,128]{1,0:T(8,128)S(1)} %get-tuple-element.26.pairs_ref, f32[16,4992]{1,0:T(8,128)S(1)} %pad_maximum_fusion.payload_ref, ...), custom_call_target="tpu_custom_call" | custom-call | flops 4000000000 | bytes 28800000 | tf_op jit(solution)/shard_map/pallas_call | solution.py:479
  12.9 0.0 collective-permute-done.3.far_pair_ref
  12.9 1.2 %collective-permute-done.2.near_pair_ref = f32[16,1536]{1,0:T(8,128)S(1)} collective-permute-done((f32[16,1536]{1,0:T(8,128)S(1)}, f32[16,1536]{1,0:T(8,128)S(1)}, u32[]{:S(2)}, u32[]{:S(2)}) %collective-permute-start.2) | collective-permute-done | bytes 98336 | tf_op jit(solution)/shard_map/ppermute | solution.py:509
  14.1 1.8 %collective-permute-start.4 = (f32[16,3200]{1,0:T(8,128)S(1)}, f32[16,3200]{1,0:T(8,128)S(1)}, u32[]{:S(2)}, u32[]{:S(2)}) collective-permute-start(f32[16,3200]{1,0:T(8,128)S(1)} %pad_maximum_fusion.2), channel_id=1, source_target_pairs={{0,1},{1,0},{2,3},{3,2},{4,5},{5,4},{6,7},{7,6},{8,9},{9,8},{10,11... | collective-permute-start | bytes 614408 | tf_op jit(solution)/shard_map/ppermute | solution.py:509
  15.9 0.0 collective-permute-done.5.payload_ref
  15.9 2.1 %shard_map.88 = (bf16[12,4,512,256]{3,2,1,0:T(8,128)(2,1)S(1)}, f32[16,4096]{1,0:T(8,128)S(1)}) custom-call(s32[8,128]{1,0:T(8,128)S(1)} %get-tuple-element.26.pairs_ref, f32[16,4864]{1,0:T(8,128)S(1)} %collective-permute-done.5.payload_ref, bf16[16,80,256]{2,1,0:T(8,128)(2,1)S(1)} %get-tuple-element.29.targets_ref, f32[16,4096]{1,0:T(8,128)S(1)} %get-tuple-element.33.start_ref), custom_call_target="tpu_custom_call" | custom-call | flops 100000000 | bytes 720000 | tf_op jit(solution)/shard_map/pallas_call | solution.py:479
  18.0 0.0 collective-permute-done.4.swapped_ref
  18.0 3.4 %shard_map.89 = (f32[16,4096]{1,0:T(8,128)S(1)}, bf16[16,64,1024]{2,1,0:T(8,128)(2,1)S(1)}) custom-call(s32[16,32]{1,0:T(8,128)S(1)} %get-tuple-element.30.at_ref, f32[16,1536]{1,0:T(8,128)S(1)} %collective-permute-done.2.near_pair_ref, f32[16,1536]{1,0:T(8,128)S(1)} %collective-permute-done.3.far_pair_ref, ...), custom_call_target="tpu_custom_call" | custom-call | flops 100000000 | bytes 720000 | tf_op jit(solution)/shard_map/pallas_call | solution.py:479
  21.4 0.0 collective-permute-done.1.payload_ref
  21.4 1.3 %shard_map.90 = (bf16[12,4,512,256]{3,2,1,0:T(8,128)(2,1)S(1)}, f32[16,4096]{1,0:T(8,128)S(1)}, f32[16,4096]{1,0:T(8,128)S(1)}, f32[16,640]{1,0:T(8,128)S(1)}) custom-call(s32[8,128]{1,0:T(8,128)S(1)} %get-tuple-element.26.pairs_ref, f32[16,4992]{1,0:T(8,128)S(1)} %collective-permute-done.1.payload_ref, ...), custom_call_target="tpu_custom_call" | custom-call | flops 2000000000 | bytes 14400000 | tf_op jit(solution)/shard_map/pallas_call | solution.py:479
  22.7 1.9 %collective-permute-start.6 = (f32[16,640]{1,0:T(8,128)S(1)}, f32[16,640]{1,0:T(8,128)S(1)}, u32[]{:S(2)}, u32[]{:S(2)}) collective-permute-start(f32[16,640]{1,0:T(8,128)S(1)} %get-tuple-element.41.payload_ref), channel_id=1, source_target_pairs={{0,1},{1,0},{2,3},{3,2},{4,5},{5,4},{6,7},{7,6},{8,9},{9,8},{10,11... | collective-permute-start | bytes 122888 | tf_op jit(solution)/shard_map/ppermute | solution.py:509
  24.6 0.1 collective-permute-start.11
  24.7 0.8 %collective-permute-done.6.beside_ref.partner_ref = f32[16,640]{1,0:T(8,128)S(1)} collective-permute-done((f32[16,640]{1,0:T(8,128)S(1)}, f32[16,640]{1,0:T(8,128)S(1)}, u32[]{:S(2)}, u32[]{:S(2)}) %collective-permute-start.6) | collective-permute-done | bytes 40992 | tf_op jit(solution)/shard_map/ppermute | solution.py:509
  25.5 0.0 collective-permute-start.9
  25.5 4.2 %collective-permute-start.8 = (f32[16,1280]{1,0:T(8,128)S(1)}, f32[16,1280]{1,0:T(8,128)S(1)}, u32[]{:S(2)}, u32[]{:S(2)}) collective-permute-start(f32[16,1280]{1,0:T(8,128)S(1)} %constant_dynamic-update-slice_fusion.2), channel_id=1, source_target_pairs={{0,2},{1,15},{2,4},{3,1},{4,6},{5,3},{6,8},{7,5},{8,10},{9,7},{10,... | collective-permute-start | bytes 245768 | tf_op jit(solution)/shard_map/ppermute | solution.py:509
  29.7 0.7 %collective-permute-start.7 = (f32[16,4224]{1,0:T(8,128)S(1)}, f32[16,4224]{1,0:T(8,128)S(1)}, u32[]{:S(2)}, u32[]{:S(2)}) collective-permute-start(f32[16,4224]{1,0:T(8,128)S(1)} %pad_maximum_fusion.1.payload_ref), channel_id=1, source_target_pairs={{1,2},{2,1},{3,4},{4,3},{5,6},{6,5},{7,8},{8,7},{9,10},{10,9},{11,... | collective-permute-start | bytes 811016 | tf_op jit(solution)/shard_map/ppermute | solution.py:509
  30.3 2.4 %shard_map.91 = (f32[16,4096]{1,0:T(8,128)S(1)}, f32[16,128]{1,0:T(8,128)S(1)}) custom-call(s32[8,128]{1,0:T(8,128)S(1)} %get-tuple-element.26.pairs_ref, f32[16,4224]{1,0:T(8,128)S(1)} %pad_maximum_fusion.1.payload_ref, f32[16,640]{1,0:T(8,128)S(1)} %collective-permute-done.6.beside_ref.partner_ref, bf16[16,512,256]{2,1,0:T(8,128)(2,1)S(1)} %get-tuple-element.42.own_ref, ...), custom_call_target="tpu_custom_call" | custom-call | flops 4000000000 | bytes 28800000 | tf_op jit(solution)/shard_map/pallas_call | solution.py:479
  32.7 0.0 collective-permute-done.9.far_pair_ref
  32.7 1.1 %collective-permute-done.8.near_pair_ref = f32[16,1280]{1,0:T(8,128)S(1)} collective-permute-done((f32[16,1280]{1,0:T(8,128)S(1)}, f32[16,1280]{1,0:T(8,128)S(1)}, u32[]{:S(2)}, u32[]{:S(2)}) %collective-permute-start.8) | collective-permute-done | bytes 81952 | tf_op jit(solution)/shard_map/ppermute | solution.py:509
  33.8 0.9 %collective-permute-start.10 = (f32[16,2688]{1,0:T(8,128)S(1)}, f32[16,2688]{1,0:T(8,128)S(1)}, u32[]{:S(2)}, u32[]{:S(2)}) collective-permute-start(f32[16,2688]{1,0:T(8,128)S(1)} %pad_maximum_fusion.3), channel_id=1, source_target_pairs={{0,1},{1,0},{2,3},{3,2},{4,5},{5,4},{6,7},{7,6},{8,9},{9,8},{10,11... | collective-permute-start | bytes 516104 | tf_op jit(solution)/shard_map/ppermute | solution.py:509
  34.7 0.0 collective-permute-done.11.payload_ref
  34.7 1.3 %shard_map.92.near_ref = f32[16,4096]{1,0:T(8,128)S(1)} custom-call(s32[8,128]{1,0:T(8,128)S(1)} %get-tuple-element.26.pairs_ref, f32[16,4096]{1,0:T(8,128)S(1)} %collective-permute-done.11.payload_ref, f32[16,4096]{1,0:T(8,128)S(1)} %get-tuple-element.45.start_ref, bf16[12,4,512,256]{3,2,1,0:T(8,128)(2,1)S(1)} %get-tuple-element.46.kept_ref), custom_call_target="tpu_custom_call" | custom-call | flops 2000000000 | bytes 14400000 | tf_op jit(solution)/shard_map/pallas_call | solution.py:479
  36.0 0.0 collective-permute-done.10.swapped_ref
  36.0 0.3 shard_map.94.one_ref
  36.3 0.6 %collective-permute-start.12 = (f32[16,128]{1,0:T(8,128)S(1)}, f32[16,128]{1,0:T(8,128)S(1)}, u32[]{:S(2)}, u32[]{:S(2)}) collective-permute-start(f32[16,128]{1,0:T(8,128)S(1)} %shard_map.94.one_ref), channel_id=1, source_target_pairs={{0,8},{1,9},{2,10},{3,11},{4,12},{5,13},{6,14},{7,15},{8,0},{9,1},... | collective-permute-start | bytes 24584 | tf_op jit(solution)/shard_map/ppermute | solution.py:509
  36.9 2.2 %shard_map.93.start_ref = f32[16,4096]{1,0:T(8,128)S(1)} custom-call(s32[16,32]{1,0:T(8,128)S(1)} %get-tuple-element.30.at_ref, f32[16,1280]{1,0:T(8,128)S(1)} %collective-permute-done.8.near_pair_ref, f32[16,1280]{1,0:T(8,128)S(1)} %collective-permute-done.9.far_pair_ref, f32[16,2688]{1,0:T(8,128)S(1)} %collective-permute-done.10.swapped_ref, ...), custom_call_target="tpu_custom_call" | custom-call | flops 2000000000 | bytes 14400000 | tf_op jit(solution)/shard_map/pallas_call | solution.py:479
  39.1 1.7 %collective-permute-done.12.two_ref = f32[16,128]{1,0:T(8,128)S(1)} collective-permute-done((f32[16,128]{1,0:T(8,128)S(1)}, f32[16,128]{1,0:T(8,128)S(1)}, u32[]{:S(2)}, u32[]{:S(2)}) %collective-permute-start.12) | collective-permute-done | bytes 8224 | tf_op jit(solution)/shard_map/ppermute | solution.py:509
  40.9 0.0 collective-permute-done.7.payload_ref
  40.9 1.8 %shard_map.95 = (f32[16,4096]{1,0:T(8,128)}, f32[16,4096]{1,0:T(8,128)}) custom-call(s32[8,128]{1,0:T(8,128)S(1)} %get-tuple-element.26.pairs_ref, f32[16,4224]{1,0:T(8,128)S(1)} %collective-permute-done.7.payload_ref, f32[16,4096]{1,0:T(8,128)S(1)} %shard_map.93.start_ref, bf16[12,4,512,256]{3,2,1,0:T(8,128)(2,1)S(1)} %get-tuple-element.48.kept_ref, ...), custom_call_target="tpu_custom_call" | custom-call | flops 1500000000 | bytes 10800000 | tf_op jit(solution)/shard_map/pallas_call | solution.py:479
  (10 shorter events, 0.1 us)
Async XLA Ops:
  2.4 1.4 %collective-permute-start = (f32[16,768]{1,0:T(8,128)S(1)}, f32[16,768]{1,0:T(8,128)S(1)}, u32[]{:S(2)}, u32[]{:S(2)}) collective-permute-start(f32[16,768]{1,0:T(8,128)S(1)} %get-tuple-element.28), channel_id=1, source_target_pairs={{0,1},{1,0},{2,3},{3,2},{4,5},{5,4},{6,7},{7,6},{8,9},{9,8},{10,11... | collective-permute-start | bytes 147464 | tf_op jit(solution)/shard_map/ppermute | solution.py:509
  3.0 12.9 %collective-permute-start.5 = (f32[16,4864]{1,0:T(8,128)S(1)}, f32[16,4864]{1,0:T(8,128)S(1)}, u32[]{:S(2)}, u32[]{:S(2)}) collective-permute-start(f32[16,4864]{1,0:T(8,128)S(1)} %get-tuple-element.27), channel_id=1, source_target_pairs={{0,1},{1,0},{2,3},{3,2},{4,5},{5,4},{6,7},{7,6},{8,9},{9,8},{10,11... | collective-permute-start | bytes 933896 | tf_op jit(solution)/shard_map/ppermute | solution.py:509
  3.9 9.0 %collective-permute-start.3 = (f32[16,1536]{1,0:T(8,128)S(1)}, f32[16,1536]{1,0:T(8,128)S(1)}, u32[]{:S(2)}, u32[]{:S(2)}) collective-permute-start(f32[16,1536]{1,0:T(8,128)S(1)} %constant_dynamic-update-slice_fusion), channel_id=1, source_target_pairs={{0,4},{1,13},{2,6},{3,15},{4,8},{5,1},{6,10},{7,3},{8,12},{9,5},{1... | collective-permute-start | bytes 294920 | tf_op jit(solution)/shard_map/ppermute | solution.py:509
  6.8 7.3 %collective-permute-start.2 = (f32[16,1536]{1,0:T(8,128)S(1)}, f32[16,1536]{1,0:T(8,128)S(1)}, u32[]{:S(2)}, u32[]{:S(2)}) collective-permute-start(f32[16,1536]{1,0:T(8,128)S(1)} %constant_dynamic-update-slice_fusion), channel_id=1, source_target_pairs={{0,2},{1,15},{2,4},{3,1},{4,6},{5,3},{6,8},{7,5},{8,10},{9,7},{10,... | collective-permute-start | bytes 294920 | tf_op jit(solution)/shard_map/ppermute | solution.py:509
  8.3 13.1 %collective-permute-start.1 = (f32[16,4992]{1,0:T(8,128)S(1)}, f32[16,4992]{1,0:T(8,128)S(1)}, u32[]{:S(2)}, u32[]{:S(2)}) collective-permute-start(f32[16,4992]{1,0:T(8,128)S(1)} %pad_maximum_fusion.payload_ref), channel_id=1, source_target_pairs={{1,2},{2,1},{3,4},{4,3},{5,6},{6,5},{7,8},{8,7},{9,10},{10,9},{11,... | collective-permute-start | bytes 958472 | tf_op jit(solution)/shard_map/ppermute | solution.py:509
  14.1 3.9 %collective-permute-start.4 = (f32[16,3200]{1,0:T(8,128)S(1)}, f32[16,3200]{1,0:T(8,128)S(1)}, u32[]{:S(2)}, u32[]{:S(2)}) collective-permute-start(f32[16,3200]{1,0:T(8,128)S(1)} %pad_maximum_fusion.2), channel_id=1, source_target_pairs={{0,1},{1,0},{2,3},{3,2},{4,5},{5,4},{6,7},{7,6},{8,9},{9,8},{10,11... | collective-permute-start | bytes 614408 | tf_op jit(solution)/shard_map/ppermute | solution.py:509
  22.7 2.7 %collective-permute-start.6 = (f32[16,640]{1,0:T(8,128)S(1)}, f32[16,640]{1,0:T(8,128)S(1)}, u32[]{:S(2)}, u32[]{:S(2)}) collective-permute-start(f32[16,640]{1,0:T(8,128)S(1)} %get-tuple-element.41.payload_ref), channel_id=1, source_target_pairs={{0,1},{1,0},{2,3},{3,2},{4,5},{5,4},{6,7},{7,6},{8,9},{9,8},{10,11... | collective-permute-start | bytes 122888 | tf_op jit(solution)/shard_map/ppermute | solution.py:509
  24.6 10.1 %collective-permute-start.11 = (f32[16,4096]{1,0:T(8,128)S(1)}, f32[16,4096]{1,0:T(8,128)S(1)}, u32[]{:S(2)}, u32[]{:S(2)}) collective-permute-start(f32[16,4096]{1,0:T(8,128)S(1)} %get-tuple-element.40), channel_id=1, source_target_pairs={{0,1},{1,0},{2,3},{3,2},{4,5},{5,4},{6,7},{7,6},{8,9},{9,8},{10,11... | collective-permute-start | bytes 786440 | tf_op jit(solution)/shard_map/ppermute | solution.py:509
  25.5 7.2 %collective-permute-start.9 = (f32[16,1280]{1,0:T(8,128)S(1)}, f32[16,1280]{1,0:T(8,128)S(1)}, u32[]{:S(2)}, u32[]{:S(2)}) collective-permute-start(f32[16,1280]{1,0:T(8,128)S(1)} %constant_dynamic-update-slice_fusion.2), channel_id=1, source_target_pairs={{0,4},{1,13},{2,6},{3,15},{4,8},{5,1},{6,10},{7,3},{8,12},{9,5},{1... | collective-permute-start | bytes 245768 | tf_op jit(solution)/shard_map/ppermute | solution.py:509
  25.5 8.3 %collective-permute-start.8 = (f32[16,1280]{1,0:T(8,128)S(1)}, f32[16,1280]{1,0:T(8,128)S(1)}, u32[]{:S(2)}, u32[]{:S(2)}) collective-permute-start(f32[16,1280]{1,0:T(8,128)S(1)} %constant_dynamic-update-slice_fusion.2), channel_id=1, source_target_pairs={{0,2},{1,15},{2,4},{3,1},{4,6},{5,3},{6,8},{7,5},{8,10},{9,7},{10,... | collective-permute-start | bytes 245768 | tf_op jit(solution)/shard_map/ppermute | solution.py:509
  29.7 11.2 %collective-permute-start.7 = (f32[16,4224]{1,0:T(8,128)S(1)}, f32[16,4224]{1,0:T(8,128)S(1)}, u32[]{:S(2)}, u32[]{:S(2)}) collective-permute-start(f32[16,4224]{1,0:T(8,128)S(1)} %pad_maximum_fusion.1.payload_ref), channel_id=1, source_target_pairs={{1,2},{2,1},{3,4},{4,3},{5,6},{6,5},{7,8},{8,7},{9,10},{10,9},{11,... | collective-permute-start | bytes 811016 | tf_op jit(solution)/shard_map/ppermute | solution.py:509
  33.8 2.2 %collective-permute-start.10 = (f32[16,2688]{1,0:T(8,128)S(1)}, f32[16,2688]{1,0:T(8,128)S(1)}, u32[]{:S(2)}, u32[]{:S(2)}) collective-permute-start(f32[16,2688]{1,0:T(8,128)S(1)} %pad_maximum_fusion.3), channel_id=1, source_target_pairs={{0,1},{1,0},{2,3},{3,2},{4,5},{5,4},{6,7},{7,6},{8,9},{9,8},{10,11... | collective-permute-start | bytes 516104 | tf_op jit(solution)/shard_map/ppermute | solution.py:509
  36.3 4.6 %collective-permute-start.12 = (f32[16,128]{1,0:T(8,128)S(1)}, f32[16,128]{1,0:T(8,128)S(1)}, u32[]{:S(2)}, u32[]{:S(2)}) collective-permute-start(f32[16,128]{1,0:T(8,128)S(1)} %shard_map.94.one_ref), channel_id=1, source_target_pairs={{0,8},{1,9},{2,10},{3,11},{4,12},{5,13},{6,14},{7,15},{8,0},{9,1},... | collective-permute-start | bytes 24584 | tf_op jit(solution)/shard_map/ppermute | solution.py:509

commit v7 on v6

--- a/solution.py
+++ b/solution.py
@@ -324,37 +324,32 @@
     put_total(cl, total_ref, None, near_out_ref)
 
 
-def partner_again_kernel(cl, pairs_ref, payload_ref, start_ref, kept_ref, near_out_ref, pieces_ref, total_ref):
+def neighbour_again_kernel(cl, which, pairs_ref, payload_ref, start_ref, kept_ref, near_out_ref, pieces_ref, total_ref):
     fill_charges(pieces_ref, payload_ref, near_out_ref.shape[1] // cl, cl)
     total_ref[...] = jnp.zeros_like(total_ref)
-    apply_list(1, pairs_ref, kept_ref, pieces_ref, total_ref, cl)
+    apply_list(which, pairs_ref, kept_ref, pieces_ref, total_ref, cl)
     put_total(cl, total_ref, start_ref, near_out_ref)
 
 
-def finish_kernel(cl, total, pairs_ref, payload_ref, start_ref, kept_ref, area_ref, image_ref, krylov_ref, one_ref, two_ref,
-                  next_hbm, second_hbm, pieces_ref, total_ref, next_ref, second_ref, sems):
+def finish_kernel(cl, total, near_ref, area_ref, image_ref, krylov_ref, one_ref, two_ref, next_hbm, second_hbm, next_ref, second_ref, sems):
     panels = image_ref.shape[1]
     clusters = panels // cl
     squared, correlation, energy, local = merged([one_ref[...], two_ref[...]])
     projection = correlation / (squared + 1e-06)
     gap = projection - local
     scaling = 1.0 / jnp.sqrt((energy + gap * gap * squared) / total + 1e-06)
-    for c in range(clusters):
-        lanes = slice(c * cl, (c + 1) * cl)
-        next_ref[:, lanes] = (image_ref[:, lanes] - projection * krylov_ref[:, lanes]) * scaling
-    moves = copies(((next_ref, next_hbm),), sems)
-    fill_charges(pieces_ref, payload_ref, clusters, cl)
-    total_ref[...] = jnp.zeros_like(total_ref)
-    apply_list(2, pairs_ref, kept_ref, pieces_ref, total_ref, cl)
-    parts = 2
+    moves = []
+    parts = 4
     for h in range(parts):
         for c in range(h * clusters // parts, (h + 1) * clusters // parts):
             lanes = slice(c * cl, (c + 1) * cl)
-            again = COULOMB * area_ref[c:c + 1, :] * (start_ref[:, lanes] + folded(total_ref[c]))
-            second_ref[:, lanes] = (again - projection * image_ref[:, lanes]) * scaling
+            image = image_ref[:, lanes]
+            next_ref[:, lanes] = (image - projection * krylov_ref[:, lanes]) * scaling
+            second_ref[:, lanes] = (COULOMB * area_ref[c:c + 1, :] * near_ref[:, lanes] - projection * image) * scaling
         lanes = slice(h * panels // parts, (h + 1) * panels // parts)
-        moves.append(pltpu.make_async_copy(second_ref.at[:, lanes], second_hbm.at[:, lanes], sems.at[1 + h]))
-        moves[-1].start()
+        for held, hbm in ((next_ref, next_hbm), (second_ref, second_hbm)):
+            moves.append(pltpu.make_async_copy(held.at[:, lanes], hbm.at[:, lanes], sems.at[len(moves)]))
+            moves[-1].start()
     for move in moves:
         move.wait()
 
@@ -598,7 +593,7 @@
     )
     swap = swapped(near_pair, far_pair, tail)
     (near,) = call(
-        functools.partial(partner_again_kernel, cl),
+        functools.partial(neighbour_again_kernel, cl, 1),
         [whole],
         [pieces, total],
         "svvp>v",
@@ -620,14 +615,22 @@
         at, near_pair, far_pair, swap, near, coupling, basis,
         us=4.0,
     )
+    (near,) = call(
+        functools.partial(neighbour_again_kernel, cl, 2),
+        [whole],
+        [pieces, total],
+        "svvp>v",
+        pairs, other, near, blocks_other,
+        us=1.5,
+    )
     here = pltpu.VMEM((rhs, panels), F32)
     return tuple(call(
         functools.partial(finish_kernel, cl, panels * devices),
         [whole, whole],
-        [pieces, total, here, here, pltpu.SemaphoreType.DMA((3,))],
-        "svvpvvpvv>hh",
-        pairs, other, near, blocks_other, area, image, krylov, one, many,
-        us=3.0,
+        [here, here, pltpu.SemaphoreType.DMA((8,))],
+        "vvvpvv>hh",
+        near, area, image, krylov, one, many,
+        us=1.0,
     ))
 
 

time: 43 us -> 42.6 us (level); the launches traced: 42.7 us -> 43.1 us
  starting transfers between devices: 15.8 us -> 10.5 us
  Pallas kernels: 20.5 us -> 23.3 us
  waiting for transfers between devices: 5.59 us -> 8.34 us
    ppermute x13, starting transfers between devices: 15.8 us -> 10.5 us  [move(): return lax.ppermute(value, 'clus', pairs)]
    pallas_call x10 -> x11, Pallas kernels: 20.5 us -> 23.3 us  [call(): pl.pallas_call(kernel, out_shape=[pltpu.VMEM(*out) if m == 'p' else jax.S...]
    ppermute x13, waiting for transfers between devices: 5.59 us -> 8.34 us  [move(): return lax.ppermute(value, 'clus', pairs)]
  transfers between devices with their start and end apart: 13 -> 13, of which waited for: 5 -> 6; matrix products, arithmetic and copies ran while one was open for 0% -> 0% of each run, Pallas kernels for 36% -> 44%
where the time goes in v7:
time: 42.6 us; the launch traced here: 43.1 us
  Pallas kernels  23.3 us (55%)
  starting transfers between devices  10.5 us (25%)
  waiting for transfers between devices  8.34 us (20%)
  between operations  0.79 us (2%)
    pallas_call x11, Pallas kernels, call(): pl.pallas_call(kernel, out_shape=[pltpu.VMEM(*out) if m == 'p' else jax.S...  23.3 us
    ppermute x13, starting transfers between devices, move(): return lax.ppermute(value, 'clus', pairs)  10.5 us
    ppermute x13, waiting for transfers between devices, move(): return lax.ppermute(value, 'clus', pairs)  8.34 us
  transfers between devices with their start and end apart: 13, of which 6 were waited for; matrix products, arithmetic and copies ran while one was open for 0% of the time, Pallas kernels for 44%

profile of v7, /device:TPU:0, one launch (start us, length us, event | category | flops | bytes accessed | tf_op | source)
XLA Modules:
  0.0 43.1 jit_solution(17319896768739893327)
XLA Ops:
  0.6 1.8 %shard_map.86 = (f32[16,4864]{1,0:T(8,128)S(1)}, f32[16,768]{1,0:T(8,128)S(1)}, f32[16,256]{1,0:T(8,128)S(1)}, f32[16,384]{1,0:T(8,128)S(1)}, s32[16,32]{1,0:T(8...) custom-call(s32[1]{0:T(128)} %bitcast.position_ref, ...), custom_call_target="tpu_custom_call" | custom-call | flops 750000000 | bytes 5400000 | tf_op jit(solution)/shard_map/pallas_call | solution.py:474
  2.4 0.5 %collective-permute-start = (f32[16,768]{1,0:T(8,128)S(1)}, f32[16,768]{1,0:T(8,128)S(1)}, u32[]{:S(2)}, u32[]{:S(2)}) collective-permute-start(f32[16,768]{1,0:T(8,128)S(1)} %get-tuple-element.28), channel_id=1, source_target_pairs={{0,1},{1,0},{2,3},{3,2},{4,5},{5,4},{6,7},{7,6},{8,9},{9,8},{10,11... | collective-permute-start | bytes 147464 | tf_op jit(solution)/shard_map/ppermute | solution.py:504
  3.0 0.1 collective-permute-start.5
  3.0 0.8 %collective-permute-done.beside_ref = f32[16,768]{1,0:T(8,128)S(1)} collective-permute-done((f32[16,768]{1,0:T(8,128)S(1)}, f32[16,768]{1,0:T(8,128)S(1)}, u32[]{:S(2)}, u32[]{:S(2)}) %collective-permute-start) | collective-permute-done | bytes 49184 | tf_op jit(solution)/shard_map/ppermute | solution.py:504
  3.8 2.9 %collective-permute-start.3 = (f32[16,1536]{1,0:T(8,128)S(1)}, f32[16,1536]{1,0:T(8,128)S(1)}, u32[]{:S(2)}, u32[]{:S(2)}) collective-permute-start(f32[16,1536]{1,0:T(8,128)S(1)} %constant_dynamic-update-slice_fusion), channel_id=1, source_target_pairs={{0,4},{1,13},{2,6},{3,15},{4,8},{5,1},{6,10},{7,3},{8,12},{9,5},{1... | collective-permute-start | bytes 294920 | tf_op jit(solution)/shard_map/ppermute | solution.py:504
  6.8 1.5 %collective-permute-start.2 = (f32[16,1536]{1,0:T(8,128)S(1)}, f32[16,1536]{1,0:T(8,128)S(1)}, u32[]{:S(2)}, u32[]{:S(2)}) collective-permute-start(f32[16,1536]{1,0:T(8,128)S(1)} %constant_dynamic-update-slice_fusion), channel_id=1, source_target_pairs={{0,2},{1,15},{2,4},{3,1},{4,6},{5,3},{6,8},{7,5},{8,10},{9,7},{10,... | collective-permute-start | bytes 294920 | tf_op jit(solution)/shard_map/ppermute | solution.py:504
  8.3 0.7 %collective-permute-start.1 = (f32[16,4992]{1,0:T(8,128)S(1)}, f32[16,4992]{1,0:T(8,128)S(1)}, u32[]{:S(2)}, u32[]{:S(2)}) collective-permute-start(f32[16,4992]{1,0:T(8,128)S(1)} %pad_maximum_fusion.payload_ref), channel_id=1, source_target_pairs={{1,2},{2,1},{3,4},{4,3},{5,6},{6,5},{7,8},{8,7},{9,10},{10,9},{11,... | collective-permute-start | bytes 958472 | tf_op jit(solution)/shard_map/ppermute | solution.py:504
  9.0 3.9 %shard_map.87 = (bf16[16,512,256]{2,1,0:T(8,128)(2,1)S(1)}, bf16[12,4,512,256]{3,2,1,0:T(8,128)(2,1)S(1)}, f32[16,4096]{1,0:T(8,128)S(1)}, bf16[16,80,256]{2,1,0:T(8,128)(2,1)S(1)}, f32[16,128]{1,0:T(8,128)S(1)}) custom-call(s32[8,128]{1,0:T(8,128)S(1)} %get-tuple-element.26.pairs_ref, f32[16,4992]{1,0:T(8,128)S(1)} %pad_maximum_fusion.payload_ref, ...), custom_call_target="tpu_custom_call" | custom-call | flops 4000000000 | bytes 28800000 | tf_op jit(solution)/shard_map/pallas_call | solution.py:474
  12.9 0.0 collective-permute-done.3.far_pair_ref
  12.9 1.2 %collective-permute-done.2.near_pair_ref = f32[16,1536]{1,0:T(8,128)S(1)} collective-permute-done((f32[16,1536]{1,0:T(8,128)S(1)}, f32[16,1536]{1,0:T(8,128)S(1)}, u32[]{:S(2)}, u32[]{:S(2)}) %collective-permute-start.2) | collective-permute-done | bytes 98336 | tf_op jit(solution)/shard_map/ppermute | solution.py:504
  14.1 0.6 %collective-permute-start.4 = (f32[16,3200]{1,0:T(8,128)S(1)}, f32[16,3200]{1,0:T(8,128)S(1)}, u32[]{:S(2)}, u32[]{:S(2)}) collective-permute-start(f32[16,3200]{1,0:T(8,128)S(1)} %pad_maximum_fusion.2), channel_id=1, source_target_pairs={{0,1},{1,0},{2,3},{3,2},{4,5},{5,4},{6,7},{7,6},{8,9},{9,8},{10,11... | collective-permute-start | bytes 614408 | tf_op jit(solution)/shard_map/ppermute | solution.py:504
  14.7 0.0 collective-permute-done.5.payload_ref
  14.7 3.9 %shard_map.88 = (bf16[12,4,512,256]{3,2,1,0:T(8,128)(2,1)S(1)}, f32[16,4096]{1,0:T(8,128)S(1)}) custom-call(s32[8,128]{1,0:T(8,128)S(1)} %get-tuple-element.26.pairs_ref, f32[16,4864]{1,0:T(8,128)S(1)} %collective-permute-done.5.payload_ref, bf16[16,80,256]{2,1,0:T(8,128)(2,1)S(1)} %get-tuple-element.29.targets_ref, f32[16,4096]{1,0:T(8,128)S(1)} %get-tuple-element.33.start_ref), custom_call_target="tpu_custom_call" | custom-call | flops 100000000 | bytes 720000 | tf_op jit(solution)/shard_map/pallas_call | solution.py:474
  18.6 0.0 collective-permute-done.4.swapped_ref
  18.6 3.4 %shard_map.89 = (f32[16,4096]{1,0:T(8,128)S(1)}, bf16[16,64,1024]{2,1,0:T(8,128)(2,1)S(1)}) custom-call(s32[16,32]{1,0:T(8,128)S(1)} %get-tuple-element.30.at_ref, f32[16,1536]{1,0:T(8,128)S(1)} %collective-permute-done.2.near_pair_ref, f32[16,1536]{1,0:T(8,128)S(1)} %collective-permute-done.3.far_pair_ref, ...), custom_call_target="tpu_custom_call" | custom-call | flops 100000000 | bytes 720000 | tf_op jit(solution)/shard_map/pallas_call | solution.py:474
  22.0 0.0 collective-permute-done.1.payload_ref
  22.0 1.3 %shard_map.90 = (bf16[12,4,512,256]{3,2,1,0:T(8,128)(2,1)S(1)}, f32[16,4096]{1,0:T(8,128)S(1)}, f32[16,4096]{1,0:T(8,128)S(1)}, f32[16,640]{1,0:T(8,128)S(1)}) custom-call(s32[8,128]{1,0:T(8,128)S(1)} %get-tuple-element.26.pairs_ref, f32[16,4992]{1,0:T(8,128)S(1)} %collective-permute-done.1.payload_ref, ...), custom_call_target="tpu_custom_call" | custom-call | flops 2000000000 | bytes 14400000 | tf_op jit(solution)/shard_map/pallas_call | solution.py:474
  23.3 0.1 collective-permute-start.6
  23.4 0.5 %collective-permute-start.11 = (f32[16,4096]{1,0:T(8,128)S(1)}, f32[16,4096]{1,0:T(8,128)S(1)}, u32[]{:S(2)}, u32[]{:S(2)}) collective-permute-start(f32[16,4096]{1,0:T(8,128)S(1)} %get-tuple-element.40), channel_id=1, source_target_pairs={{0,1},{1,0},{2,3},{3,2},{4,5},{5,4},{6,7},{7,6},{8,9},{9,8},{10,11... | collective-permute-start | bytes 786440 | tf_op jit(solution)/shard_map/ppermute | solution.py:504
  23.9 0.7 %collective-permute-done.6.beside_ref.partner_ref = f32[16,640]{1,0:T(8,128)S(1)} collective-permute-done((f32[16,640]{1,0:T(8,128)S(1)}, f32[16,640]{1,0:T(8,128)S(1)}, u32[]{:S(2)}, u32[]{:S(2)}) %collective-permute-start.6) | collective-permute-done | bytes 40992 | tf_op jit(solution)/shard_map/ppermute | solution.py:504
  24.6 2.9 %collective-permute-start.9 = (f32[16,1280]{1,0:T(8,128)S(1)}, f32[16,1280]{1,0:T(8,128)S(1)}, u32[]{:S(2)}, u32[]{:S(2)}) collective-permute-start(f32[16,1280]{1,0:T(8,128)S(1)} %constant_dynamic-update-slice_fusion.2), channel_id=1, source_target_pairs={{0,4},{1,13},{2,6},{3,15},{4,8},{5,1},{6,10},{7,3},{8,12},{9,5},{1... | collective-permute-start | bytes 245768 | tf_op jit(solution)/shard_map/ppermute | solution.py:504
  27.5 0.0 collective-permute-start.8
  27.6 0.7 %collective-permute-start.7 = (f32[16,4224]{1,0:T(8,128)S(1)}, f32[16,4224]{1,0:T(8,128)S(1)}, u32[]{:S(2)}, u32[]{:S(2)}) collective-permute-start(f32[16,4224]{1,0:T(8,128)S(1)} %pad_maximum_fusion.1.payload_ref), channel_id=1, source_target_pairs={{1,2},{2,1},{3,4},{4,3},{5,6},{6,5},{7,8},{8,7},{9,10},{10,9},{11,... | collective-permute-start | bytes 811016 | tf_op jit(solution)/shard_map/ppermute | solution.py:504
  28.2 2.3 %shard_map.91 = (f32[16,4096]{1,0:T(8,128)S(1)}, f32[16,128]{1,0:T(8,128)S(1)}) custom-call(s32[8,128]{1,0:T(8,128)S(1)} %get-tuple-element.26.pairs_ref, f32[16,4224]{1,0:T(8,128)S(1)} %pad_maximum_fusion.1.payload_ref, f32[16,640]{1,0:T(8,128)S(1)} %collective-permute-done.6.beside_ref.partner_ref, bf16[16,512,256]{2,1,0:T(8,128)(2,1)S(1)} %get-tuple-element.42.own_ref, ...), custom_call_target="tpu_custom_call" | custom-call | flops 4000000000 | bytes 28800000 | tf_op jit(solution)/shard_map/pallas_call | solution.py:474
  30.6 0.4 collective-permute-done.9.far_pair_ref
  31.0 3.7 %collective-permute-done.8.near_pair_ref = f32[16,1280]{1,0:T(8,128)S(1)} collective-permute-done((f32[16,1280]{1,0:T(8,128)S(1)}, f32[16,1280]{1,0:T(8,128)S(1)}, u32[]{:S(2)}, u32[]{:S(2)}) %collective-permute-start.8) | collective-permute-done | bytes 81952 | tf_op jit(solution)/shard_map/ppermute | solution.py:504
  34.7 0.1 collective-permute-start.10
  34.8 0.0 collective-permute-done.11.payload_ref
  34.8 2.2 %shard_map.92.near_ref = f32[16,4096]{1,0:T(8,128)S(1)} custom-call(s32[8,128]{1,0:T(8,128)S(1)} %get-tuple-element.26.pairs_ref, f32[16,4096]{1,0:T(8,128)S(1)} %collective-permute-done.11.payload_ref, f32[16,4096]{1,0:T(8,128)S(1)} %get-tuple-element.45.start_ref, bf16[12,4,512,256]{3,2,1,0:T(8,128)(2,1)S(1)} %get-tuple-element.46.kept_ref), custom_call_target="tpu_custom_call" | custom-call | flops 2000000000 | bytes 14400000 | tf_op jit(solution)/shard_map/pallas_call | solution.py:474
  37.0 0.0 collective-permute-done.10.swapped_ref
  37.0 0.3 shard_map.95.one_ref
  37.3 0.0 collective-permute-start.12
  37.3 2.2 %shard_map.93.start_ref = f32[16,4096]{1,0:T(8,128)S(1)} custom-call(s32[16,32]{1,0:T(8,128)S(1)} %get-tuple-element.30.at_ref, f32[16,1280]{1,0:T(8,128)S(1)} %collective-permute-done.8.near_pair_ref, f32[16,1280]{1,0:T(8,128)S(1)} %collective-permute-done.9.far_pair_ref, f32[16,2688]{1,0:T(8,128)S(1)} %collective-permute-done.10.swapped_ref, ...), custom_call_target="tpu_custom_call" | custom-call | flops 2000000000 | bytes 14400000 | tf_op jit(solution)/shard_map/pallas_call | solution.py:474
  39.6 0.0 collective-permute-done.7.payload_ref
  39.6 0.7 %shard_map.94.near_ref = f32[16,4096]{1,0:T(8,128)S(1)} custom-call(s32[8,128]{1,0:T(8,128)S(1)} %get-tuple-element.26.pairs_ref, f32[16,4224]{1,0:T(8,128)S(1)} %collective-permute-done.7.payload_ref, f32[16,4096]{1,0:T(8,128)S(1)} %shard_map.93.start_ref, bf16[12,4,512,256]{3,2,1,0:T(8,128)(2,1)S(1)} %get-tuple-element.48.kept_ref), custom_call_target="tpu_custom_call" | custom-call | flops 750000000 | bytes 5400000 | tf_op jit(solution)/shard_map/pallas_call | solution.py:474
  40.3 1.5 %collective-permute-done.12.two_ref = f32[16,128]{1,0:T(8,128)S(1)} collective-permute-done((f32[16,128]{1,0:T(8,128)S(1)}, f32[16,128]{1,0:T(8,128)S(1)}, u32[]{:S(2)}, u32[]{:S(2)}) %collective-permute-start.12) | collective-permute-done | bytes 8224 | tf_op jit(solution)/shard_map/ppermute | solution.py:504
  41.9 1.2 %shard_map.96 = (f32[16,4096]{1,0:T(8,128)}, f32[16,4096]{1,0:T(8,128)}) custom-call(f32[16,4096]{1,0:T(8,128)S(1)} %shard_map.94.near_ref, f32[16,256]{1,0:T(8,128)S(1)} %get-tuple-element.38.area_ref, f32[16,4096]{1,0:T(8,128)S(1)} %get-tuple-element.49.image_ref, f32[16,4096]{1,0:T(8,128)S(1)} %get-tuple-element.39.krylov_ref, ...), custom_call_target="tpu_custom_call" | custom-call | flops 500000000 | bytes 3600000 | tf_op jit(solution)/shard_map/pallas_call | solution.py:474
  (10 shorter events, 0.1 us)
Async XLA Ops:
  2.4 1.4 %collective-permute-start = (f32[16,768]{1,0:T(8,128)S(1)}, f32[16,768]{1,0:T(8,128)S(1)}, u32[]{:S(2)}, u32[]{:S(2)}) collective-permute-start(f32[16,768]{1,0:T(8,128)S(1)} %get-tuple-element.28), channel_id=1, source_target_pairs={{0,1},{1,0},{2,3},{3,2},{4,5},{5,4},{6,7},{7,6},{8,9},{9,8},{10,11... | collective-permute-start | bytes 147464 | tf_op jit(solution)/shard_map/ppermute | solution.py:504
  3.0 11.7 %collective-permute-start.5 = (f32[16,4864]{1,0:T(8,128)S(1)}, f32[16,4864]{1,0:T(8,128)S(1)}, u32[]{:S(2)}, u32[]{:S(2)}) collective-permute-start(f32[16,4864]{1,0:T(8,128)S(1)} %get-tuple-element.27), channel_id=1, source_target_pairs={{0,1},{1,0},{2,3},{3,2},{4,5},{5,4},{6,7},{7,6},{8,9},{9,8},{10,11... | collective-permute-start | bytes 933896 | tf_op jit(solution)/shard_map/ppermute | solution.py:504
  3.8 9.1 %collective-permute-start.3 = (f32[16,1536]{1,0:T(8,128)S(1)}, f32[16,1536]{1,0:T(8,128)S(1)}, u32[]{:S(2)}, u32[]{:S(2)}) collective-permute-start(f32[16,1536]{1,0:T(8,128)S(1)} %constant_dynamic-update-slice_fusion), channel_id=1, source_target_pairs={{0,4},{1,13},{2,6},{3,15},{4,8},{5,1},{6,10},{7,3},{8,12},{9,5},{1... | collective-permute-start | bytes 294920 | tf_op jit(solution)/shard_map/ppermute | solution.py:504
  6.8 7.3 %collective-permute-start.2 = (f32[16,1536]{1,0:T(8,128)S(1)}, f32[16,1536]{1,0:T(8,128)S(1)}, u32[]{:S(2)}, u32[]{:S(2)}) collective-permute-start(f32[16,1536]{1,0:T(8,128)S(1)} %constant_dynamic-update-slice_fusion), channel_id=1, source_target_pairs={{0,2},{1,15},{2,4},{3,1},{4,6},{5,3},{6,8},{7,5},{8,10},{9,7},{10,... | collective-permute-start | bytes 294920 | tf_op jit(solution)/shard_map/ppermute | solution.py:504
  8.3 13.7 %collective-permute-start.1 = (f32[16,4992]{1,0:T(8,128)S(1)}, f32[16,4992]{1,0:T(8,128)S(1)}, u32[]{:S(2)}, u32[]{:S(2)}) collective-permute-start(f32[16,4992]{1,0:T(8,128)S(1)} %pad_maximum_fusion.payload_ref), channel_id=1, source_target_pairs={{1,2},{2,1},{3,4},{4,3},{5,6},{6,5},{7,8},{8,7},{9,10},{10,9},{11,... | collective-permute-start | bytes 958472 | tf_op jit(solution)/shard_map/ppermute | solution.py:504
  14.1 4.5 %collective-permute-start.4 = (f32[16,3200]{1,0:T(8,128)S(1)}, f32[16,3200]{1,0:T(8,128)S(1)}, u32[]{:S(2)}, u32[]{:S(2)}) collective-permute-start(f32[16,3200]{1,0:T(8,128)S(1)} %pad_maximum_fusion.2), channel_id=1, source_target_pairs={{0,1},{1,0},{2,3},{3,2},{4,5},{5,4},{6,7},{7,6},{8,9},{9,8},{10,11... | collective-permute-start | bytes 614408 | tf_op jit(solution)/shard_map/ppermute | solution.py:504
  23.3 1.3 %collective-permute-start.6 = (f32[16,640]{1,0:T(8,128)S(1)}, f32[16,640]{1,0:T(8,128)S(1)}, u32[]{:S(2)}, u32[]{:S(2)}) collective-permute-start(f32[16,640]{1,0:T(8,128)S(1)} %get-tuple-element.41.payload_ref), channel_id=1, source_target_pairs={{0,1},{1,0},{2,3},{3,2},{4,5},{5,4},{6,7},{7,6},{8,9},{9,8},{10,11... | collective-permute-start | bytes 122888 | tf_op jit(solution)/shard_map/ppermute | solution.py:504
  23.4 11.3 %collective-permute-start.11 = (f32[16,4096]{1,0:T(8,128)S(1)}, f32[16,4096]{1,0:T(8,128)S(1)}, u32[]{:S(2)}, u32[]{:S(2)}) collective-permute-start(f32[16,4096]{1,0:T(8,128)S(1)} %get-tuple-element.40), channel_id=1, source_target_pairs={{0,1},{1,0},{2,3},{3,2},{4,5},{5,4},{6,7},{7,6},{8,9},{9,8},{10,11... | collective-permute-start | bytes 786440 | tf_op jit(solution)/shard_map/ppermute | solution.py:504
  24.6 6.3 %collective-permute-start.9 = (f32[16,1280]{1,0:T(8,128)S(1)}, f32[16,1280]{1,0:T(8,128)S(1)}, u32[]{:S(2)}, u32[]{:S(2)}) collective-permute-start(f32[16,1280]{1,0:T(8,128)S(1)} %constant_dynamic-update-slice_fusion.2), channel_id=1, source_target_pairs={{0,4},{1,13},{2,6},{3,15},{4,8},{5,1},{6,10},{7,3},{8,12},{9,5},{1... | collective-permute-start | bytes 245768 | tf_op jit(solution)/shard_map/ppermute | solution.py:504
  27.5 7.1 %collective-permute-start.8 = (f32[16,1280]{1,0:T(8,128)S(1)}, f32[16,1280]{1,0:T(8,128)S(1)}, u32[]{:S(2)}, u32[]{:S(2)}) collective-permute-start(f32[16,1280]{1,0:T(8,128)S(1)} %constant_dynamic-update-slice_fusion.2), channel_id=1, source_target_pairs={{0,2},{1,15},{2,4},{3,1},{4,6},{5,3},{6,8},{7,5},{8,10},{9,7},{10,... | collective-permute-start | bytes 245768 | tf_op jit(solution)/shard_map/ppermute | solution.py:504
  27.6 12.0 %collective-permute-start.7 = (f32[16,4224]{1,0:T(8,128)S(1)}, f32[16,4224]{1,0:T(8,128)S(1)}, u32[]{:S(2)}, u32[]{:S(2)}) collective-permute-start(f32[16,4224]{1,0:T(8,128)S(1)} %pad_maximum_fusion.1.payload_ref), channel_id=1, source_target_pairs={{1,2},{2,1},{3,4},{4,3},{5,6},{6,5},{7,8},{8,7},{9,10},{10,9},{11,... | collective-permute-start | bytes 811016 | tf_op jit(solution)/shard_map/ppermute | solution.py:504
  34.7 2.3 %collective-permute-start.10 = (f32[16,2688]{1,0:T(8,128)S(1)}, f32[16,2688]{1,0:T(8,128)S(1)}, u32[]{:S(2)}, u32[]{:S(2)}) collective-permute-start(f32[16,2688]{1,0:T(8,128)S(1)} %pad_maximum_fusion.3), channel_id=1, source_target_pairs={{0,1},{1,0},{2,3},{3,2},{4,5},{5,4},{6,7},{7,6},{8,9},{9,8},{10,11... | collective-permute-start | bytes 516104 | tf_op jit(solution)/shard_map/ppermute | solution.py:504
  37.3 4.6 %collective-permute-start.12 = (f32[16,128]{1,0:T(8,128)S(1)}, f32[16,128]{1,0:T(8,128)S(1)}, u32[]{:S(2)}, u32[]{:S(2)}) collective-permute-start(f32[16,128]{1,0:T(8,128)S(1)} %shard_map.95.one_ref), channel_id=1, source_target_pairs={{0,8},{1,9},{2,10},{3,11},{4,12},{5,13},{6,14},{7,15},{8,0},{9,1},... | collective-permute-start | bytes 24584 | tf_op jit(solution)/shard_map/ppermute | solution.py:504

commit v8 on v7

--- a/solution.py
+++ b/solution.py
@@ -387,13 +387,12 @@
 
 def far_fields(gathered_ref, coupling_ref, fields_ref):
     for c in range(gathered_ref.shape[0]):
-        field = quartered(dot_nt(coupling_ref[c], gathered_ref[c]))
-        field = jnp.concatenate(split(field), axis=1)
-        fields_ref[c] = jnp.concatenate([field, field], axis=0)
+        field = quartered(dot_nt(gathered_ref[c], coupling_ref[c]))
+        fields_ref[c] = stacked(jnp.concatenate([field, field], axis=1))
 
 
 def far_potential(fields_ref, c, basis):
-    return folded(dot_tn(fields_ref[c], basis))
+    return folded(dot_nn(fields_ref[c], basis))
 
 
 def far_kernel(cl, rank, at_ref, near_pair_ref, far_pair_ref, swapped_ref, center_ref, near_ref, basis_ref, offsets_ref,
@@ -503,13 +502,14 @@
     def move(value, pairs):
         return lax.ppermute(value, "clus", pairs)
 
-    def outward(value, steps):
-        return move(value, [(i, (i + steps * (1 - 2 * (i % 2))) % devices) for i in range(devices)])
-
-    def exchange(payload, table):
+    def outward(value, steps, wrap=True):
+        moves = [(i, i + steps * (1 - 2 * (i % 2))) for i in range(devices)]
+        return move(value, [(i, j % devices if wrap or 0 <= j < devices else i + 1 - 2 * (i % 2)) for i, j in moves])
+
+    def exchange(payload, table, wrap):
         beside = move(table, pairing)
         pair = jnp.concatenate([table, beside], axis=1)
-        near_pair, far_pair = outward(pair, 2), outward(pair, 4)
+        near_pair, far_pair = outward(pair, 2, wrap), outward(pair, 4, wrap)
         sent = jnp.concatenate([payload, beside[:, beside.shape[1] - LANES:]], axis=1)
         return sent, beside, near_pair, far_pair, move(sent, bridging), move(payload, pairing)
 
@@ -537,7 +537,7 @@
         position, vertices, panel_vertices, krylov, basis, far_pairs, near_pairs.T, offsets,
         us=1.5,
     )
-    sent, beside, near_pair, far_pair, other, partner = exchange(payload, table)
+    sent, beside, near_pair, far_pair, other, partner = exchange(payload, table, False)
     group = 4
     own = ((clusters, 2 * cl, cl), BF16)
     kept = ((clusters * (slots - 1) // group, group, 2 * cl, cl), BF16)
@@ -565,7 +565,7 @@
     tiles = 6 * per * span // LANES
     window = pltpu.VMEM((tiles, 2 * rhs, LANES), BF16)
     gathered = pltpu.VMEM((clusters, 2 * rhs, partners * rank), BF16)
-    fields = pltpu.VMEM((clusters, 2 * rank, 2 * rhs), BF16)
+    fields = pltpu.VMEM((clusters, 2 * rhs, 2 * rank), BF16)
     near, coupling = call(
         functools.partial(far_kernel, cl, rank),
         [whole, ((clusters, 2 * rank, partners * rank), BF16)],
@@ -582,7 +582,7 @@
         pairs, other, targets, near, area, krylov, basis,
         us=4.0,
     )
-    sent, beside, near_pair, far_pair, other, partner = exchange(payload, table)
+    sent, beside, near_pair, far_pair, other, partner = exchange(payload, table, True)
     near, tail = call(
         functools.partial(own_again_kernel, cl),
         [whole, sums_shape],

time: 42.6 us -> 42.5 us (level); the launches traced: 43.1 us -> 42.6 us
  starting transfers between devices: 10.5 us -> 13.1 us
  waiting for transfers between devices: 8.34 us -> 6.46 us
  Pallas kernels: 23.3 us -> 22.1 us
    ppermute x13, starting transfers between devices: 10.5 us -> 13.1 us  [move(): return lax.ppermute(value, 'clus', pairs)]
    ppermute x13, waiting for transfers between devices: 8.34 us -> 6.46 us  [move(): return lax.ppermute(value, 'clus', pairs)]
    pallas_call x11, Pallas kernels: 23.3 us -> 22.1 us  [call(): pl.pallas_call(kernel, out_shape=[pltpu.VMEM(*out) if m == 'p' else jax.S...]
  transfers between devices with their start and end apart: 13 -> 13, of which waited for: 6 -> 4; matrix products, arithmetic and copies ran while one was open for 0% -> 0% of each run, Pallas kernels for 44% -> 42%
where the time goes in v8:
time: 42.5 us; the launch traced here: 42.6 us
  Pallas kernels  22.1 us (52%)
  starting transfers between devices  13.1 us (31%)
  waiting for transfers between devices  6.46 us (15%)
  between operations  0.81 us (2%)
    pallas_call x11, Pallas kernels, call(): pl.pallas_call(kernel, out_shape=[pltpu.VMEM(*out) if m == 'p' else jax.S...  22.1 us
    ppermute x13, starting transfers between devices, move(): return lax.ppermute(value, 'clus', pairs)  13.1 us
    ppermute x13, waiting for transfers between devices, move(): return lax.ppermute(value, 'clus', pairs)  6.46 us
  transfers between devices with their start and end apart: 13, of which 4 were waited for; matrix products, arithmetic and copies ran while one was open for 0% of the time, Pallas kernels for 42%

profile of v8, /device:TPU:0, one launch (start us, length us, event | category | flops | bytes accessed | tf_op | source)
XLA Modules:
  0.0 42.6 jit_solution(15311403348760333254)
XLA Ops:
  0.6 1.8 %shard_map.86 = (f32[16,4864]{1,0:T(8,128)S(1)}, f32[16,768]{1,0:T(8,128)S(1)}, f32[16,256]{1,0:T(8,128)S(1)}, f32[16,384]{1,0:T(8,128)S(1)}, s32[16,32]{1,0:T(8...) custom-call(s32[1]{0:T(128)} %bitcast.position_ref, ...), custom_call_target="tpu_custom_call" | custom-call | flops 750000000 | bytes 5400000 | tf_op jit(solution)/shard_map/pallas_call | solution.py:473
  2.4 0.5 %collective-permute-start = (f32[16,768]{1,0:T(8,128)S(1)}, f32[16,768]{1,0:T(8,128)S(1)}, u32[]{:S(2)}, u32[]{:S(2)}) collective-permute-start(f32[16,768]{1,0:T(8,128)S(1)} %get-tuple-element.28), channel_id=1, source_target_pairs={{0,1},{1,0},{2,3},{3,2},{4,5},{5,4},{6,7},{7,6},{8,9},{9,8},{10,11... | collective-permute-start | bytes 147464 | tf_op jit(solution)/shard_map/ppermute | solution.py:503
  3.0 0.1 collective-permute-start.5
  3.0 0.8 %collective-permute-done.beside_ref = f32[16,768]{1,0:T(8,128)S(1)} collective-permute-done((f32[16,768]{1,0:T(8,128)S(1)}, f32[16,768]{1,0:T(8,128)S(1)}, u32[]{:S(2)}, u32[]{:S(2)}) %collective-permute-start) | collective-permute-done | bytes 49184 | tf_op jit(solution)/shard_map/ppermute | solution.py:503
  3.8 2.9 %collective-permute-start.3 = (f32[16,1536]{1,0:T(8,128)S(1)}, f32[16,1536]{1,0:T(8,128)S(1)}, u32[]{:S(2)}, u32[]{:S(2)}) collective-permute-start(f32[16,1536]{1,0:T(8,128)S(1)} %constant_dynamic-update-slice_fusion), channel_id=1, source_target_pairs={{0,4},{1,0},{2,6},{3,2},{4,8},{5,1},{6,10},{7,3},{8,12},{9,5},{10,... | collective-permute-start | bytes 294920 | tf_op jit(solution)/shard_map/ppermute | solution.py:503
  6.8 1.5 %collective-permute-start.2 = (f32[16,1536]{1,0:T(8,128)S(1)}, f32[16,1536]{1,0:T(8,128)S(1)}, u32[]{:S(2)}, u32[]{:S(2)}) collective-permute-start(f32[16,1536]{1,0:T(8,128)S(1)} %constant_dynamic-update-slice_fusion), channel_id=1, source_target_pairs={{0,2},{1,0},{2,4},{3,1},{4,6},{5,3},{6,8},{7,5},{8,10},{9,7},{10,1... | collective-permute-start | bytes 294920 | tf_op jit(solution)/shard_map/ppermute | solution.py:503
  8.3 0.7 %collective-permute-start.1 = (f32[16,4992]{1,0:T(8,128)S(1)}, f32[16,4992]{1,0:T(8,128)S(1)}, u32[]{:S(2)}, u32[]{:S(2)}) collective-permute-start(f32[16,4992]{1,0:T(8,128)S(1)} %pad_maximum_fusion.payload_ref), channel_id=1, source_target_pairs={{1,2},{2,1},{3,4},{4,3},{5,6},{6,5},{7,8},{8,7},{9,10},{10,9},{11,... | collective-permute-start | bytes 958472 | tf_op jit(solution)/shard_map/ppermute | solution.py:503
  9.0 3.9 %shard_map.87 = (bf16[16,512,256]{2,1,0:T(8,128)(2,1)S(1)}, bf16[12,4,512,256]{3,2,1,0:T(8,128)(2,1)S(1)}, f32[16,4096]{1,0:T(8,128)S(1)}, bf16[16,80,256]{2,1,0:T(8,128)(2,1)S(1)}, f32[16,128]{1,0:T(8,128)S(1)}) custom-call(s32[8,128]{1,0:T(8,128)S(1)} %get-tuple-element.26.pairs_ref, f32[16,4992]{1,0:T(8,128)S(1)} %pad_maximum_fusion.payload_ref, ...), custom_call_target="tpu_custom_call" | custom-call | flops 4000000000 | bytes 28800000 | tf_op jit(solution)/shard_map/pallas_call | solution.py:473
  12.9 0.0 collective-permute-done.3.far_pair_ref
  12.9 0.0 collective-permute-done.2.near_pair_ref
  12.9 1.7 %collective-permute-start.4 = (f32[16,3200]{1,0:T(8,128)S(1)}, f32[16,3200]{1,0:T(8,128)S(1)}, u32[]{:S(2)}, u32[]{:S(2)}) collective-permute-start(f32[16,3200]{1,0:T(8,128)S(1)} %pad_maximum_fusion.2), channel_id=1, source_target_pairs={{0,1},{1,0},{2,3},{3,2},{4,5},{5,4},{6,7},{7,6},{8,9},{9,8},{10,11... | collective-permute-start | bytes 614408 | tf_op jit(solution)/shard_map/ppermute | solution.py:503
  14.7 0.0 collective-permute-done.5.payload_ref
  14.7 3.3 %shard_map.88 = (bf16[12,4,512,256]{3,2,1,0:T(8,128)(2,1)S(1)}, f32[16,4096]{1,0:T(8,128)S(1)}) custom-call(s32[8,128]{1,0:T(8,128)S(1)} %get-tuple-element.26.pairs_ref, f32[16,4864]{1,0:T(8,128)S(1)} %collective-permute-done.5.payload_ref, bf16[16,80,256]{2,1,0:T(8,128)(2,1)S(1)} %get-tuple-element.29.targets_ref, f32[16,4096]{1,0:T(8,128)S(1)} %get-tuple-element.33.start_ref), custom_call_target="tpu_custom_call" | custom-call | flops 100000000 | bytes 720000 | tf_op jit(solution)/shard_map/pallas_call | solution.py:473
  18.0 0.0 collective-permute-done.4.swapped_ref
  18.0 3.2 %shard_map.89 = (f32[16,4096]{1,0:T(8,128)S(1)}, bf16[16,64,1024]{2,1,0:T(8,128)(2,1)S(1)}) custom-call(s32[16,32]{1,0:T(8,128)S(1)} %get-tuple-element.30.at_ref, f32[16,1536]{1,0:T(8,128)S(1)} %collective-permute-done.2.near_pair_ref, f32[16,1536]{1,0:T(8,128)S(1)} %collective-permute-done.3.far_pair_ref, ...), custom_call_target="tpu_custom_call" | custom-call | flops 100000000 | bytes 720000 | tf_op jit(solution)/shard_map/pallas_call | solution.py:473
  21.2 0.0 collective-permute-done.1.payload_ref
  21.2 1.3 %shard_map.90 = (bf16[12,4,512,256]{3,2,1,0:T(8,128)(2,1)S(1)}, f32[16,4096]{1,0:T(8,128)S(1)}, f32[16,4096]{1,0:T(8,128)S(1)}, f32[16,640]{1,0:T(8,128)S(1)}) custom-call(s32[8,128]{1,0:T(8,128)S(1)} %get-tuple-element.26.pairs_ref, f32[16,4992]{1,0:T(8,128)S(1)} %collective-permute-done.1.payload_ref, ...), custom_call_target="tpu_custom_call" | custom-call | flops 2000000000 | bytes 14400000 | tf_op jit(solution)/shard_map/pallas_call | solution.py:473
  22.5 0.1 collective-permute-start.6
  22.6 0.5 %collective-permute-start.11 = (f32[16,4096]{1,0:T(8,128)S(1)}, f32[16,4096]{1,0:T(8,128)S(1)}, u32[]{:S(2)}, u32[]{:S(2)}) collective-permute-start(f32[16,4096]{1,0:T(8,128)S(1)} %get-tuple-element.40), channel_id=1, source_target_pairs={{0,1},{1,0},{2,3},{3,2},{4,5},{5,4},{6,7},{7,6},{8,9},{9,8},{10,11... | collective-permute-start | bytes 786440 | tf_op jit(solution)/shard_map/ppermute | solution.py:503
  23.1 0.7 %collective-permute-done.6.beside_ref.partner_ref = f32[16,640]{1,0:T(8,128)S(1)} collective-permute-done((f32[16,640]{1,0:T(8,128)S(1)}, f32[16,640]{1,0:T(8,128)S(1)}, u32[]{:S(2)}, u32[]{:S(2)}) %collective-permute-start.6) | collective-permute-done | bytes 40992 | tf_op jit(solution)/shard_map/ppermute | solution.py:503
  23.8 3.4 %collective-permute-start.9 = (f32[16,1280]{1,0:T(8,128)S(1)}, f32[16,1280]{1,0:T(8,128)S(1)}, u32[]{:S(2)}, u32[]{:S(2)}) collective-permute-start(f32[16,1280]{1,0:T(8,128)S(1)} %constant_dynamic-update-slice_fusion.2), channel_id=1, source_target_pairs={{0,4},{1,13},{2,6},{3,15},{4,8},{5,1},{6,10},{7,3},{8,12},{9,5},{1... | collective-permute-start | bytes 245768 | tf_op jit(solution)/shard_map/ppermute | solution.py:503
  27.2 0.9 %collective-permute-start.8 = (f32[16,1280]{1,0:T(8,128)S(1)}, f32[16,1280]{1,0:T(8,128)S(1)}, u32[]{:S(2)}, u32[]{:S(2)}) collective-permute-start(f32[16,1280]{1,0:T(8,128)S(1)} %constant_dynamic-update-slice_fusion.2), channel_id=1, source_target_pairs={{0,2},{1,15},{2,4},{3,1},{4,6},{5,3},{6,8},{7,5},{8,10},{9,7},{10,... | collective-permute-start | bytes 245768 | tf_op jit(solution)/shard_map/ppermute | solution.py:503
  28.1 0.7 %collective-permute-start.7 = (f32[16,4224]{1,0:T(8,128)S(1)}, f32[16,4224]{1,0:T(8,128)S(1)}, u32[]{:S(2)}, u32[]{:S(2)}) collective-permute-start(f32[16,4224]{1,0:T(8,128)S(1)} %pad_maximum_fusion.1.payload_ref), channel_id=1, source_target_pairs={{1,2},{2,1},{3,4},{4,3},{5,6},{6,5},{7,8},{8,7},{9,10},{10,9},{11,... | collective-permute-start | bytes 811016 | tf_op jit(solution)/shard_map/ppermute | solution.py:503
  28.8 2.3 %shard_map.91 = (f32[16,4096]{1,0:T(8,128)S(1)}, f32[16,128]{1,0:T(8,128)S(1)}) custom-call(s32[8,128]{1,0:T(8,128)S(1)} %get-tuple-element.26.pairs_ref, f32[16,4224]{1,0:T(8,128)S(1)} %pad_maximum_fusion.1.payload_ref, f32[16,640]{1,0:T(8,128)S(1)} %collective-permute-done.6.beside_ref.partner_ref, bf16[16,512,256]{2,1,0:T(8,128)(2,1)S(1)} %get-tuple-element.42.own_ref, ...), custom_call_target="tpu_custom_call" | custom-call | flops 4000000000 | bytes 28800000 | tf_op jit(solution)/shard_map/pallas_call | solution.py:473
  31.2 0.0 collective-permute-done.9.far_pair_ref
  31.2 3.2 %collective-permute-done.8.near_pair_ref = f32[16,1280]{1,0:T(8,128)S(1)} collective-permute-done((f32[16,1280]{1,0:T(8,128)S(1)}, f32[16,1280]{1,0:T(8,128)S(1)}, u32[]{:S(2)}, u32[]{:S(2)}) %collective-permute-start.8) | collective-permute-done | bytes 81952 | tf_op jit(solution)/shard_map/ppermute | solution.py:503
  34.4 0.1 collective-permute-start.10
  34.5 0.0 collective-permute-done.11.payload_ref
  34.5 1.9 %shard_map.92.near_ref = f32[16,4096]{1,0:T(8,128)S(1)} custom-call(s32[8,128]{1,0:T(8,128)S(1)} %get-tuple-element.26.pairs_ref, f32[16,4096]{1,0:T(8,128)S(1)} %collective-permute-done.11.payload_ref, f32[16,4096]{1,0:T(8,128)S(1)} %get-tuple-element.45.start_ref, bf16[12,4,512,256]{3,2,1,0:T(8,128)(2,1)S(1)} %get-tuple-element.46.kept_ref), custom_call_target="tpu_custom_call" | custom-call | flops 2000000000 | bytes 14400000 | tf_op jit(solution)/shard_map/pallas_call | solution.py:473
  36.4 0.0 collective-permute-done.10.swapped_ref
  36.5 0.3 shard_map.95.one_ref
  36.8 0.0 collective-permute-start.12
  36.8 2.1 %shard_map.93.start_ref = f32[16,4096]{1,0:T(8,128)S(1)} custom-call(s32[16,32]{1,0:T(8,128)S(1)} %get-tuple-element.30.at_ref, f32[16,1280]{1,0:T(8,128)S(1)} %collective-permute-done.8.near_pair_ref, f32[16,1280]{1,0:T(8,128)S(1)} %collective-permute-done.9.far_pair_ref, f32[16,2688]{1,0:T(8,128)S(1)} %collective-permute-done.10.swapped_ref, ...), custom_call_target="tpu_custom_call" | custom-call | flops 2000000000 | bytes 14400000 | tf_op jit(solution)/shard_map/pallas_call | solution.py:473
  38.9 0.0 collective-permute-done.7.payload_ref
  38.9 0.7 %shard_map.94.near_ref = f32[16,4096]{1,0:T(8,128)S(1)} custom-call(s32[8,128]{1,0:T(8,128)S(1)} %get-tuple-element.26.pairs_ref, f32[16,4224]{1,0:T(8,128)S(1)} %collective-permute-done.7.payload_ref, f32[16,4096]{1,0:T(8,128)S(1)} %shard_map.93.start_ref, bf16[12,4,512,256]{3,2,1,0:T(8,128)(2,1)S(1)} %get-tuple-element.48.kept_ref), custom_call_target="tpu_custom_call" | custom-call | flops 750000000 | bytes 5400000 | tf_op jit(solution)/shard_map/pallas_call | solution.py:473
  39.6 1.7 %collective-permute-done.12.two_ref = f32[16,128]{1,0:T(8,128)S(1)} collective-permute-done((f32[16,128]{1,0:T(8,128)S(1)}, f32[16,128]{1,0:T(8,128)S(1)}, u32[]{:S(2)}, u32[]{:S(2)}) %collective-permute-start.12) | collective-permute-done | bytes 8224 | tf_op jit(solution)/shard_map/ppermute | solution.py:503
  41.3 1.2 %shard_map.96 = (f32[16,4096]{1,0:T(8,128)}, f32[16,4096]{1,0:T(8,128)}) custom-call(f32[16,4096]{1,0:T(8,128)S(1)} %shard_map.94.near_ref, f32[16,256]{1,0:T(8,128)S(1)} %get-tuple-element.38.area_ref, f32[16,4096]{1,0:T(8,128)S(1)} %get-tuple-element.49.image_ref, f32[16,4096]{1,0:T(8,128)S(1)} %get-tuple-element.39.krylov_ref, ...), custom_call_target="tpu_custom_call" | custom-call | flops 500000000 | bytes 3600000 | tf_op jit(solution)/shard_map/pallas_call | solution.py:473
  (10 shorter events, 0.1 us)
Async XLA Ops:
  2.4 1.4 %collective-permute-start = (f32[16,768]{1,0:T(8,128)S(1)}, f32[16,768]{1,0:T(8,128)S(1)}, u32[]{:S(2)}, u32[]{:S(2)}) collective-permute-start(f32[16,768]{1,0:T(8,128)S(1)} %get-tuple-element.28), channel_id=1, source_target_pairs={{0,1},{1,0},{2,3},{3,2},{4,5},{5,4},{6,7},{7,6},{8,9},{9,8},{10,11... | collective-permute-start | bytes 147464 | tf_op jit(solution)/shard_map/ppermute | solution.py:503
  3.0 11.7 %collective-permute-start.5 = (f32[16,4864]{1,0:T(8,128)S(1)}, f32[16,4864]{1,0:T(8,128)S(1)}, u32[]{:S(2)}, u32[]{:S(2)}) collective-permute-start(f32[16,4864]{1,0:T(8,128)S(1)} %get-tuple-element.27), channel_id=1, source_target_pairs={{0,1},{1,0},{2,3},{3,2},{4,5},{5,4},{6,7},{7,6},{8,9},{9,8},{10,11... | collective-permute-start | bytes 933896 | tf_op jit(solution)/shard_map/ppermute | solution.py:503
  3.8 9.1 %collective-permute-start.3 = (f32[16,1536]{1,0:T(8,128)S(1)}, f32[16,1536]{1,0:T(8,128)S(1)}, u32[]{:S(2)}, u32[]{:S(2)}) collective-permute-start(f32[16,1536]{1,0:T(8,128)S(1)} %constant_dynamic-update-slice_fusion), channel_id=1, source_target_pairs={{0,4},{1,0},{2,6},{3,2},{4,8},{5,1},{6,10},{7,3},{8,12},{9,5},{10,... | collective-permute-start | bytes 294920 | tf_op jit(solution)/shard_map/ppermute | solution.py:503
  6.8 6.1 %collective-permute-start.2 = (f32[16,1536]{1,0:T(8,128)S(1)}, f32[16,1536]{1,0:T(8,128)S(1)}, u32[]{:S(2)}, u32[]{:S(2)}) collective-permute-start(f32[16,1536]{1,0:T(8,128)S(1)} %constant_dynamic-update-slice_fusion), channel_id=1, source_target_pairs={{0,2},{1,0},{2,4},{3,1},{4,6},{5,3},{6,8},{7,5},{8,10},{9,7},{10,1... | collective-permute-start | bytes 294920 | tf_op jit(solution)/shard_map/ppermute | solution.py:503
  8.3 12.9 %collective-permute-start.1 = (f32[16,4992]{1,0:T(8,128)S(1)}, f32[16,4992]{1,0:T(8,128)S(1)}, u32[]{:S(2)}, u32[]{:S(2)}) collective-permute-start(f32[16,4992]{1,0:T(8,128)S(1)} %pad_maximum_fusion.payload_ref), channel_id=1, source_target_pairs={{1,2},{2,1},{3,4},{4,3},{5,6},{6,5},{7,8},{8,7},{9,10},{10,9},{11,... | collective-permute-start | bytes 958472 | tf_op jit(solution)/shard_map/ppermute | solution.py:503
  12.9 5.0 %collective-permute-start.4 = (f32[16,3200]{1,0:T(8,128)S(1)}, f32[16,3200]{1,0:T(8,128)S(1)}, u32[]{:S(2)}, u32[]{:S(2)}) collective-permute-start(f32[16,3200]{1,0:T(8,128)S(1)} %pad_maximum_fusion.2), channel_id=1, source_target_pairs={{0,1},{1,0},{2,3},{3,2},{4,5},{5,4},{6,7},{7,6},{8,9},{9,8},{10,11... | collective-permute-start | bytes 614408 | tf_op jit(solution)/shard_map/ppermute | solution.py:503
  22.5 1.3 %collective-permute-start.6 = (f32[16,640]{1,0:T(8,128)S(1)}, f32[16,640]{1,0:T(8,128)S(1)}, u32[]{:S(2)}, u32[]{:S(2)}) collective-permute-start(f32[16,640]{1,0:T(8,128)S(1)} %get-tuple-element.41.payload_ref), channel_id=1, source_target_pairs={{0,1},{1,0},{2,3},{3,2},{4,5},{5,4},{6,7},{7,6},{8,9},{9,8},{10,11... | collective-permute-start | bytes 122888 | tf_op jit(solution)/shard_map/ppermute | solution.py:503
  22.6 11.9 %collective-permute-start.11 = (f32[16,4096]{1,0:T(8,128)S(1)}, f32[16,4096]{1,0:T(8,128)S(1)}, u32[]{:S(2)}, u32[]{:S(2)}) collective-permute-start(f32[16,4096]{1,0:T(8,128)S(1)} %get-tuple-element.40), channel_id=1, source_target_pairs={{0,1},{1,0},{2,3},{3,2},{4,5},{5,4},{6,7},{7,6},{8,9},{9,8},{10,11... | collective-permute-start | bytes 786440 | tf_op jit(solution)/shard_map/ppermute | solution.py:503
  23.8 7.4 %collective-permute-start.9 = (f32[16,1280]{1,0:T(8,128)S(1)}, f32[16,1280]{1,0:T(8,128)S(1)}, u32[]{:S(2)}, u32[]{:S(2)}) collective-permute-start(f32[16,1280]{1,0:T(8,128)S(1)} %constant_dynamic-update-slice_fusion.2), channel_id=1, source_target_pairs={{0,4},{1,13},{2,6},{3,15},{4,8},{5,1},{6,10},{7,3},{8,12},{9,5},{1... | collective-permute-start | bytes 245768 | tf_op jit(solution)/shard_map/ppermute | solution.py:503
  27.2 7.2 %collective-permute-start.8 = (f32[16,1280]{1,0:T(8,128)S(1)}, f32[16,1280]{1,0:T(8,128)S(1)}, u32[]{:S(2)}, u32[]{:S(2)}) collective-permute-start(f32[16,1280]{1,0:T(8,128)S(1)} %constant_dynamic-update-slice_fusion.2), channel_id=1, source_target_pairs={{0,2},{1,15},{2,4},{3,1},{4,6},{5,3},{6,8},{7,5},{8,10},{9,7},{10,... | collective-permute-start | bytes 245768 | tf_op jit(solution)/shard_map/ppermute | solution.py:503
  28.1 10.8 %collective-permute-start.7 = (f32[16,4224]{1,0:T(8,128)S(1)}, f32[16,4224]{1,0:T(8,128)S(1)}, u32[]{:S(2)}, u32[]{:S(2)}) collective-permute-start(f32[16,4224]{1,0:T(8,128)S(1)} %pad_maximum_fusion.1.payload_ref), channel_id=1, source_target_pairs={{1,2},{2,1},{3,4},{4,3},{5,6},{6,5},{7,8},{8,7},{9,10},{10,9},{11,... | collective-permute-start | bytes 811016 | tf_op jit(solution)/shard_map/ppermute | solution.py:503
  34.4 2.0 %collective-permute-start.10 = (f32[16,2688]{1,0:T(8,128)S(1)}, f32[16,2688]{1,0:T(8,128)S(1)}, u32[]{:S(2)}, u32[]{:S(2)}) collective-permute-start(f32[16,2688]{1,0:T(8,128)S(1)} %pad_maximum_fusion.3), channel_id=1, source_target_pairs={{0,1},{1,0},{2,3},{3,2},{4,5},{5,4},{6,7},{7,6},{8,9},{9,8},{10,11... | collective-permute-start | bytes 516104 | tf_op jit(solution)/shard_map/ppermute | solution.py:503
  36.8 4.6 %collective-permute-start.12 = (f32[16,128]{1,0:T(8,128)S(1)}, f32[16,128]{1,0:T(8,128)S(1)}, u32[]{:S(2)}, u32[]{:S(2)}) collective-permute-start(f32[16,128]{1,0:T(8,128)S(1)} %shard_map.95.one_ref), channel_id=1, source_target_pairs={{0,8},{1,9},{2,10},{3,11},{4,12},{5,13},{6,14},{7,15},{8,0},{9,1},... | collective-permute-start | bytes 24584 | tf_op jit(solution)/shard_map/ppermute | solution.py:503

commit v9 on v8

--- a/solution.py
+++ b/solution.py
@@ -377,11 +377,16 @@
     return (far_ref, 0), (far_ref, width), (near_ref, 0), (swapped_ref, width), (swapped_ref, 0), (swapped_ref, 3 * width)
 
 
-def pick(source_ref, at_ref, c, g, per, lane):
+def lane_masks(shape, rank, kind):
+    lane = (lax.broadcasted_iota(jnp.int32, shape, 1) // rank).astype(kind)
+    return [lane == jnp.asarray(u, kind) for u in range(LANES // rank)]
+
+
+def pick(source_ref, at_ref, c, g, masks):
     row = None
-    for u in range(per):
-        take = source_ref[at_ref[c, g * per + u]]
-        row = take if row is None else jnp.where(lane == u, take, row)
+    for u, mask in enumerate(masks):
+        take = source_ref[at_ref[c, g * len(masks) + u]]
+        row = take if row is None else jnp.where(mask, take, row)
     return row
 
 
@@ -400,13 +405,14 @@
     clusters = near_ref.shape[1] // cl
     per = LANES // rank
     load_window(six_tables(near_pair_ref, far_pair_ref, swapped_ref), clusters, rank, pieces_ref, middle_ref)
-    lane = lax.broadcasted_iota(jnp.int32, (1, LANES), 1) // rank
+    wide = lane_masks(middle_ref.shape[1:], rank, jnp.int32)
+    masks = lane_masks(pieces_ref.shape[1:], rank, jnp.int16)
     for c in range(clusters):
         mine = [offsets_ref[3, k:k + 1, :] - center_ref[c:c + 1, k * LANES:(k + 1) * LANES] for k in range(3)]
         for g in range(at_ref.shape[1] // per):
             lanes = slice(g * LANES, (g + 1) * LANES)
-            gathered_ref[c, :, lanes] = pick(pieces_ref, at_ref, c, g, per, lane)
-            center = pick(middle_ref, at_ref, c, g, per, lane)
+            gathered_ref[c, :, lanes] = pick(pieces_ref, at_ref, c, g, masks)
+            center = pick(middle_ref, at_ref, c, g, wide)
             gap = [(center[k:k + 1] + mine[k]) - offsets_ref[k] for k in range(3)]
             high, low = split(lax.rsqrt(gap[0] * gap[0] + gap[1] * gap[1] + gap[2] * gap[2] + SMOOTHING))
             coupling_ref[c, 0:rank, lanes] = high
@@ -422,10 +428,10 @@
     clusters = near_ref.shape[1] // cl
     per = LANES // rank
     load_window(six_tables(near_pair_ref, far_pair_ref, swapped_ref), clusters, rank, pieces_ref, None)
-    lane = lax.broadcasted_iota(jnp.int32, (1, LANES), 1) // rank
+    masks = lane_masks(pieces_ref.shape[1:], rank, jnp.int16)
     for c in range(clusters):
         for g in range(at_ref.shape[1] // per):
-            gathered_ref[c, :, g * LANES:(g + 1) * LANES] = pick(pieces_ref, at_ref, c, g, per, lane)
+            gathered_ref[c, :, g * LANES:(g + 1) * LANES] = pick(pieces_ref, at_ref, c, g, masks)
     far_fields(gathered_ref, coupling_ref, fields_ref)
     for c in range(clusters):
         lanes = slice(c * cl, (c + 1) * cl)
@@ -538,7 +544,7 @@
         us=1.5,
     )
     sent, beside, near_pair, far_pair, other, partner = exchange(payload, table, False)
-    group = 4
+    group = 2
     own = ((clusters, 2 * cl, cl), BF16)
     kept = ((clusters * (slots - 1) // group, group, 2 * cl, cl), BF16)
     sums_shape = ((rhs, LANES), F32)

time: 42.5 us -> 43.8 us (1.031); the launches traced: 42.6 us -> 43.3 us
  Pallas kernels: 22.1 us -> 26.4 us
  starting transfers between devices: 13.1 us -> 9.87 us
    pallas_call x11, Pallas kernels: 22.1 us -> 26.4 us  [call(): pl.pallas_call(kernel, out_shape=[pltpu.VMEM(*out) if m == 'p' else jax.S...]
    ppermute x13, starting transfers between devices: 13.1 us -> 9.87 us  [move(): return lax.ppermute(value, 'clus', pairs)]
  transfers between devices with their start and end apart: 13 -> 13, of which waited for: 4 -> 5; matrix products, arithmetic and copies ran while one was open for 0% -> 0% of each run, Pallas kernels for 42% -> 51%
where the time goes in v9:
time: 43.8 us; the launch traced here: 43.3 us
  Pallas kernels  26.4 us (60%)
  starting transfers between devices  9.87 us (23%)
  waiting for transfers between devices  6.12 us (14%)
  between operations  0.8 us (2%)
    pallas_call x11, Pallas kernels, call(): pl.pallas_call(kernel, out_shape=[pltpu.VMEM(*out) if m == 'p' else jax.S...  26.4 us
    ppermute x13, starting transfers between devices, move(): return lax.ppermute(value, 'clus', pairs)  9.87 us
    ppermute x13, waiting for transfers between devices, move(): return lax.ppermute(value, 'clus', pairs)  6.12 us
  transfers between devices with their start and end apart: 13, of which 5 were waited for; matrix products, arithmetic and copies ran while one was open for 0% of the time, Pallas kernels for 51%

profile of v9, /device:TPU:0, one launch (start us, length us, event | category | flops | bytes accessed | tf_op | source)
XLA Modules:
  0.0 43.3 jit_solution(17548665344005815255)
XLA Ops:
  0.6 1.8 %shard_map.86 = (f32[16,4864]{1,0:T(8,128)S(1)}, f32[16,768]{1,0:T(8,128)S(1)}, f32[16,256]{1,0:T(8,128)S(1)}, f32[16,384]{1,0:T(8,128)S(1)}, s32[16,32]{1,0:T(8...) custom-call(s32[1]{0:T(128)} %bitcast.position_ref, ...), custom_call_target="tpu_custom_call" | custom-call | flops 750000000 | bytes 5400000 | tf_op jit(solution)/shard_map/pallas_call | solution.py:479
  2.4 0.5 %collective-permute-start = (f32[16,768]{1,0:T(8,128)S(1)}, f32[16,768]{1,0:T(8,128)S(1)}, u32[]{:S(2)}, u32[]{:S(2)}) collective-permute-start(f32[16,768]{1,0:T(8,128)S(1)} %get-tuple-element.28), channel_id=1, source_target_pairs={{0,1},{1,0},{2,3},{3,2},{4,5},{5,4},{6,7},{7,6},{8,9},{9,8},{10,11... | collective-permute-start | bytes 147464 | tf_op jit(solution)/shard_map/ppermute | solution.py:509
  3.0 0.1 collective-permute-start.5
  3.0 0.8 %collective-permute-done.beside_ref = f32[16,768]{1,0:T(8,128)S(1)} collective-permute-done((f32[16,768]{1,0:T(8,128)S(1)}, f32[16,768]{1,0:T(8,128)S(1)}, u32[]{:S(2)}, u32[]{:S(2)}) %collective-permute-start) | collective-permute-done | bytes 49184 | tf_op jit(solution)/shard_map/ppermute | solution.py:509
  3.8 2.9 %collective-permute-start.3 = (f32[16,1536]{1,0:T(8,128)S(1)}, f32[16,1536]{1,0:T(8,128)S(1)}, u32[]{:S(2)}, u32[]{:S(2)}) collective-permute-start(f32[16,1536]{1,0:T(8,128)S(1)} %constant_dynamic-update-slice_fusion), channel_id=1, source_target_pairs={{0,4},{1,0},{2,6},{3,2},{4,8},{5,1},{6,10},{7,3},{8,12},{9,5},{10,... | collective-permute-start | bytes 294920 | tf_op jit(solution)/shard_map/ppermute | solution.py:509
  6.8 1.5 %collective-permute-start.2 = (f32[16,1536]{1,0:T(8,128)S(1)}, f32[16,1536]{1,0:T(8,128)S(1)}, u32[]{:S(2)}, u32[]{:S(2)}) collective-permute-start(f32[16,1536]{1,0:T(8,128)S(1)} %constant_dynamic-update-slice_fusion), channel_id=1, source_target_pairs={{0,2},{1,0},{2,4},{3,1},{4,6},{5,3},{6,8},{7,5},{8,10},{9,7},{10,1... | collective-permute-start | bytes 294920 | tf_op jit(solution)/shard_map/ppermute | solution.py:509
  8.3 0.7 %collective-permute-start.1 = (f32[16,4992]{1,0:T(8,128)S(1)}, f32[16,4992]{1,0:T(8,128)S(1)}, u32[]{:S(2)}, u32[]{:S(2)}) collective-permute-start(f32[16,4992]{1,0:T(8,128)S(1)} %pad_maximum_fusion.payload_ref), channel_id=1, source_target_pairs={{1,2},{2,1},{3,4},{4,3},{5,6},{6,5},{7,8},{8,7},{9,10},{10,9},{11,... | collective-permute-start | bytes 958472 | tf_op jit(solution)/shard_map/ppermute | solution.py:509
  9.0 5.3 %shard_map.87 = (bf16[16,512,256]{2,1,0:T(8,128)(2,1)S(1)}, bf16[24,2,512,256]{3,2,1,0:T(8,128)(2,1)S(1)}, f32[16,4096]{1,0:T(8,128)S(1)}, bf16[16,80,256]{2,1,0:T(8,128)(2,1)S(1)}, f32[16,128]{1,0:T(8,128)S(1)}) custom-call(s32[8,128]{1,0:T(8,128)S(1)} %get-tuple-element.26.pairs_ref, f32[16,4992]{1,0:T(8,128)S(1)} %pad_maximum_fusion.payload_ref, ...), custom_call_target="tpu_custom_call" | custom-call | flops 4000000000 | bytes 28800000 | tf_op jit(solution)/shard_map/pallas_call | solution.py:479
  14.3 0.0 collective-permute-done.3.far_pair_ref
  14.3 0.0 collective-permute-done.2.near_pair_ref
  14.3 0.6 %collective-permute-start.4 = (f32[16,3200]{1,0:T(8,128)S(1)}, f32[16,3200]{1,0:T(8,128)S(1)}, u32[]{:S(2)}, u32[]{:S(2)}) collective-permute-start(f32[16,3200]{1,0:T(8,128)S(1)} %pad_maximum_fusion.2), channel_id=1, source_target_pairs={{0,1},{1,0},{2,3},{3,2},{4,5},{5,4},{6,7},{7,6},{8,9},{9,8},{10,11... | collective-permute-start | bytes 614408 | tf_op jit(solution)/shard_map/ppermute | solution.py:509
  15.0 0.0 collective-permute-done.5.payload_ref
  15.0 5.0 %shard_map.88 = (bf16[24,2,512,256]{3,2,1,0:T(8,128)(2,1)S(1)}, f32[16,4096]{1,0:T(8,128)S(1)}) custom-call(s32[8,128]{1,0:T(8,128)S(1)} %get-tuple-element.26.pairs_ref, f32[16,4864]{1,0:T(8,128)S(1)} %collective-permute-done.5.payload_ref, bf16[16,80,256]{2,1,0:T(8,128)(2,1)S(1)} %get-tuple-element.29.targets_ref, f32[16,4096]{1,0:T(8,128)S(1)} %get-tuple-element.33.start_ref), custom_call_target="tpu_custom_call" | custom-call | flops 100000000 | bytes 720000 | tf_op jit(solution)/shard_map/pallas_call | solution.py:479
  20.0 0.0 collective-permute-done.4.swapped_ref
  20.0 3.1 %shard_map.89 = (f32[16,4096]{1,0:T(8,128)S(1)}, bf16[16,64,1024]{2,1,0:T(8,128)(2,1)S(1)}) custom-call(s32[16,32]{1,0:T(8,128)S(1)} %get-tuple-element.30.at_ref, f32[16,1536]{1,0:T(8,128)S(1)} %collective-permute-done.2.near_pair_ref, f32[16,1536]{1,0:T(8,128)S(1)} %collective-permute-done.3.far_pair_ref, ...), custom_call_target="tpu_custom_call" | custom-call | flops 100000000 | bytes 720000 | tf_op jit(solution)/shard_map/pallas_call | solution.py:479
  23.1 0.0 collective-permute-done.1.payload_ref
  23.2 1.3 %shard_map.90 = (bf16[24,2,512,256]{3,2,1,0:T(8,128)(2,1)S(1)}, f32[16,4096]{1,0:T(8,128)S(1)}, f32[16,4096]{1,0:T(8,128)S(1)}, f32[16,640]{1,0:T(8,128)S(1)}) custom-call(s32[8,128]{1,0:T(8,128)S(1)} %get-tuple-element.26.pairs_ref, f32[16,4992]{1,0:T(8,128)S(1)} %collective-permute-done.1.payload_ref, ...), custom_call_target="tpu_custom_call" | custom-call | flops 2000000000 | bytes 14400000 | tf_op jit(solution)/shard_map/pallas_call | solution.py:479
  24.5 0.1 collective-permute-start.6
  24.6 0.5 %collective-permute-start.11 = (f32[16,4096]{1,0:T(8,128)S(1)}, f32[16,4096]{1,0:T(8,128)S(1)}, u32[]{:S(2)}, u32[]{:S(2)}) collective-permute-start(f32[16,4096]{1,0:T(8,128)S(1)} %get-tuple-element.40), channel_id=1, source_target_pairs={{0,1},{1,0},{2,3},{3,2},{4,5},{5,4},{6,7},{7,6},{8,9},{9,8},{10,11... | collective-permute-start | bytes 786440 | tf_op jit(solution)/shard_map/ppermute | solution.py:509
  25.1 0.7 %collective-permute-done.6.beside_ref.partner_ref = f32[16,640]{1,0:T(8,128)S(1)} collective-permute-done((f32[16,640]{1,0:T(8,128)S(1)}, f32[16,640]{1,0:T(8,128)S(1)}, u32[]{:S(2)}, u32[]{:S(2)}) %collective-permute-start.6) | collective-permute-done | bytes 40992 | tf_op jit(solution)/shard_map/ppermute | solution.py:509
  25.8 0.0 collective-permute-start.9
  25.8 2.2 %collective-permute-start.8 = (f32[16,1280]{1,0:T(8,128)S(1)}, f32[16,1280]{1,0:T(8,128)S(1)}, u32[]{:S(2)}, u32[]{:S(2)}) collective-permute-start(f32[16,1280]{1,0:T(8,128)S(1)} %constant_dynamic-update-slice_fusion.2), channel_id=1, source_target_pairs={{0,2},{1,15},{2,4},{3,1},{4,6},{5,3},{6,8},{7,5},{8,10},{9,7},{10,... | collective-permute-start | bytes 245768 | tf_op jit(solution)/shard_map/ppermute | solution.py:509
  28.0 0.7 %collective-permute-start.7 = (f32[16,4224]{1,0:T(8,128)S(1)}, f32[16,4224]{1,0:T(8,128)S(1)}, u32[]{:S(2)}, u32[]{:S(2)}) collective-permute-start(f32[16,4224]{1,0:T(8,128)S(1)} %pad_maximum_fusion.1.payload_ref), channel_id=1, source_target_pairs={{1,2},{2,1},{3,4},{4,3},{5,6},{6,5},{7,8},{8,7},{9,10},{10,9},{11,... | collective-permute-start | bytes 811016 | tf_op jit(solution)/shard_map/ppermute | solution.py:509
  28.7 2.9 %shard_map.91 = (f32[16,4096]{1,0:T(8,128)S(1)}, f32[16,128]{1,0:T(8,128)S(1)}) custom-call(s32[8,128]{1,0:T(8,128)S(1)} %get-tuple-element.26.pairs_ref, f32[16,4224]{1,0:T(8,128)S(1)} %pad_maximum_fusion.1.payload_ref, f32[16,640]{1,0:T(8,128)S(1)} %collective-permute-done.6.beside_ref.partner_ref, bf16[16,512,256]{2,1,0:T(8,128)(2,1)S(1)} %get-tuple-element.42.own_ref, ...), custom_call_target="tpu_custom_call" | custom-call | flops 4000000000 | bytes 28800000 | tf_op jit(solution)/shard_map/pallas_call | solution.py:479
  31.6 1.0 %collective-permute-done.9.far_pair_ref = f32[16,1280]{1,0:T(8,128)S(1)} collective-permute-done((f32[16,1280]{1,0:T(8,128)S(1)}, f32[16,1280]{1,0:T(8,128)S(1)}, u32[]{:S(2)}, u32[]{:S(2)}) %collective-permute-start.9) | collective-permute-done | bytes 81952 | tf_op jit(solution)/shard_map/ppermute | solution.py:509
  32.6 1.8 %collective-permute-done.8.near_pair_ref = f32[16,1280]{1,0:T(8,128)S(1)} collective-permute-done((f32[16,1280]{1,0:T(8,128)S(1)}, f32[16,1280]{1,0:T(8,128)S(1)}, u32[]{:S(2)}, u32[]{:S(2)}) %collective-permute-start.8) | collective-permute-done | bytes 81952 | tf_op jit(solution)/shard_map/ppermute | solution.py:509
  34.5 0.1 collective-permute-start.10
  34.6 0.0 collective-permute-done.11.payload_ref
  34.6 2.6 %shard_map.92.near_ref = f32[16,4096]{1,0:T(8,128)S(1)} custom-call(s32[8,128]{1,0:T(8,128)S(1)} %get-tuple-element.26.pairs_ref, f32[16,4096]{1,0:T(8,128)S(1)} %collective-permute-done.11.payload_ref, f32[16,4096]{1,0:T(8,128)S(1)} %get-tuple-element.45.start_ref, bf16[24,2,512,256]{3,2,1,0:T(8,128)(2,1)S(1)} %get-tuple-element.46.kept_ref), custom_call_target="tpu_custom_call" | custom-call | flops 2000000000 | bytes 14400000 | tf_op jit(solution)/shard_map/pallas_call | solution.py:479
  37.2 0.0 collective-permute-done.10.swapped_ref
  37.2 0.3 shard_map.95.one_ref
  37.5 0.0 collective-permute-start.12
  37.5 2.1 %shard_map.93.start_ref = f32[16,4096]{1,0:T(8,128)S(1)} custom-call(s32[16,32]{1,0:T(8,128)S(1)} %get-tuple-element.30.at_ref, f32[16,1280]{1,0:T(8,128)S(1)} %collective-permute-done.8.near_pair_ref, f32[16,1280]{1,0:T(8,128)S(1)} %collective-permute-done.9.far_pair_ref, f32[16,2688]{1,0:T(8,128)S(1)} %collective-permute-done.10.swapped_ref, ...), custom_call_target="tpu_custom_call" | custom-call | flops 2000000000 | bytes 14400000 | tf_op jit(solution)/shard_map/pallas_call | solution.py:479
  39.6 0.0 collective-permute-done.7.payload_ref
  39.6 0.7 %shard_map.94.near_ref = f32[16,4096]{1,0:T(8,128)S(1)} custom-call(s32[8,128]{1,0:T(8,128)S(1)} %get-tuple-element.26.pairs_ref, f32[16,4224]{1,0:T(8,128)S(1)} %collective-permute-done.7.payload_ref, f32[16,4096]{1,0:T(8,128)S(1)} %shard_map.93.start_ref, bf16[24,2,512,256]{3,2,1,0:T(8,128)(2,1)S(1)} %get-tuple-element.48.kept_ref), custom_call_target="tpu_custom_call" | custom-call | flops 750000000 | bytes 5400000 | tf_op jit(solution)/shard_map/pallas_call | solution.py:479
  40.3 1.7 %collective-permute-done.12.two_ref = f32[16,128]{1,0:T(8,128)S(1)} collective-permute-done((f32[16,128]{1,0:T(8,128)S(1)}, f32[16,128]{1,0:T(8,128)S(1)}, u32[]{:S(2)}, u32[]{:S(2)}) %collective-permute-start.12) | collective-permute-done | bytes 8224 | tf_op jit(solution)/shard_map/ppermute | solution.py:509
  42.0 1.2 %shard_map.96 = (f32[16,4096]{1,0:T(8,128)}, f32[16,4096]{1,0:T(8,128)}) custom-call(f32[16,4096]{1,0:T(8,128)S(1)} %shard_map.94.near_ref, f32[16,256]{1,0:T(8,128)S(1)} %get-tuple-element.38.area_ref, f32[16,4096]{1,0:T(8,128)S(1)} %get-tuple-element.49.image_ref, f32[16,4096]{1,0:T(8,128)S(1)} %get-tuple-element.39.krylov_ref, ...), custom_call_target="tpu_custom_call" | custom-call | flops 500000000 | bytes 3600000 | tf_op jit(solution)/shard_map/pallas_call | solution.py:479
  (10 shorter events, 0.1 us)
Async XLA Ops:
  2.4 1.4 %collective-permute-start = (f32[16,768]{1,0:T(8,128)S(1)}, f32[16,768]{1,0:T(8,128)S(1)}, u32[]{:S(2)}, u32[]{:S(2)}) collective-permute-start(f32[16,768]{1,0:T(8,128)S(1)} %get-tuple-element.28), channel_id=1, source_target_pairs={{0,1},{1,0},{2,3},{3,2},{4,5},{5,4},{6,7},{7,6},{8,9},{9,8},{10,11... | collective-permute-start | bytes 147464 | tf_op jit(solution)/shard_map/ppermute | solution.py:509
  3.0 12.0 %collective-permute-start.5 = (f32[16,4864]{1,0:T(8,128)S(1)}, f32[16,4864]{1,0:T(8,128)S(1)}, u32[]{:S(2)}, u32[]{:S(2)}) collective-permute-start(f32[16,4864]{1,0:T(8,128)S(1)} %get-tuple-element.27), channel_id=1, source_target_pairs={{0,1},{1,0},{2,3},{3,2},{4,5},{5,4},{6,7},{7,6},{8,9},{9,8},{10,11... | collective-permute-start | bytes 933896 | tf_op jit(solution)/shard_map/ppermute | solution.py:509
  3.8 10.5 %collective-permute-start.3 = (f32[16,1536]{1,0:T(8,128)S(1)}, f32[16,1536]{1,0:T(8,128)S(1)}, u32[]{:S(2)}, u32[]{:S(2)}) collective-permute-start(f32[16,1536]{1,0:T(8,128)S(1)} %constant_dynamic-update-slice_fusion), channel_id=1, source_target_pairs={{0,4},{1,0},{2,6},{3,2},{4,8},{5,1},{6,10},{7,3},{8,12},{9,5},{10,... | collective-permute-start | bytes 294920 | tf_op jit(solution)/shard_map/ppermute | solution.py:509
  6.8 7.5 %collective-permute-start.2 = (f32[16,1536]{1,0:T(8,128)S(1)}, f32[16,1536]{1,0:T(8,128)S(1)}, u32[]{:S(2)}, u32[]{:S(2)}) collective-permute-start(f32[16,1536]{1,0:T(8,128)S(1)} %constant_dynamic-update-slice_fusion), channel_id=1, source_target_pairs={{0,2},{1,0},{2,4},{3,1},{4,6},{5,3},{6,8},{7,5},{8,10},{9,7},{10,1... | collective-permute-start | bytes 294920 | tf_op jit(solution)/shard_map/ppermute | solution.py:509
  8.3 14.8 %collective-permute-start.1 = (f32[16,4992]{1,0:T(8,128)S(1)}, f32[16,4992]{1,0:T(8,128)S(1)}, u32[]{:S(2)}, u32[]{:S(2)}) collective-permute-start(f32[16,4992]{1,0:T(8,128)S(1)} %pad_maximum_fusion.payload_ref), channel_id=1, source_target_pairs={{1,2},{2,1},{3,4},{4,3},{5,6},{6,5},{7,8},{8,7},{9,10},{10,9},{11,... | collective-permute-start | bytes 958472 | tf_op jit(solution)/shard_map/ppermute | solution.py:509
  14.3 5.7 %collective-permute-start.4 = (f32[16,3200]{1,0:T(8,128)S(1)}, f32[16,3200]{1,0:T(8,128)S(1)}, u32[]{:S(2)}, u32[]{:S(2)}) collective-permute-start(f32[16,3200]{1,0:T(8,128)S(1)} %pad_maximum_fusion.2), channel_id=1, source_target_pairs={{0,1},{1,0},{2,3},{3,2},{4,5},{5,4},{6,7},{7,6},{8,9},{9,8},{10,11... | collective-permute-start | bytes 614408 | tf_op jit(solution)/shard_map/ppermute | solution.py:509
  24.5 1.3 %collective-permute-start.6 = (f32[16,640]{1,0:T(8,128)S(1)}, f32[16,640]{1,0:T(8,128)S(1)}, u32[]{:S(2)}, u32[]{:S(2)}) collective-permute-start(f32[16,640]{1,0:T(8,128)S(1)} %get-tuple-element.41.payload_ref), channel_id=1, source_target_pairs={{0,1},{1,0},{2,3},{3,2},{4,5},{5,4},{6,7},{7,6},{8,9},{9,8},{10,11... | collective-permute-start | bytes 122888 | tf_op jit(solution)/shard_map/ppermute | solution.py:509
  24.6 10.0 %collective-permute-start.11 = (f32[16,4096]{1,0:T(8,128)S(1)}, f32[16,4096]{1,0:T(8,128)S(1)}, u32[]{:S(2)}, u32[]{:S(2)}) collective-permute-start(f32[16,4096]{1,0:T(8,128)S(1)} %get-tuple-element.40), channel_id=1, source_target_pairs={{0,1},{1,0},{2,3},{3,2},{4,5},{5,4},{6,7},{7,6},{8,9},{9,8},{10,11... | collective-permute-start | bytes 786440 | tf_op jit(solution)/shard_map/ppermute | solution.py:509
  25.8 6.8 %collective-permute-start.9 = (f32[16,1280]{1,0:T(8,128)S(1)}, f32[16,1280]{1,0:T(8,128)S(1)}, u32[]{:S(2)}, u32[]{:S(2)}) collective-permute-start(f32[16,1280]{1,0:T(8,128)S(1)} %constant_dynamic-update-slice_fusion.2), channel_id=1, source_target_pairs={{0,4},{1,13},{2,6},{3,15},{4,8},{5,1},{6,10},{7,3},{8,12},{9,5},{1... | collective-permute-start | bytes 245768 | tf_op jit(solution)/shard_map/ppermute | solution.py:509
  25.8 8.7 %collective-permute-start.8 = (f32[16,1280]{1,0:T(8,128)S(1)}, f32[16,1280]{1,0:T(8,128)S(1)}, u32[]{:S(2)}, u32[]{:S(2)}) collective-permute-start(f32[16,1280]{1,0:T(8,128)S(1)} %constant_dynamic-update-slice_fusion.2), channel_id=1, source_target_pairs={{0,2},{1,15},{2,4},{3,1},{4,6},{5,3},{6,8},{7,5},{8,10},{9,7},{10,... | collective-permute-start | bytes 245768 | tf_op jit(solution)/shard_map/ppermute | solution.py:509
  28.0 11.6 %collective-permute-start.7 = (f32[16,4224]{1,0:T(8,128)S(1)}, f32[16,4224]{1,0:T(8,128)S(1)}, u32[]{:S(2)}, u32[]{:S(2)}) collective-permute-start(f32[16,4224]{1,0:T(8,128)S(1)} %pad_maximum_fusion.1.payload_ref), channel_id=1, source_target_pairs={{1,2},{2,1},{3,4},{4,3},{5,6},{6,5},{7,8},{8,7},{9,10},{10,9},{11,... | collective-permute-start | bytes 811016 | tf_op jit(solution)/shard_map/ppermute | solution.py:509
  34.5 2.7 %collective-permute-start.10 = (f32[16,2688]{1,0:T(8,128)S(1)}, f32[16,2688]{1,0:T(8,128)S(1)}, u32[]{:S(2)}, u32[]{:S(2)}) collective-permute-start(f32[16,2688]{1,0:T(8,128)S(1)} %pad_maximum_fusion.3), channel_id=1, source_target_pairs={{0,1},{1,0},{2,3},{3,2},{4,5},{5,4},{6,7},{7,6},{8,9},{9,8},{10,11... | collective-permute-start | bytes 516104 | tf_op jit(solution)/shard_map/ppermute | solution.py:509
  37.5 4.6 %collective-permute-start.12 = (f32[16,128]{1,0:T(8,128)S(1)}, f32[16,128]{1,0:T(8,128)S(1)}, u32[]{:S(2)}, u32[]{:S(2)}) collective-permute-start(f32[16,128]{1,0:T(8,128)S(1)} %shard_map.95.one_ref), channel_id=1, source_target_pairs={{0,8},{1,9},{2,10},{3,11},{4,12},{5,13},{6,14},{7,15},{8,0},{9,1},... | collective-permute-start | bytes 24584 | tf_op jit(solution)/shard_map/ppermute | solution.py:509

commit v10 on v9

--- a/solution.py
+++ b/solution.py
@@ -544,7 +544,7 @@
         us=1.5,
     )
     sent, beside, near_pair, far_pair, other, partner = exchange(payload, table, False)
-    group = 2
+    group = 4
     own = ((clusters, 2 * cl, cl), BF16)
     kept = ((clusters * (slots - 1) // group, group, 2 * cl, cl), BF16)
     sums_shape = ((rhs, LANES), F32)

time: 43.8 us -> 41.4 us (0.945)
  Pallas kernels: 26.4 us -> 21.1 us
  starting transfers between devices: 9.87 us -> 14.7 us
  waiting for transfers between devices: 6.12 us -> 4.06 us
    pallas_call x11, Pallas kernels: 26.4 us -> 21.1 us  [call(): pl.pallas_call(kernel, out_shape=[pltpu.VMEM(*out) if m == 'p' else jax.S...]
    ppermute x13, starting transfers between devices: 9.87 us -> 14.7 us  [move(): return lax.ppermute(value, 'clus', pairs)]
    ppermute x13, waiting for transfers between devices: 6.12 us -> 4.06 us  [move(): return lax.ppermute(value, 'clus', pairs)]
  transfers between devices with their start and end apart: 13 -> 13, of which waited for: 5 -> 4; matrix products, arithmetic and copies ran while one was open for 0% -> 0% of each run, Pallas kernels for 51% -> 41%
where the time goes in v10:
time: 41.4 us; the launch traced here: 40.7 us
  Pallas kernels  21.1 us (51%)
  starting transfers between devices  14.7 us (36%)
  waiting for transfers between devices  4.06 us (10%)
  between operations  0.77 us (2%)
    pallas_call x11, Pallas kernels, call(): pl.pallas_call(kernel, out_shape=[pltpu.VMEM(*out) if m == 'p' else jax.S...  21.1 us
    ppermute x13, starting transfers between devices, move(): return lax.ppermute(value, 'clus', pairs)  14.7 us
    ppermute x13, waiting for transfers between devices, move(): return lax.ppermute(value, 'clus', pairs)  4.06 us
  transfers between devices with their start and end apart: 13, of which 4 were waited for; matrix products, arithmetic and copies ran while one was open for 0% of the time, Pallas kernels for 41%

profile of v10, /device:TPU:0, one launch (start us, length us, event | category | flops | bytes accessed | tf_op | source)
XLA Modules:
  0.0 40.7 jit_solution(12169082560811687784)
XLA Ops:
  0.6 1.8 %shard_map.86 = (f32[16,4864]{1,0:T(8,128)S(1)}, f32[16,768]{1,0:T(8,128)S(1)}, f32[16,256]{1,0:T(8,128)S(1)}, f32[16,384]{1,0:T(8,128)S(1)}, s32[16,32]{1,0:T(8...) custom-call(s32[1]{0:T(128)} %bitcast.position_ref, ...), custom_call_target="tpu_custom_call" | custom-call | flops 750000000 | bytes 5400000 | tf_op jit(solution)/shard_map/pallas_call | solution.py:479
  2.4 0.5 %collective-permute-start = (f32[16,768]{1,0:T(8,128)S(1)}, f32[16,768]{1,0:T(8,128)S(1)}, u32[]{:S(2)}, u32[]{:S(2)}) collective-permute-start(f32[16,768]{1,0:T(8,128)S(1)} %get-tuple-element.28), channel_id=1, source_target_pairs={{0,1},{1,0},{2,3},{3,2},{4,5},{5,4},{6,7},{7,6},{8,9},{9,8},{10,11... | collective-permute-start | bytes 147464 | tf_op jit(solution)/shard_map/ppermute | solution.py:509
  3.0 0.1 collective-permute-start.5
  3.0 0.8 %collective-permute-done.beside_ref = f32[16,768]{1,0:T(8,128)S(1)} collective-permute-done((f32[16,768]{1,0:T(8,128)S(1)}, f32[16,768]{1,0:T(8,128)S(1)}, u32[]{:S(2)}, u32[]{:S(2)}) %collective-permute-start) | collective-permute-done | bytes 49184 | tf_op jit(solution)/shard_map/ppermute | solution.py:509
  3.8 2.9 %collective-permute-start.3 = (f32[16,1536]{1,0:T(8,128)S(1)}, f32[16,1536]{1,0:T(8,128)S(1)}, u32[]{:S(2)}, u32[]{:S(2)}) collective-permute-start(f32[16,1536]{1,0:T(8,128)S(1)} %constant_dynamic-update-slice_fusion), channel_id=1, source_target_pairs={{0,4},{1,0},{2,6},{3,2},{4,8},{5,1},{6,10},{7,3},{8,12},{9,5},{10,... | collective-permute-start | bytes 294920 | tf_op jit(solution)/shard_map/ppermute | solution.py:509
  6.8 1.5 %collective-permute-start.2 = (f32[16,1536]{1,0:T(8,128)S(1)}, f32[16,1536]{1,0:T(8,128)S(1)}, u32[]{:S(2)}, u32[]{:S(2)}) collective-permute-start(f32[16,1536]{1,0:T(8,128)S(1)} %constant_dynamic-update-slice_fusion), channel_id=1, source_target_pairs={{0,2},{1,0},{2,4},{3,1},{4,6},{5,3},{6,8},{7,5},{8,10},{9,7},{10,1... | collective-permute-start | bytes 294920 | tf_op jit(solution)/shard_map/ppermute | solution.py:509
  8.3 0.7 %collective-permute-start.1 = (f32[16,4992]{1,0:T(8,128)S(1)}, f32[16,4992]{1,0:T(8,128)S(1)}, u32[]{:S(2)}, u32[]{:S(2)}) collective-permute-start(f32[16,4992]{1,0:T(8,128)S(1)} %pad_maximum_fusion.payload_ref), channel_id=1, source_target_pairs={{1,2},{2,1},{3,4},{4,3},{5,6},{6,5},{7,8},{8,7},{9,10},{10,9},{11,... | collective-permute-start | bytes 958472 | tf_op jit(solution)/shard_map/ppermute | solution.py:509
  9.0 3.9 %shard_map.87 = (bf16[16,512,256]{2,1,0:T(8,128)(2,1)S(1)}, bf16[12,4,512,256]{3,2,1,0:T(8,128)(2,1)S(1)}, f32[16,4096]{1,0:T(8,128)S(1)}, bf16[16,80,256]{2,1,0:T(8,128)(2,1)S(1)}, f32[16,128]{1,0:T(8,128)S(1)}) custom-call(s32[8,128]{1,0:T(8,128)S(1)} %get-tuple-element.26.pairs_ref, f32[16,4992]{1,0:T(8,128)S(1)} %pad_maximum_fusion.payload_ref, ...), custom_call_target="tpu_custom_call" | custom-call | flops 4000000000 | bytes 28800000 | tf_op jit(solution)/shard_map/pallas_call | solution.py:479
  12.9 0.0 collective-permute-done.3.far_pair_ref
  12.9 0.0 collective-permute-done.2.near_pair_ref
  12.9 1.7 %collective-permute-start.4 = (f32[16,3200]{1,0:T(8,128)S(1)}, f32[16,3200]{1,0:T(8,128)S(1)}, u32[]{:S(2)}, u32[]{:S(2)}) collective-permute-start(f32[16,3200]{1,0:T(8,128)S(1)} %pad_maximum_fusion.2), channel_id=1, source_target_pairs={{0,1},{1,0},{2,3},{3,2},{4,5},{5,4},{6,7},{7,6},{8,9},{9,8},{10,11... | collective-permute-start | bytes 614408 | tf_op jit(solution)/shard_map/ppermute | solution.py:509
  14.7 0.0 collective-permute-done.5.payload_ref
  14.7 2.7 %shard_map.88 = (bf16[12,4,512,256]{3,2,1,0:T(8,128)(2,1)S(1)}, f32[16,4096]{1,0:T(8,128)S(1)}) custom-call(s32[8,128]{1,0:T(8,128)S(1)} %get-tuple-element.26.pairs_ref, f32[16,4864]{1,0:T(8,128)S(1)} %collective-permute-done.5.payload_ref, bf16[16,80,256]{2,1,0:T(8,128)(2,1)S(1)} %get-tuple-element.29.targets_ref, f32[16,4096]{1,0:T(8,128)S(1)} %get-tuple-element.33.start_ref), custom_call_target="tpu_custom_call" | custom-call | flops 100000000 | bytes 720000 | tf_op jit(solution)/shard_map/pallas_call | solution.py:479
  17.4 0.0 collective-permute-done.4.swapped_ref
  17.4 3.1 %shard_map.89 = (f32[16,4096]{1,0:T(8,128)S(1)}, bf16[16,64,1024]{2,1,0:T(8,128)(2,1)S(1)}) custom-call(s32[16,32]{1,0:T(8,128)S(1)} %get-tuple-element.30.at_ref, f32[16,1536]{1,0:T(8,128)S(1)} %collective-permute-done.2.near_pair_ref, f32[16,1536]{1,0:T(8,128)S(1)} %collective-permute-done.3.far_pair_ref, ...), custom_call_target="tpu_custom_call" | custom-call | flops 100000000 | bytes 720000 | tf_op jit(solution)/shard_map/pallas_call | solution.py:479
  20.5 0.0 collective-permute-done.1.payload_ref
  20.5 1.3 %shard_map.90 = (bf16[12,4,512,256]{3,2,1,0:T(8,128)(2,1)S(1)}, f32[16,4096]{1,0:T(8,128)S(1)}, f32[16,4096]{1,0:T(8,128)S(1)}, f32[16,640]{1,0:T(8,128)S(1)}) custom-call(s32[8,128]{1,0:T(8,128)S(1)} %get-tuple-element.26.pairs_ref, f32[16,4992]{1,0:T(8,128)S(1)} %collective-permute-done.1.payload_ref, ...), custom_call_target="tpu_custom_call" | custom-call | flops 2000000000 | bytes 14400000 | tf_op jit(solution)/shard_map/pallas_call | solution.py:479
  21.9 0.7 %collective-permute-start.6 = (f32[16,640]{1,0:T(8,128)S(1)}, f32[16,640]{1,0:T(8,128)S(1)}, u32[]{:S(2)}, u32[]{:S(2)}) collective-permute-start(f32[16,640]{1,0:T(8,128)S(1)} %get-tuple-element.41.payload_ref), channel_id=1, source_target_pairs={{0,1},{1,0},{2,3},{3,2},{4,5},{5,4},{6,7},{7,6},{8,9},{9,8},{10,11... | collective-permute-start | bytes 122888 | tf_op jit(solution)/shard_map/ppermute | solution.py:509
  22.6 0.1 collective-permute-start.11
  22.6 0.8 %collective-permute-done.6.beside_ref.partner_ref = f32[16,640]{1,0:T(8,128)S(1)} collective-permute-done((f32[16,640]{1,0:T(8,128)S(1)}, f32[16,640]{1,0:T(8,128)S(1)}, u32[]{:S(2)}, u32[]{:S(2)}) %collective-permute-start.6) | collective-permute-done | bytes 40992 | tf_op jit(solution)/shard_map/ppermute | solution.py:509
  23.4 1.6 %collective-permute-start.9 = (f32[16,1280]{1,0:T(8,128)S(1)}, f32[16,1280]{1,0:T(8,128)S(1)}, u32[]{:S(2)}, u32[]{:S(2)}) collective-permute-start(f32[16,1280]{1,0:T(8,128)S(1)} %constant_dynamic-update-slice_fusion.2), channel_id=1, source_target_pairs={{0,4},{1,13},{2,6},{3,15},{4,8},{5,1},{6,10},{7,3},{8,12},{9,5},{1... | collective-permute-start | bytes 245768 | tf_op jit(solution)/shard_map/ppermute | solution.py:509
  25.0 3.3 %collective-permute-start.8 = (f32[16,1280]{1,0:T(8,128)S(1)}, f32[16,1280]{1,0:T(8,128)S(1)}, u32[]{:S(2)}, u32[]{:S(2)}) collective-permute-start(f32[16,1280]{1,0:T(8,128)S(1)} %constant_dynamic-update-slice_fusion.2), channel_id=1, source_target_pairs={{0,2},{1,15},{2,4},{3,1},{4,6},{5,3},{6,8},{7,5},{8,10},{9,7},{10,... | collective-permute-start | bytes 245768 | tf_op jit(solution)/shard_map/ppermute | solution.py:509
  28.3 0.7 %collective-permute-start.7 = (f32[16,4224]{1,0:T(8,128)S(1)}, f32[16,4224]{1,0:T(8,128)S(1)}, u32[]{:S(2)}, u32[]{:S(2)}) collective-permute-start(f32[16,4224]{1,0:T(8,128)S(1)} %pad_maximum_fusion.1.payload_ref), channel_id=1, source_target_pairs={{1,2},{2,1},{3,4},{4,3},{5,6},{6,5},{7,8},{8,7},{9,10},{10,9},{11,... | collective-permute-start | bytes 811016 | tf_op jit(solution)/shard_map/ppermute | solution.py:509
  29.0 2.3 %shard_map.91 = (f32[16,4096]{1,0:T(8,128)S(1)}, f32[16,128]{1,0:T(8,128)S(1)}) custom-call(s32[8,128]{1,0:T(8,128)S(1)} %get-tuple-element.26.pairs_ref, f32[16,4224]{1,0:T(8,128)S(1)} %pad_maximum_fusion.1.payload_ref, f32[16,640]{1,0:T(8,128)S(1)} %collective-permute-done.6.beside_ref.partner_ref, bf16[16,512,256]{2,1,0:T(8,128)(2,1)S(1)} %get-tuple-element.42.own_ref, ...), custom_call_target="tpu_custom_call" | custom-call | flops 4000000000 | bytes 28800000 | tf_op jit(solution)/shard_map/pallas_call | solution.py:479
  31.4 0.0 collective-permute-done.9.far_pair_ref
  31.4 0.8 %collective-permute-done.8.near_pair_ref = f32[16,1280]{1,0:T(8,128)S(1)} collective-permute-done((f32[16,1280]{1,0:T(8,128)S(1)}, f32[16,1280]{1,0:T(8,128)S(1)}, u32[]{:S(2)}, u32[]{:S(2)}) %collective-permute-start.8) | collective-permute-done | bytes 81952 | tf_op jit(solution)/shard_map/ppermute | solution.py:509
  32.2 0.8 %collective-permute-start.10 = (f32[16,2688]{1,0:T(8,128)S(1)}, f32[16,2688]{1,0:T(8,128)S(1)}, u32[]{:S(2)}, u32[]{:S(2)}) collective-permute-start(f32[16,2688]{1,0:T(8,128)S(1)} %pad_maximum_fusion.3), channel_id=1, source_target_pairs={{0,1},{1,0},{2,3},{3,2},{4,5},{5,4},{6,7},{7,6},{8,9},{9,8},{10,11... | collective-permute-start | bytes 516104 | tf_op jit(solution)/shard_map/ppermute | solution.py:509
  33.0 0.0 collective-permute-done.11.payload_ref
  33.0 1.6 %shard_map.92.near_ref = f32[16,4096]{1,0:T(8,128)S(1)} custom-call(s32[8,128]{1,0:T(8,128)S(1)} %get-tuple-element.26.pairs_ref, f32[16,4096]{1,0:T(8,128)S(1)} %collective-permute-done.11.payload_ref, f32[16,4096]{1,0:T(8,128)S(1)} %get-tuple-element.45.start_ref, bf16[12,4,512,256]{3,2,1,0:T(8,128)(2,1)S(1)} %get-tuple-element.46.kept_ref), custom_call_target="tpu_custom_call" | custom-call | flops 2000000000 | bytes 14400000 | tf_op jit(solution)/shard_map/pallas_call | solution.py:479
  34.6 0.0 collective-permute-done.10.swapped_ref
  34.6 0.3 shard_map.95.one_ref
  34.9 0.1 collective-permute-start.12
  35.1 2.1 %shard_map.93.start_ref = f32[16,4096]{1,0:T(8,128)S(1)} custom-call(s32[16,32]{1,0:T(8,128)S(1)} %get-tuple-element.30.at_ref, f32[16,1280]{1,0:T(8,128)S(1)} %collective-permute-done.8.near_pair_ref, f32[16,1280]{1,0:T(8,128)S(1)} %collective-permute-done.9.far_pair_ref, f32[16,2688]{1,0:T(8,128)S(1)} %collective-permute-done.10.swapped_ref, ...), custom_call_target="tpu_custom_call" | custom-call | flops 2000000000 | bytes 14400000 | tf_op jit(solution)/shard_map/pallas_call | solution.py:479
  37.1 0.0 collective-permute-done.7.payload_ref
  37.1 0.7 %shard_map.94.near_ref = f32[16,4096]{1,0:T(8,128)S(1)} custom-call(s32[8,128]{1,0:T(8,128)S(1)} %get-tuple-element.26.pairs_ref, f32[16,4224]{1,0:T(8,128)S(1)} %collective-permute-done.7.payload_ref, f32[16,4096]{1,0:T(8,128)S(1)} %shard_map.93.start_ref, bf16[12,4,512,256]{3,2,1,0:T(8,128)(2,1)S(1)} %get-tuple-element.48.kept_ref), custom_call_target="tpu_custom_call" | custom-call | flops 750000000 | bytes 5400000 | tf_op jit(solution)/shard_map/pallas_call | solution.py:479
  37.9 1.6 %collective-permute-done.12.two_ref = f32[16,128]{1,0:T(8,128)S(1)} collective-permute-done((f32[16,128]{1,0:T(8,128)S(1)}, f32[16,128]{1,0:T(8,128)S(1)}, u32[]{:S(2)}, u32[]{:S(2)}) %collective-permute-start.12) | collective-permute-done | bytes 8224 | tf_op jit(solution)/shard_map/ppermute | solution.py:509
  39.5 1.2 %shard_map.96 = (f32[16,4096]{1,0:T(8,128)}, f32[16,4096]{1,0:T(8,128)}) custom-call(f32[16,4096]{1,0:T(8,128)S(1)} %shard_map.94.near_ref, f32[16,256]{1,0:T(8,128)S(1)} %get-tuple-element.38.area_ref, f32[16,4096]{1,0:T(8,128)S(1)} %get-tuple-element.49.image_ref, f32[16,4096]{1,0:T(8,128)S(1)} %get-tuple-element.39.krylov_ref, ...), custom_call_target="tpu_custom_call" | custom-call | flops 500000000 | bytes 3600000 | tf_op jit(solution)/shard_map/pallas_call | solution.py:479
  (10 shorter events, 0.1 us)
Async XLA Ops:
  2.4 1.4 %collective-permute-start = (f32[16,768]{1,0:T(8,128)S(1)}, f32[16,768]{1,0:T(8,128)S(1)}, u32[]{:S(2)}, u32[]{:S(2)}) collective-permute-start(f32[16,768]{1,0:T(8,128)S(1)} %get-tuple-element.28), channel_id=1, source_target_pairs={{0,1},{1,0},{2,3},{3,2},{4,5},{5,4},{6,7},{7,6},{8,9},{9,8},{10,11... | collective-permute-start | bytes 147464 | tf_op jit(solution)/shard_map/ppermute | solution.py:509
  3.0 11.7 %collective-permute-start.5 = (f32[16,4864]{1,0:T(8,128)S(1)}, f32[16,4864]{1,0:T(8,128)S(1)}, u32[]{:S(2)}, u32[]{:S(2)}) collective-permute-start(f32[16,4864]{1,0:T(8,128)S(1)} %get-tuple-element.27), channel_id=1, source_target_pairs={{0,1},{1,0},{2,3},{3,2},{4,5},{5,4},{6,7},{7,6},{8,9},{9,8},{10,11... | collective-permute-start | bytes 933896 | tf_op jit(solution)/shard_map/ppermute | solution.py:509
  3.8 9.0 %collective-permute-start.3 = (f32[16,1536]{1,0:T(8,128)S(1)}, f32[16,1536]{1,0:T(8,128)S(1)}, u32[]{:S(2)}, u32[]{:S(2)}) collective-permute-start(f32[16,1536]{1,0:T(8,128)S(1)} %constant_dynamic-update-slice_fusion), channel_id=1, source_target_pairs={{0,4},{1,0},{2,6},{3,2},{4,8},{5,1},{6,10},{7,3},{8,12},{9,5},{10,... | collective-permute-start | bytes 294920 | tf_op jit(solution)/shard_map/ppermute | solution.py:509
  6.8 6.1 %collective-permute-start.2 = (f32[16,1536]{1,0:T(8,128)S(1)}, f32[16,1536]{1,0:T(8,128)S(1)}, u32[]{:S(2)}, u32[]{:S(2)}) collective-permute-start(f32[16,1536]{1,0:T(8,128)S(1)} %constant_dynamic-update-slice_fusion), channel_id=1, source_target_pairs={{0,2},{1,0},{2,4},{3,1},{4,6},{5,3},{6,8},{7,5},{8,10},{9,7},{10,1... | collective-permute-start | bytes 294920 | tf_op jit(solution)/shard_map/ppermute | solution.py:509
  8.3 12.2 %collective-permute-start.1 = (f32[16,4992]{1,0:T(8,128)S(1)}, f32[16,4992]{1,0:T(8,128)S(1)}, u32[]{:S(2)}, u32[]{:S(2)}) collective-permute-start(f32[16,4992]{1,0:T(8,128)S(1)} %pad_maximum_fusion.payload_ref), channel_id=1, source_target_pairs={{1,2},{2,1},{3,4},{4,3},{5,6},{6,5},{7,8},{8,7},{9,10},{10,9},{11,... | collective-permute-start | bytes 958472 | tf_op jit(solution)/shard_map/ppermute | solution.py:509
  12.9 4.4 %collective-permute-start.4 = (f32[16,3200]{1,0:T(8,128)S(1)}, f32[16,3200]{1,0:T(8,128)S(1)}, u32[]{:S(2)}, u32[]{:S(2)}) collective-permute-start(f32[16,3200]{1,0:T(8,128)S(1)} %pad_maximum_fusion.2), channel_id=1, source_target_pairs={{0,1},{1,0},{2,3},{3,2},{4,5},{5,4},{6,7},{7,6},{8,9},{9,8},{10,11... | collective-permute-start | bytes 614408 | tf_op jit(solution)/shard_map/ppermute | solution.py:509
  21.9 1.6 %collective-permute-start.6 = (f32[16,640]{1,0:T(8,128)S(1)}, f32[16,640]{1,0:T(8,128)S(1)}, u32[]{:S(2)}, u32[]{:S(2)}) collective-permute-start(f32[16,640]{1,0:T(8,128)S(1)} %get-tuple-element.41.payload_ref), channel_id=1, source_target_pairs={{0,1},{1,0},{2,3},{3,2},{4,5},{5,4},{6,7},{7,6},{8,9},{9,8},{10,11... | collective-permute-start | bytes 122888 | tf_op jit(solution)/shard_map/ppermute | solution.py:509
  22.6 10.5 %collective-permute-start.11 = (f32[16,4096]{1,0:T(8,128)S(1)}, f32[16,4096]{1,0:T(8,128)S(1)}, u32[]{:S(2)}, u32[]{:S(2)}) collective-permute-start(f32[16,4096]{1,0:T(8,128)S(1)} %get-tuple-element.40), channel_id=1, source_target_pairs={{0,1},{1,0},{2,3},{3,2},{4,5},{5,4},{6,7},{7,6},{8,9},{9,8},{10,11... | collective-permute-start | bytes 786440 | tf_op jit(solution)/shard_map/ppermute | solution.py:509
  23.4 7.9 %collective-permute-start.9 = (f32[16,1280]{1,0:T(8,128)S(1)}, f32[16,1280]{1,0:T(8,128)S(1)}, u32[]{:S(2)}, u32[]{:S(2)}) collective-permute-start(f32[16,1280]{1,0:T(8,128)S(1)} %constant_dynamic-update-slice_fusion.2), channel_id=1, source_target_pairs={{0,4},{1,13},{2,6},{3,15},{4,8},{5,1},{6,10},{7,3},{8,12},{9,5},{1... | collective-permute-start | bytes 245768 | tf_op jit(solution)/shard_map/ppermute | solution.py:509
  25.0 7.2 %collective-permute-start.8 = (f32[16,1280]{1,0:T(8,128)S(1)}, f32[16,1280]{1,0:T(8,128)S(1)}, u32[]{:S(2)}, u32[]{:S(2)}) collective-permute-start(f32[16,1280]{1,0:T(8,128)S(1)} %constant_dynamic-update-slice_fusion.2), channel_id=1, source_target_pairs={{0,2},{1,15},{2,4},{3,1},{4,6},{5,3},{6,8},{7,5},{8,10},{9,7},{10,... | collective-permute-start | bytes 245768 | tf_op jit(solution)/shard_map/ppermute | solution.py:509
  28.3 8.8 %collective-permute-start.7 = (f32[16,4224]{1,0:T(8,128)S(1)}, f32[16,4224]{1,0:T(8,128)S(1)}, u32[]{:S(2)}, u32[]{:S(2)}) collective-permute-start(f32[16,4224]{1,0:T(8,128)S(1)} %pad_maximum_fusion.1.payload_ref), channel_id=1, source_target_pairs={{1,2},{2,1},{3,4},{4,3},{5,6},{6,5},{7,8},{8,7},{9,10},{10,9},{11,... | collective-permute-start | bytes 811016 | tf_op jit(solution)/shard_map/ppermute | solution.py:509
  32.2 2.4 %collective-permute-start.10 = (f32[16,2688]{1,0:T(8,128)S(1)}, f32[16,2688]{1,0:T(8,128)S(1)}, u32[]{:S(2)}, u32[]{:S(2)}) collective-permute-start(f32[16,2688]{1,0:T(8,128)S(1)} %pad_maximum_fusion.3), channel_id=1, source_target_pairs={{0,1},{1,0},{2,3},{3,2},{4,5},{5,4},{6,7},{7,6},{8,9},{9,8},{10,11... | collective-permute-start | bytes 516104 | tf_op jit(solution)/shard_map/ppermute | solution.py:509
  34.9 4.6 %collective-permute-start.12 = (f32[16,128]{1,0:T(8,128)S(1)}, f32[16,128]{1,0:T(8,128)S(1)}, u32[]{:S(2)}, u32[]{:S(2)}) collective-permute-start(f32[16,128]{1,0:T(8,128)S(1)} %shard_map.95.one_ref), channel_id=1, source_target_pairs={{0,8},{1,9},{2,10},{3,11},{4,12},{5,13},{6,14},{7,15},{8,0},{9,1},... | collective-permute-start | bytes 24584 | tf_op jit(solution)/shard_map/ppermute | solution.py:509
